TPU v7x, 32 devices: a whole 2x2x4 slice. The times are simulated.
32 devices in a mesh: img: 8 (over z, y), rows: 4 (over x, core).
Axes of the slice: x: 2, y: 2, z: 4, core: 2. Of those that a mesh axis runs over, the one named last changes fastest.
Arguments:
- inputs: bfloat16 [4, 256, 16, 16, 1024], P(None, 'img', 'rows'), may hold values from -18 to 18
- masks: int32 [4, 256, 16, 16], P(None, 'img', 'rows'), may hold values from 0 to 1, as said below
- partner: int32 [4, 256], P(None, ('img', 'rows')), may hold values from 0 to 255, as said below
- live: int32 [4, 256], P(None, ('img', 'rows')), may hold values from 0 to 1, as said below
- params: float32 [20738048], P(('img', 'rows')), may hold values from -1.5 to 1.5, as said below
- first: float32 [20738048], P(('img', 'rows')), may hold values from -1 to 1
- second: float32 [20738048], P(('img', 'rows')), may hold values from 0 to 1
- running: float32 [2, 11776], replicated, may hold values from -1 to 2
Outputs:
- loss_sums: float32 [4], replicated
- pair_counts: int32 [4], replicated
- new_params: float32 [20738048], P(('img', 'rows'))
- new_first: float32 [20738048], P(('img', 'rows'))
- new_second: float32 [20738048], P(('img', 'rows'))
- new_copy: bfloat16 [20738048], P(('img', 'rows'))
- new_running: float32 [2, 11776], replicated
Inputs may be any that keep to these rules, and one draw needn't show every extreme that they name: `masks`: each image is valid on all 16 x 16 pixels, on its first 12 rows, or on its first 12 columns. partner[m, i] lies in the same aligned block of 8 images as i, differs from i, and partner[m, partner[m, i]] = i. live is equal on both images of a pair. `params`: the entries past the first 20734976 are zero.
All inputs are finite; a program needn't handle non-finite values.
Results may differ from a plain program's by a relative error of at most 0.025.
Values may be sent and summed in bfloat16 or wider, within the bound.
No kernel may reach another device: no remote copies, remote signals or barrier semaphores. Data moves between devices by JAX's collectives and lax.ppermute only.
A program may use at most 960 MiB of HBM per device.

v0:
```python
import jax
import jax.numpy as jnp
from jax import lax
from jax.experimental import pallas as pl
from jax.experimental.pallas import tpu as pltpu
from jax.sharding import Mesh, PartitionSpec as P

D_IN = 1024
MID = 512
OUT = 2048
PRED = 512
MB = 4
STEP = 5
NORM = 11776
PARAMS = 20734976

EPS_NORM = 1e-05
MOMENTUM = 0.1
RATE = 0.03
BETA_ONE = 0.5
BETA_TWO = 0.5
DECAY = 0.01
ADAM_EPS = 1e-08
COS_EPS = 1e-06

ROW_CIN, ROW_CMID, ROW_COUT, ROW_SIDE = 0, 256, 1408, 1920
ROW_PROJ, ROW_PIN, ROW_POUT, ROW_VEC = 2944, 9088, 9600, 10112
LANES = 8
ALL = ("g", "p", "x", "c")
PLANE = ("p", "x", "c")
F32, BF16 = jnp.float32, jnp.bfloat16


def params_of(mib=60, steps=1):
    return pltpu.CompilerParams(
        vmem_limit_bytes=mib << 20, dimension_semantics=("arbitrary",) * steps
    )


def whole_block(shape):
    zeros = (0,) * len(shape)
    return pl.BlockSpec(shape, lambda *_: zeros)


def sigmoid(v):
    return 1.0 / (1.0 + jnp.exp(-v))


def dot(a, b):
    return jnp.dot(a, b, preferred_element_type=F32)


def dot_nt(a, b):
    return lax.dot_general(a, b, (((1,), (1,)), ((), ())), preferred_element_type=F32)


def dot_tn(a, b):
    return lax.dot_general(a, b, (((0,), (0,)), ((), ())), preferred_element_type=F32)


def fold(v):
    return jnp.sum(v.reshape(-1, 8, v.shape[-1]), axis=0)


def unwide(wide_ref, scratch, out_ref):
    rows = wide_ref.shape[0]
    for part in range(4):
        for col in range(4):
            lanes = pl.ds(part * 512 + col * 128, 128)
            scratch[col, pl.ds(part, rows, stride=4), :] = wide_ref[:, lanes].astype(F32)
    for col in range(4):
        out_ref[:, col * 128 : (col + 1) * 128] = scratch[col].astype(BF16)


def window_kernel(off_ref, flat_ref, out_ref):
    off = off_ref[0]
    rows = out_ref.shape[0]
    for col in range(16):
        out_ref[:, col * 128 : (col + 1) * 128] = flat_ref[pl.ds(off + col, rows, stride=16), :].astype(BF16)


def flat_to_window(params, rows, shift, index, count):
    own = params.shape[0] // 128
    head = shift * count
    nxt = lax.ppermute(
        params[: head * 128].astype(BF16), ALL, [(i + 1, i) for i in range(count - 1)]
    )
    flat = jnp.concatenate([params, nxt.astype(F32), jnp.zeros((1024,), F32)]).reshape(-1, 128)
    return pl.pallas_call(
        window_kernel,
        out_shape=jax.ShapeDtypeStruct((rows, 2048), BF16),
        in_specs=[pl.BlockSpec(memory_space=pltpu.SMEM), whole_block((own + head + 8, 128))],
        out_specs=whole_block((rows, 2048)),
        compiler_params=pltpu.CompilerParams(vmem_limit_bytes=40 << 20),
    )((index * shift).astype(jnp.int32)[None], flat)


def adam(grad, params, first, second):
    new_first = BETA_ONE * first + (1.0 - BETA_ONE) * grad
    new_second = BETA_TWO * second + (1.0 - BETA_TWO) * grad * grad
    corrected_first = new_first / (1.0 - BETA_ONE**STEP)
    corrected_second = new_second / (1.0 - BETA_TWO**STEP)
    new_params = params - RATE * (
        corrected_first / (jnp.sqrt(corrected_second) + ADAM_EPS) + DECAY * params
    )
    return new_params, new_first, new_second


def adam_kernel(off_ref, tail_ref, win_ref, p_ref, m_ref, v_ref, po_ref, mo_ref, vo_ref, co_ref, flat):
    step = pl.program_id(0)

    @pl.when(step == 0)
    def _():
        tail = tail_ref.shape[0]
        rows = win_ref.shape[0]
        for col in range(16):
            lanes = pl.ds(col * 128, 128)
            flat[pl.ds(col, tail, stride=16), :] = tail_ref[:, lanes].astype(F32)
            flat[pl.ds(tail * 16 + col, rows, stride=16), :] = win_ref[:, lanes].astype(F32)

    size = p_ref.shape[0]
    grad = flat[pl.ds(off_ref[0] + step * size, size), :]
    po_ref[...], mo_ref[...], vo_ref[...] = adam(grad, p_ref[...], m_ref[...], v_ref[...])
    co_ref[...] = po_ref[...].astype(BF16)


def adam_from_window(window, shift, index, count, params, first, second):
    own = params.shape[0] // 128
    rows = window.shape[0]
    tail = -(-shift * (count - 1) // 256) * 16
    block = 512
    steps = -(-own // block)
    assert steps * block <= rows * 16
    prev = lax.ppermute(window[rows - tail :], ALL, [(i, i + 1) for i in range(count - 1)])
    off = (tail * 16 - index * shift).astype(jnp.int32)[None]
    spec = pl.BlockSpec((block, 128), lambda i: (i, 0))
    shaped = [v.reshape(own, 128) for v in (params, first, second)]
    outs = pl.pallas_call(
        adam_kernel,
        grid=(steps,),
        out_shape=[jax.ShapeDtypeStruct((own, 128), F32)] * 3 + [jax.ShapeDtypeStruct((own, 128), BF16)],
        in_specs=[pl.BlockSpec(memory_space=pltpu.SMEM), whole_block((tail, 2048)), whole_block((rows, 2048))] + [spec] * 3,
        out_specs=[spec] * 4,
        scratch_shapes=[pltpu.VMEM(((tail + rows) * 16, 128), F32)],
        compiler_params=params_of(40),
    )(off, prev, window, *shaped)
    return [v.reshape(-1) for v in outs]


def conv_in_kernel(x_ref, xh_ref, w_ref, w2_ref, wide_ref, h_ref, hh_ref, xe_ref, st_ref, wf, wb, hs, xs):
    micro, part = pl.program_id(0), pl.program_id(1)

    @pl.when((micro == 0) & (part == 0))
    def _():
        unwide(wide_ref, wf, wb)

    images = x_ref.shape[1] // 64
    h = dot(x_ref[0], wb[...])
    hh = dot(xh_ref[0], wb[...])
    for col in range(4):
        hs[col, 0 : images * 64, :] = h[:, col * 128 : (col + 1) * 128]
        hs[col, images * 64 :, :] = hh[:, col * 128 : (col + 1) * 128]

    def body(i, carry):
        at = pl.multiple_of(i * 64, 64)
        low = pl.multiple_of(i * 16, 16)
        w = jnp.broadcast_to(w_ref[0, pl.ds(at, 64), :], (64, 128))
        new = []
        for col in range(4):
            lanes = slice(col * 128, (col + 1) * 128)
            h = hs[col, pl.ds(at, 64), :] * w
            new.append((carry[col][0] + fold(h), carry[col][1] + fold(h * h)))
            hs[col, pl.ds(at, 64), :] = h
            for side in range(2):
                half = hs[col, pl.ds(at + side, 32, stride=2), :].reshape(2, 2, 8, 128)
                for row in range(2):
                    h_ref[0, 2 * row + side, pl.ds(low, 16), lanes] = half[:, row].reshape(16, 128)
                hat = pl.multiple_of(i * 8, 8)
                hh_ref[0, side, pl.ds(hat, 8), lanes] = hs[col, pl.ds(images * 64 + low + side, 8, stride=2), :]
        w = jnp.broadcast_to(w2_ref[0, pl.ds(low, 16), :], (16, 128))
        for col in range(8):
            lanes = slice(col * 128, (col + 1) * 128)
            for row in range(2):
                xs[col, row * 16 : row * 16 + 16, :] = x_ref[0, pl.ds(at + row * 32, 16), lanes].astype(F32)
            xe_ref[0, pl.ds(low, 16), lanes] = (xs[col, pl.ds(0, 16, stride=2), :] * w).astype(BF16)
        return tuple(new)

    zero = jnp.zeros((8, 128), F32)
    found = lax.fori_loop(0, images, body, ((zero, zero),) * 4)

    @pl.when(part == 0)
    def _():
        st_ref[...] = jnp.zeros_like(st_ref)

    for col in range(4):
        lanes = slice(col * 128, (col + 1) * 128)
        for k in range(2):
            st_ref[0, k : k + 1, lanes] += jnp.sum(found[col][k], axis=0, keepdims=True)


def conv_in(x, xh, w, w2, wide):
    micros, pixels, _ = x.shape
    images = pixels // 64
    parts = 2
    b = images // parts
    return pl.pallas_call(
        conv_in_kernel,
        grid=(micros, parts),
        out_shape=[
            jax.ShapeDtypeStruct((micros, 4, images * 16, MID), F32),
            jax.ShapeDtypeStruct((micros, 2, images * 8, MID), F32),
            jax.ShapeDtypeStruct((micros, images * 16, D_IN), BF16),
            jax.ShapeDtypeStruct((micros, 8, MID), F32),
        ],
        in_specs=[
            pl.BlockSpec((1, b * 64, D_IN), lambda m, k: (m, k, 0)),
            pl.BlockSpec((1, b * 16, D_IN), lambda m, k: (m, k, 0)),
            pl.BlockSpec((1, b * 64, 1), lambda m, k: (m, k, 0)),
            pl.BlockSpec((1, b * 16, 1), lambda m, k: (m, k, 0)),
            whole_block((256, 2048)),
        ],
        out_specs=[
            pl.BlockSpec((1, 4, b * 16, MID), lambda m, k: (m, 0, k, 0)),
            pl.BlockSpec((1, 2, b * 8, MID), lambda m, k: (m, 0, k, 0)),
            pl.BlockSpec((1, b * 16, D_IN), lambda m, k: (m, k, 0)),
            pl.BlockSpec((1, 8, MID), lambda m, k: (m, 0, 0)),
        ],
        scratch_shapes=[
            pltpu.VMEM((4, D_IN, 128), F32),
            pltpu.VMEM((D_IN, MID), BF16),
            pltpu.VMEM((4, b * 80, 128), F32),
            pltpu.VMEM((8, 32, 128), F32),
        ],
        compiler_params=params_of(56, 2),
        cost_estimate=pl.CostEstimate(
            flops=2 * micros * images * 80 * D_IN * MID, bytes_accessed=40 << 20, transcendentals=0
        ),
    )(x, xh, w, w2, wide)


def side_kernel(xe_ref, w_ref, hs_ref, st_ref):
    h = dot(xe_ref[0], w_ref[...])
    hs_ref[0] = h
    st_ref[...] = jnp.zeros_like(st_ref)
    st_ref[0, 0:1, :] = jnp.sum(h, axis=0, keepdims=True)
    st_ref[0, 1:2, :] = jnp.sum(h * h, axis=0, keepdims=True)


def conv_side(xe, weight):
    micros, rows, _ = xe.shape
    cols = 4
    n = OUT // cols
    return pl.pallas_call(
        side_kernel,
        grid=(micros, cols),
        out_shape=[
            jax.ShapeDtypeStruct((micros, rows, OUT), F32),
            jax.ShapeDtypeStruct((micros, 8, OUT), F32),
        ],
        in_specs=[
            pl.BlockSpec((1, rows, D_IN), lambda m, k: (m, 0, 0)),
            pl.BlockSpec((D_IN, n), lambda m, k: (0, k)),
        ],
        out_specs=[
            pl.BlockSpec((1, rows, n), lambda m, k: (m, 0, k)),
            pl.BlockSpec((1, 8, n), lambda m, k: (m, 0, k)),
        ],
        compiler_params=params_of(56, 2),
        cost_estimate=pl.CostEstimate(
            flops=2 * micros * rows * D_IN * OUT, bytes_accessed=16 << 20, transcendentals=0
        ),
    )(xe, weight)


def shift_right(v):
    moved = pltpu.roll(v, 1, 1)
    return jnp.where(lax.broadcasted_iota(jnp.int32, v.shape, 1) == 0, 0.0, moved)


def shift_left(v):
    moved = pltpu.roll(v, 7, 1)
    return jnp.where(lax.broadcasted_iota(jnp.int32, v.shape, 1) == 7, 0.0, moved)


def conv_mid_kernel(h_ref, hh_ref, cf_ref, w_ref, wh_ref, wide_ref, cols_ref, hm_ref, st_ref, wb, wf):
    micro = pl.program_id(0)

    @pl.when(micro == 0)
    def _():
        unwide(wide_ref, wf, wb)

    images = h_ref.shape[2] // 16
    scale, shift = cf_ref[0, 0:1, :], cf_ref[0, 1:2, :]

    def act(h, w):
        v = h * scale + shift
        return v * sigmoid(v) * w

    def body(i, carry):
        at = pl.ds(pl.multiple_of(i * 16, 16), 16)
        half = pl.ds(pl.multiple_of(i * 8, 8), 8)
        a = [act(h_ref[0, k, at, :], w_ref[0, k, at, :]).reshape(2, 8, MID) for k in range(4)]
        above = [act(hh_ref[0, k, half, :], wh_ref[0, k, half, :]).reshape(1, 8, MID) for k in range(2)]
        a1s, a3s = shift_right(a[1]), shift_right(a[3])
        up2 = jnp.concatenate([above[0], a[2][:1]], axis=0)
        up3 = jnp.concatenate([above[1], a[3][:1]], axis=0)
        up3s = jnp.concatenate([shift_right(above[1]), a3s[:1]], axis=0)
        for tap, value in enumerate([up3s, up2, up3, a1s, a[0], a[1], a3s, a[2], a[3]]):
            cols_ref[0, at, tap * MID : (tap + 1) * MID] = value.reshape(16, MID).astype(BF16)
        return carry

    lax.fori_loop(0, images, body, 0)
    h = dot(cols_ref[0], wb[...])
    hm_ref[0] = h
    hw = h * w_ref[0, 0]
    st_ref[...] = jnp.zeros_like(st_ref)
    st_ref[0, 0:1, :] = jnp.sum(hw, axis=0, keepdims=True)
    st_ref[0, 1:2, :] = jnp.sum(hw * hw, axis=0, keepdims=True)


def conv_mid(h, hh, coef, wph, whalo, wide):
    micros, _, rows, _ = h.shape
    return pl.pallas_call(
        conv_mid_kernel,
        grid=(micros,),
        out_shape=[
            jax.ShapeDtypeStruct((micros, rows, 9 * MID), BF16),
            jax.ShapeDtypeStruct((micros, rows, MID), F32),
            jax.ShapeDtypeStruct((micros, 8, MID), F32),
            jax.ShapeDtypeStruct((9 * MID, MID), BF16),
        ],
        in_specs=[
            pl.BlockSpec((1, 4, rows, MID), lambda m: (m, 0, 0, 0)),
            pl.BlockSpec((1, 2, rows // 2, MID), lambda m: (m, 0, 0, 0)),
            pl.BlockSpec((1, 8, MID), lambda m: (m, 0, 0)),
            pl.BlockSpec((1, 4, rows, 1), lambda m: (m, 0, 0, 0)),
            pl.BlockSpec((1, 2, rows // 2, 1), lambda m: (m, 0, 0, 0)),
            whole_block((1152, 2048)),
        ],
        out_specs=[
            pl.BlockSpec((1, rows, 9 * MID), lambda m: (m, 0, 0)),
            pl.BlockSpec((1, rows, MID), lambda m: (m, 0, 0)),
            pl.BlockSpec((1, 8, MID), lambda m: (m, 0, 0)),
            pl.BlockSpec((9 * MID, MID), lambda m: (0, 0), pipeline_mode=pl.Buffered(1)),
        ],
        scratch_shapes=[pltpu.VMEM((4, 9 * MID, 128), F32)],
        compiler_params=params_of(60),
        cost_estimate=pl.CostEstimate(
            flops=2 * micros * rows * 9 * MID * MID, bytes_accessed=50 << 20, transcendentals=0
        ),
    )(h, hh, coef, wph, whalo, wide)


def conv_out_kernel(hm_ref, cf_ref, w_ref, weight_ref, am_ref, ho_ref, st_ref):
    v = hm_ref[0] * cf_ref[0, 0:1, :] + cf_ref[0, 1:2, :]
    am = (v * sigmoid(v) * w_ref[0, 0]).astype(BF16)
    am_ref[0] = am
    st_ref[...] = jnp.zeros_like(st_ref)
    for k in range(4):
        lanes = slice(k * 512, (k + 1) * 512)
        h = dot(am, weight_ref[:, lanes])
        ho_ref[0, :, lanes] = h
        st_ref[0, 0:1, lanes] = jnp.sum(h, axis=0, keepdims=True)
        st_ref[0, 1:2, lanes] = jnp.sum(h * h, axis=0, keepdims=True)


def conv_out(hm, coef, wph, weight):
    micros, rows, _ = hm.shape
    return pl.pallas_call(
        conv_out_kernel,
        grid=(micros,),
        out_shape=[
            jax.ShapeDtypeStruct((micros, rows, MID), BF16),
            jax.ShapeDtypeStruct((micros, rows, OUT), F32),
            jax.ShapeDtypeStruct((micros, 8, OUT), F32),
        ],
        in_specs=[
            pl.BlockSpec((1, rows, MID), lambda m: (m, 0, 0)),
            pl.BlockSpec((1, 8, MID), lambda m: (m, 0, 0)),
            pl.BlockSpec((1, 1, rows, 1), lambda m: (m, 0, 0, 0)),
            whole_block((MID, OUT)),
        ],
        out_specs=[
            pl.BlockSpec((1, rows, MID), lambda m: (m, 0, 0)),
            pl.BlockSpec((1, rows, OUT), lambda m: (m, 0, 0)),
            pl.BlockSpec((1, 8, OUT), lambda m: (m, 0, 0)),
        ],
        compiler_params=params_of(56),
        cost_estimate=pl.CostEstimate(
            flops=2 * micros * rows * MID * OUT, bytes_accessed=18 << 20, transcendentals=0
        ),
    )(hm, coef, wph, weight)


def pool_kernel(ho_ref, hs_ref, cf_ref, w_ref, out_ref):
    images = out_ref.shape[1]
    so, ss, shift = cf_ref[0, 0:1, :], cf_ref[0, 1:2, :], cf_ref[0, 2:3, :]

    def body(i, carry):
        total = []
        for k in range(8):
            at = pl.ds(pl.multiple_of(i * 128 + k * 16, 16), 16)
            j = ho_ref[0, at, :] * so + hs_ref[0, at, :] * ss + shift
            r = j * sigmoid(j) * w_ref[0, 0, at, :]
            total.append(jnp.sum(r, axis=0, keepdims=True))
        out_ref[0, pl.ds(pl.multiple_of(i * 8, 8), 8), :] = jnp.concatenate(total, axis=0)
        return carry

    lax.fori_loop(0, images // 8, body, 0)


def pool(ho, hs, coef, wph):
    micros, rows, _ = ho.shape
    n = 512
    images = rows // 16
    return pl.pallas_call(
        pool_kernel,
        grid=(micros, OUT // n),
        out_shape=jax.ShapeDtypeStruct((micros, images, OUT), F32),
        in_specs=[
            pl.BlockSpec((1, rows, n), lambda m, k: (m, 0, k)),
            pl.BlockSpec((1, rows, n), lambda m, k: (m, 0, k)),
            pl.BlockSpec((1, 8, n), lambda m, k: (m, 0, k)),
            pl.BlockSpec((1, 1, rows, 1), lambda m, k: (m, 0, 0, 0)),
        ],
        out_specs=pl.BlockSpec((1, images, n), lambda m, k: (m, 0, k)),
        compiler_params=params_of(56, 2),
        cost_estimate=pl.CostEstimate(
            flops=20 * micros * rows * OUT, bytes_accessed=18 << 20, transcendentals=micros * rows * OUT
        ),
    )(ho, hs, coef, wph)


def slope_kernel(ho_ref, hs_ref, cf_ref, w_ref, out_ref):
    images = out_ref.shape[2]
    so, ss, shift = cf_ref[0, 0:1, :], cf_ref[0, 1:2, :], cf_ref[0, 2:3, :]

    def body(i, carry):
        plain, out, side = [], [], []
        for k in range(8):
            at = pl.ds(pl.multiple_of(i * 128 + k * 16, 16), 16)
            ho, hs = ho_ref[0, at, :], hs_ref[0, at, :]
            j = ho * so + hs * ss + shift
            s = sigmoid(j)
            d = s * (1.0 + j * (1.0 - s)) * w_ref[0, 0, at, :]
            plain.append(jnp.sum(d, axis=0, keepdims=True))
            out.append(jnp.sum(d * ho, axis=0, keepdims=True))
            side.append(jnp.sum(d * hs, axis=0, keepdims=True))
        at = pl.ds(pl.multiple_of(i * 8, 8), 8)
        for k, value in enumerate((plain, out, side)):
            out_ref[0, k, at, :] = jnp.concatenate(value, axis=0)
        return carry

    lax.fori_loop(0, images // 8, body, 0)


def slopes(ho, hs, coef, wph):
    micros, rows, _ = ho.shape
    n = 512
    images = rows // 16
    return pl.pallas_call(
        slope_kernel,
        grid=(micros, OUT // n),
        out_shape=jax.ShapeDtypeStruct((micros, 3, images, OUT), F32),
        in_specs=[
            pl.BlockSpec((1, rows, n), lambda m, k: (m, 0, k)),
            pl.BlockSpec((1, rows, n), lambda m, k: (m, 0, k)),
            pl.BlockSpec((1, 8, n), lambda m, k: (m, 0, k)),
            pl.BlockSpec((1, 1, rows, 1), lambda m, k: (m, 0, 0, 0)),
        ],
        out_specs=pl.BlockSpec((1, 3, images, n), lambda m, k: (m, 0, 0, k)),
        compiler_params=params_of(56, 2),
        cost_estimate=pl.CostEstimate(
            flops=30 * micros * rows * OUT, bytes_accessed=20 << 20, transcendentals=micros * rows * OUT
        ),
    )(ho, hs, coef, wph)


def back_out_kernel(
    ho_ref, hs_ref, gs_ref, cf_ref, w_ref, am_ref, xe_ref, wo_ref, hm_ref, cm_ref,
    d_ref, st_ref, gw_ref, amt, xet, da, dho, dhs, acc_out, acc_side,
):
    micro, part = pl.program_id(0), pl.program_id(1)
    parts = pl.num_programs(1)
    images = gs_ref.shape[1]

    @pl.when(part == 0)
    def _():
        amt[...] = am_ref[0].T
        xet[...] = xe_ref[0].T

    cf = [cf_ref[0, k : k + 1, :] for k in range(7)]

    def body(i, carry):
        gs = gs_ref[0, pl.ds(pl.multiple_of(i * 8, 8), 8), :]
        for k in range(8):
            at = pl.ds(pl.multiple_of(i * 128 + k * 16, 16), 16)
            ho, hs = ho_ref[0, at, :], hs_ref[0, at, :]
            w = w_ref[0, 0, at, :]
            j = ho * cf[0] + hs * cf[1] + cf[2]
            s = sigmoid(j)
            g = s * (1.0 + j * (1.0 - s)) * gs[k : k + 1, :]
            dho[at, :] = ((g * cf[0] + cf[3] + ho * cf[4]) * w).astype(BF16)
            dhs[at, :] = ((g * cf[1] + cf[5] + hs * cf[6]) * w).astype(BF16)
        return carry

    lax.fori_loop(0, images // 8, body, 0)
    g_out = dot(amt[...], dho[...])
    g_side = dot(xet[...], dhs[...])
    back = dot_nt(dho[...], wo_ref[...])

    @pl.when(micro == 0)
    def _():
        acc_out[part] = g_out
        acc_side[part] = g_side

    @pl.when(micro > 0)
    def _():
        acc_out[part] += g_out
        acc_side[part] += g_side

    @pl.when(part == 0)
    def _():
        da[...] = back

    @pl.when(part > 0)
    def _():
        da[...] += back

    @pl.when(part == parts - 1)
    def _():
        hm = hm_ref[0]
        v = hm * cm_ref[0, 0:1, :] + cm_ref[0, 1:2, :]
        s = sigmoid(v)
        d = s * (1.0 + v * (1.0 - s)) * da[...] * w_ref[0, 0]
        d_ref[0] = d
        st_ref[...] = jnp.zeros_like(st_ref)
        st_ref[0, 0:1, :] = jnp.sum(d, axis=0, keepdims=True)
        st_ref[0, 1:2, :] = jnp.sum(d * hm, axis=0, keepdims=True)

    @pl.when((micro == pl.num_programs(0) - 1) & (part == parts - 1))
    def _():
        for k in range(4):
            for half in range(2):
                lanes = slice(half * 256, half * 256 + 256)
                gw_ref[2 * k + half, 0:MID, :] = acc_out[k, :, lanes].astype(BF16)
                gw_ref[2 * k + half, MID:, :] = acc_side[k, :, lanes].astype(BF16)


def back_out(ho, hs, gs, coef, wph, am, xe, weight, hm, coef_mid):
    micros, rows, _ = ho.shape
    n = 512
    images = rows // 16
    return pl.pallas_call(
        back_out_kernel,
        grid=(micros, OUT // n),
        out_shape=[
            jax.ShapeDtypeStruct((micros, rows, MID), F32),
            jax.ShapeDtypeStruct((micros, 8, MID), F32),
            jax.ShapeDtypeStruct((LANES, MID + D_IN, 256), BF16),
        ],
        in_specs=[
            pl.BlockSpec((1, rows, n), lambda m, k: (m, 0, k)),
            pl.BlockSpec((1, rows, n), lambda m, k: (m, 0, k)),
            pl.BlockSpec((1, images, n), lambda m, k: (m, 0, k)),
            pl.BlockSpec((1, 8, n), lambda m, k: (m, 0, k)),
            pl.BlockSpec((1, 1, rows, 1), lambda m, k: (m, 0, 0, 0)),
            pl.BlockSpec((1, rows, MID), lambda m, k: (m, 0, 0)),
            pl.BlockSpec((1, rows, D_IN), lambda m, k: (m, 0, 0)),
            pl.BlockSpec((MID, n), lambda m, k: (0, k)),
            pl.BlockSpec((1, rows, MID), lambda m, k: (m, 0, 0)),
            pl.BlockSpec((1, 8, MID), lambda m, k: (m, 0, 0)),
        ],
        out_specs=[
            pl.BlockSpec((1, rows, MID), lambda m, k: (m, 0, 0)),
            pl.BlockSpec((1, 8, MID), lambda m, k: (m, 0, 0)),
            whole_block((LANES, MID + D_IN, 256)),
        ],
        scratch_shapes=[
            pltpu.VMEM((MID, rows), BF16),
            pltpu.VMEM((D_IN, rows), BF16),
            pltpu.VMEM((rows, MID), F32),
            pltpu.VMEM((rows, n), BF16),
            pltpu.VMEM((rows, n), BF16),
            pltpu.VMEM((OUT // n, MID, n), F32),
            pltpu.VMEM((OUT // n, D_IN, n), F32),
        ],
        compiler_params=params_of(60, 2),
        cost_estimate=pl.CostEstimate(
            flops=2 * micros * rows * OUT * (2 * MID + D_IN), bytes_accessed=40 << 20, transcendentals=micros * rows * OUT
        ),
    )(ho, hs, gs, coef, wph, am, xe, weight, hm, coef_mid)


def back_mid_kernel(
    hm_ref, d_ref, cm_ref, cols_ref, wb, h_ref, hh_ref, cf_ref, w_ref, wh_ref,
    din_ref, dh_ref, st_ref, gw_ref, dt, acc,
):
    micro = pl.program_id(0)
    images = h_ref.shape[2] // 16

    low = ((d_ref[0] * cm_ref[0, 0:1, :] + cm_ref[0, 1:2, :] + hm_ref[0] * cm_ref[0, 2:3, :]) * w_ref[0, 0]).astype(BF16)
    for tap in range(9):
        lanes = slice(tap * MID, (tap + 1) * MID)
        g = dot_tn(cols_ref[0, :, lanes], low)

        @pl.when(micro == 0)
        def _():
            for col in range(4):
                acc[col, lanes, :] = g[:, col * 128 : (col + 1) * 128]

        @pl.when(micro > 0)
        def _():
            for col in range(4):
                acc[col, lanes, :] += g[:, col * 128 : (col + 1) * 128]

    scale, shift = cf_ref[0, 0:1, :], cf_ref[0, 1:2, :]
    zero = jnp.zeros((8, MID), F32)

    def back(h, grad, w):
        v = h * scale + shift
        s = sigmoid(v)
        return s * (1.0 + v * (1.0 - s)) * grad * w

    def body(i, carry):
        total, product = carry
        at = pl.ds(pl.multiple_of(i * 16, 16), 16)
        half = pl.ds(pl.multiple_of(i * 8, 8), 8)
        near = pl.ds(pl.multiple_of((i % (images // 2)) * 16, 16), 16)
        t = [dt[k, near, :].reshape(2, 8, MID) for k in range(9)]
        below1 = t[1]
        below3 = t[2] + shift_left(t[0])
        last = jnp.zeros((1, 8, MID), F32)
        grads = [
            t[4],
            t[5] + shift_left(t[3]),
            t[7] + jnp.concatenate([below1[1:], last], axis=0),
            t[8] + shift_left(t[6]) + jnp.concatenate([below3[1:], last], axis=0),
        ]
        for k in range(4):
            h = h_ref[0, k, at, :]
            d = back(h, grads[k].reshape(16, MID), w_ref[0, k, at, :])
            din_ref[0, k, at, :] = d.astype(BF16)
            total = total + fold(d)
            product = product + fold(d * h)
        for k, grad in enumerate((below1, below3)):
            h = hh_ref[0, k, half, :]
            d = back(h, grad[0], wh_ref[0, k, half, :])
            dh_ref[0, k, half, :] = d
            total = total + d
            product = product + d * h
        return total, product

    found = (zero, zero)
    for part in range(2):
        start, stop = part * images // 2, (part + 1) * images // 2
        for tap in range(9):
            dt[tap] = dot_nt(low[start * 16 : stop * 16], wb[tap * MID : (tap + 1) * MID, :])
        found = lax.fori_loop(start, stop, body, found)
    total, product = found
    st_ref[...] = jnp.zeros_like(st_ref)
    st_ref[0, 0:1, :] = jnp.sum(total, axis=0, keepdims=True)
    st_ref[0, 1:2, :] = jnp.sum(product, axis=0, keepdims=True)

    @pl.when(micro == pl.num_programs(0) - 1)
    def _():
        for k in range(LANES):
            for half in range(2):
                found = acc[(k % 2) * 2 + half, pl.ds(k // 2, 9 * MID // 4, stride=4), :]
                gw_ref[k, :, half * 128 : half * 128 + 128] = found.astype(BF16)


def back_mid(hm, d, coef_mid, cols, weight, h, hh, coef, wph, whalo):
    micros, _, rows, _ = h.shape
    return pl.pallas_call(
        back_mid_kernel,
        grid=(micros,),
        out_shape=[
            jax.ShapeDtypeStruct((micros, 4, rows, MID), BF16),
            jax.ShapeDtypeStruct((micros, 2, rows // 2, MID), F32),
            jax.ShapeDtypeStruct((micros, 8, MID), F32),
            jax.ShapeDtypeStruct((LANES, 1152, 256), BF16),
        ],
        in_specs=[
            pl.BlockSpec((1, rows, MID), lambda m: (m, 0, 0)),
            pl.BlockSpec((1, rows, MID), lambda m: (m, 0, 0)),
            pl.BlockSpec((1, 8, MID), lambda m: (m, 0, 0)),
            pl.BlockSpec((1, rows, 9 * MID), lambda m: (m, 0, 0)),
            pl.BlockSpec((9 * MID, MID), lambda m: (0, 0), pipeline_mode=pl.Buffered(1)),
            pl.BlockSpec((1, 4, rows, MID), lambda m: (m, 0, 0, 0)),
            pl.BlockSpec((1, 2, rows // 2, MID), lambda m: (m, 0, 0, 0)),
            pl.BlockSpec((1, 8, MID), lambda m: (m, 0, 0)),
            pl.BlockSpec((1, 4, rows, 1), lambda m: (m, 0, 0, 0)),
            pl.BlockSpec((1, 2, rows // 2, 1), lambda m: (m, 0, 0, 0)),
        ],
        out_specs=[
            pl.BlockSpec((1, 4, rows, MID), lambda m: (m, 0, 0, 0)),
            pl.BlockSpec((1, 2, rows // 2, MID), lambda m: (m, 0, 0, 0)),
            pl.BlockSpec((1, 8, MID), lambda m: (m, 0, 0)),
            pl.BlockSpec((LANES, 1152, 256), lambda m: (0, 0, 0), pipeline_mode=pl.Buffered(1)),
        ],
        scratch_shapes=[
            pltpu.VMEM((9, rows // 2, MID), F32),
            pltpu.VMEM((4, 9 * MID, 128), F32),
        ],
        compiler_params=params_of(62),
        cost_estimate=pl.CostEstimate(
            flops=4 * micros * rows * 9 * MID * MID, bytes_accessed=60 << 20, transcendentals=micros * rows * 5 * MID
        ),
    )(hm, d, coef_mid, cols, weight, h, hh, coef, wph, whalo)


def back_in_kernel(h_ref, din_ref, dh_ref, cf_ref, w_ref, wh_ref, x_ref, xh_ref, gw_ref, ds, acc, turned):
    micro, part = pl.program_id(0), pl.program_id(1)
    images = h_ref.shape[2] // 16
    ca, cb, cc = cf_ref[0, 0:1, :], cf_ref[0, 1:2, :], cf_ref[0, 2:3, :]

    def body(i, carry):
        at = pl.ds(pl.multiple_of(i * 16, 16), 16)
        half = pl.ds(pl.multiple_of(i * 8, 8), 8)
        for k in range(4):
            h = h_ref[0, k, at, :]
            d = (din_ref[0, k, at, :].astype(F32) * ca + cb + h * cc) * w_ref[0, k, at, :]
            row, side = k // 2, k % 2
            for o in range(2):
                for col in range(4):
                    to = pl.ds(i * 64 + (2 * o + row) * 16 + side, 8, stride=2)
                    ds[col, to, :] = d[o * 8 : o * 8 + 8, col * 128 : (col + 1) * 128]
        for side in range(2):
            d = dh_ref[0, side, half, :] * ca
            for col in range(4):
                ds[col, pl.ds(images * 64 + i * 16 + side, 8, stride=2), :] = d[:, col * 128 : (col + 1) * 128]
        return carry

    lax.fori_loop(0, images, body, 0)
    low = jnp.concatenate([ds[col].astype(BF16) for col in range(4)], axis=1)
    g = dot_tn(low[: images * 64], x_ref[0]) + dot_tn(low[images * 64 :], xh_ref[0])

    @pl.when((micro == 0) & (part == 0))
    def _():
        acc[...] = g

    @pl.when((micro > 0) | (part > 0))
    def _():
        acc[...] += g

    @pl.when((micro == pl.num_programs(0) - 1) & (part == pl.num_programs(1) - 1))
    def _():
        for col in range(4):
            turned[col] = acc[col * 128 : (col + 1) * 128, :].T
        for k in range(LANES):
            for half in range(2):
                found = turned[(k % 2) * 2 + half, pl.ds(k // 2, D_IN // 4, stride=4), :]
                gw_ref[k, :, half * 128 : half * 128 + 128] = found.astype(BF16)


def back_in(h, din, dhalo, coef, wph, whalo, x, xh):
    micros, _, rows, _ = h.shape
    parts = 2
    r = rows // parts
    return pl.pallas_call(
        back_in_kernel,
        grid=(micros, parts),
        out_shape=jax.ShapeDtypeStruct((LANES, 256, 256), BF16),
        in_specs=[
            pl.BlockSpec((1, 4, r, MID), lambda m, k: (m, 0, k, 0)),
            pl.BlockSpec((1, 4, r, MID), lambda m, k: (m, 0, k, 0)),
            pl.BlockSpec((1, 2, r // 2, MID), lambda m, k: (m, 0, k, 0)),
            pl.BlockSpec((1, 8, MID), lambda m, k: (m, 0, 0)),
            pl.BlockSpec((1, 4, r, 1), lambda m, k: (m, 0, k, 0)),
            pl.BlockSpec((1, 2, r // 2, 1), lambda m, k: (m, 0, k, 0)),
            pl.BlockSpec((1, r * 4, D_IN), lambda m, k: (m, k, 0)),
            pl.BlockSpec((1, r, D_IN), lambda m, k: (m, k, 0)),
        ],
        out_specs=whole_block((LANES, 256, 256)),
        scratch_shapes=[
            pltpu.VMEM((4, r * 5, 128), F32),
            pltpu.VMEM((MID, D_IN), F32),
            pltpu.VMEM((4, D_IN, 128), F32),
        ],
        compiler_params=params_of(60, 2),
        cost_estimate=pl.CostEstimate(
            flops=2 * micros * rows * 5 * D_IN * MID, bytes_accessed=50 << 20, transcendentals=0
        ),
    )(h, din, dhalo, coef, wph, whalo, x, xh)


def swap(value, axis, bit):
    size = lax.axis_size(axis)
    return lax.ppermute(value, axis, [(i, i ^ bit) for i in range(size)])


def bits_of(axis):
    size, bit, found = lax.axis_size(axis), 1, []
    while bit < size:
        found.append(bit)
        bit *= 2
    return found


def add_all(value, axes=("c", "x", "p", "g")):
    for axis in axes:
        for bit in bits_of(axis):
            value = value + swap(value, axis, bit)
    return value


def exchange_planes(value):
    planes = lax.axis_size("g")
    here = lax.axis_index("g")
    own = lax.dynamic_index_in_dim(value, here, 0, keepdims=True)
    result = lax.dynamic_update_slice_in_dim(jnp.zeros_like(value), own, here, 0)
    for step in range(1, planes):
        block = lax.dynamic_index_in_dim(value, (here + step) % planes, 0, keepdims=True)
        got = lax.ppermute(block, "g", [(i, (i + step) % planes) for i in range(planes)])
        result = lax.dynamic_update_slice_in_dim(result, got, (here + planes - step) % planes, 0)
    return result


def gather_axis(value, axis):
    value = value[None]
    for bit in bits_of(axis):
        other = swap(value, axis, bit)
        mine = (lax.axis_index(axis) // bit) % 2
        value = jnp.where(mine == 0, jnp.concatenate([value, other]), jnp.concatenate([other, value]))
    return value


def to_heads(value):
    routed = exchange_planes(value)
    for axis in ("p", "x", "c"):
        routed = gather_axis(routed, axis)
    order = (3, 2, 1, 0, 4) + tuple(range(5, routed.ndim))
    routed = jnp.transpose(routed, order)
    return routed.reshape((-1,) + value.shape[2:])


def norm_ranges():
    widths = [MID, MID, OUT, OUT, OUT, OUT, OUT, PRED]
    return [(sum(widths[:layer]), widths[layer]) for layer in range(8)]


def silu_back(value, grad):
    gate = jax.nn.sigmoid(value)
    return grad * gate * (1.0 + value * (1.0 - gate))


def head_norm(hidden, gamma, beta):
    count = hidden.shape[0]
    average = jnp.sum(hidden, axis=0) / count
    variance = jnp.sum(hidden * hidden, axis=0) / count - average * average
    scale = lax.rsqrt(variance + EPS_NORM)
    normed = (hidden - average) * scale
    return gamma * normed + beta, (normed, scale), average, variance


def head_norm_back(grad, kept, gamma):
    normed, scale = kept
    count = grad.shape[0]
    beta_sum = jnp.sum(grad, axis=0)
    gamma_sum = jnp.sum(grad * normed, axis=0)
    back = gamma * scale * (grad - beta_sum / count - normed * gamma_sum / count)
    return back, gamma_sum, beta_sum


def heads(pooled_low, wall, gammas, betas, bias, partner, live):
    project = [wall[ROW_PROJ + 2048 * k : ROW_PROJ + 2048 * (k + 1)] for k in range(3)]
    predict_in = wall[ROW_PIN:ROW_POUT].reshape(OUT, PRED)
    predict_out = wall[ROW_POUT:ROW_VEC]
    means, variances, kept_all, normed_all, lows = [], [], [], [], []
    low = pooled_low
    for k in range(3):
        normed, kept, mean, variance = head_norm(dot(low, project[k]), gammas[4 + k], betas[4 + k])
        means.append(mean)
        variances.append(variance)
        kept_all.append(kept)
        normed_all.append(normed)
        lows.append(low)
        low = (jax.nn.silu(normed) if k < 2 else normed).astype(BF16)
    latent, latent_low = normed, low
    normed_q, kept_q, mean, variance = head_norm(dot(latent_low, predict_in), gammas[7], betas[7])
    means.append(mean)
    variances.append(variance)
    act = jax.nn.silu(normed_q).astype(BF16)
    predicted = dot(act, predict_out) + bias
    choose = (partner[:, None] == jnp.arange(latent.shape[0])[None, :]).astype(F32)
    target = jnp.dot(choose, latent, precision=lax.Precision.HIGHEST)
    inner = jnp.sum(predicted * target, axis=-1)
    inv_pred = lax.rsqrt(jnp.sum(predicted * predicted, axis=-1) + COS_EPS)
    inv_goal = lax.rsqrt(jnp.sum(target * target, axis=-1) + COS_EPS)
    flags = live.astype(F32)
    loss_sum = -jnp.sum(flags * inner * inv_pred * inv_goal)
    live_count = jnp.sum(flags)
    grad_cos = -flags / live_count
    grad_pred = grad_cos[:, None] * (
        target * (inv_pred * inv_goal)[:, None] - (inner * inv_pred**3 * inv_goal)[:, None] * predicted
    )
    grad_bias = jnp.sum(grad_pred, axis=0)
    low_p = grad_pred.astype(BF16)
    grad_act = dot_nt(low_p, predict_out)
    grad_q, gamma_q, beta_q = head_norm_back(silu_back(normed_q, grad_act), kept_q, gammas[7])
    low_q = grad_q.astype(BF16)
    grad_act = dot_nt(low_q, predict_in)
    low_f, gamma_sums, beta_sums = [None] * 3, [None] * 3, [None] * 3
    for k in (2, 1, 0):
        grad_normed = grad_act if k == 2 else silu_back(normed_all[k], grad_act)
        grad_hidden, gamma_sums[k], beta_sums[k] = head_norm_back(grad_normed, kept_all[k], gammas[4 + k])
        low_f[k] = grad_hidden.astype(BF16)
        grad_act = dot_nt(low_f[k], project[k])
    block = (lax.axis_index("p") % 2) * 4 + lax.axis_index("x") * 2 + lax.axis_index("c")

    def columns(v, start):
        return lax.dynamic_slice_in_dim(v, start, 256, 1)

    rows = [dot_tn(lows[k], columns(low_f[k], block * 256)).astype(BF16) for k in range(3)]
    g_in = dot_tn(latent_low, columns(low_q, (block % 2) * 256)).astype(BF16)
    rows.append(lax.dynamic_index_in_dim(g_in.reshape(PRED, 4, 256), block // 2, 1, keepdims=False))
    rows.append(dot_tn(act, columns(low_p, block * 256)).astype(BF16))
    vector = (gamma_sums + [gamma_q], beta_sums + [beta_q], grad_bias)
    return grad_act, jnp.concatenate(rows, axis=0), vector, block, loss_sum, live_count, means, variances


def norm_coefs(sums, total, gamma, beta):
    mean = sums[:, 0] / total[:, None]
    variance = sums[:, 1] / total[:, None] - mean * mean
    scale = lax.rsqrt(variance + EPS_NORM)
    a = gamma * scale
    return mean, variance, scale, a, beta - a * mean


def pack(rows):
    rows = list(rows) + [jnp.zeros_like(rows[0])] * (8 - len(rows))
    return jnp.stack(rows, axis=1)


def back_coefs(grad_sum, product_sum, mean, scale, a, total):
    gamma_sum = scale * (product_sum - mean * grad_sum)
    c = -a * scale * gamma_sum / total[:, None]
    b = -a * grad_sum / total[:, None] - c * mean
    return b, c, gamma_sum


def on_device(inputs, masks, partner, live, params, first, second, running):
    count = lax.axis_size(ALL)
    index = lax.axis_index(ALL)
    plane = lax.axis_index("g")
    own = params.shape[0] // 128
    micros, images, rows, width, _ = inputs.shape
    out_rows, out_cols = rows // 2, width // 2
    window_rows = -(-own // 256) * 16
    shift = window_rows * 16 - own
    near = shift * count <= own and window_rows * count % (16 * lax.axis_size("g")) == 0 and lax.axis_size(PLANE) == LANES

    around = [(i, i + 1) for i in range(lax.axis_size(("x", "c")) - 1)]
    x_halo = lax.ppermute(inputs[:, :, -1], ("x", "c"), around).reshape(micros, images * width, D_IN)
    mask = masks.astype(F32)
    mask_halo = lax.ppermute(masks[:, :, -1], ("x", "c"), around).astype(F32)
    x = inputs.reshape(micros, images * rows * width, D_IN)

    if near:
        wall = lax.all_gather(flat_to_window(params, window_rows, shift, index, count), ALL, axis=0, tiled=True)
    else:
        wall = lax.all_gather(params.astype(BF16), ALL, axis=0, tiled=True).reshape(-1, 2048)

    w_in = mask.reshape(micros, -1, 1)
    split = mask.reshape(micros, images, out_rows, 2, out_cols, 2)
    wph = jnp.transpose(split, (0, 3, 5, 1, 2, 4)).reshape(micros, 4, -1, 1)
    whalo = jnp.transpose(mask_halo.reshape(micros, images, out_cols, 2), (0, 3, 1, 2)).reshape(micros, 2, -1, 1)
    total_in = jnp.sum(mask, axis=(1, 2, 3))
    image_pixels = jnp.sum(split[:, :, :, 0, :, 0], axis=(2, 3))
    image_pixels = add_all(image_pixels, ("c", "x"))
    totals = add_all(
        jnp.stack([total_in, jnp.sum(image_pixels, axis=1) / lax.axis_size(("x", "c"))]), ("c", "x", "p", "g")
    )
    total_in, total_out = totals[0], totals[1]
    partner_all, live_all = to_heads(partner), to_heads(live)
    share_index = lax.axis_index(("x", "c"))

    vec = wall[ROW_VEC : ROW_VEC + 16].astype(F32).reshape(-1)
    ranges = norm_ranges()
    gammas = [vec[start : start + n] for start, n in ranges]
    betas = [vec[NORM + start : NORM + start + n] for start, n in ranges]
    bias = vec[2 * NORM : 2 * NORM + OUT]

    h, hh, xe, st = conv_in(x, x_halo, w_in, wph[:, 0], wall[ROW_CIN:ROW_CMID])
    sums = add_all(st)
    mean_in, var_in, scale_in, a_in, b_in = norm_coefs(sums, total_in, gammas[0], betas[0])
    coef_in = pack([a_in, b_in])
    hs, st_side = conv_side(xe, wall[ROW_SIDE:ROW_PROJ])
    cols, hm, st, w_mid = conv_mid(h, hh, coef_in, wph, whalo, wall[ROW_CMID:ROW_COUT])
    sums = add_all(jnp.concatenate([st[:, :2], st_side[:, :2]], axis=2))
    mean_mid, var_mid, scale_mid, a_mid, b_mid = norm_coefs(sums[..., :MID], total_out, gammas[1], betas[1])
    mean_side, var_side, scale_side, a_side, b_side = norm_coefs(sums[..., MID:], total_out, gammas[3], betas[3])
    am, ho, st = conv_out(hm, pack([a_mid, b_mid]), wph, wall[ROW_COUT:ROW_SIDE])
    sums = add_all(st[:, :2])
    mean_out, var_out, scale_out, a_out, b_out = norm_coefs(sums, total_out, gammas[2], betas[2])
    coef_join = pack([a_out, a_side, b_out + b_side])
    pooled = pool(ho, hs, coef_join, wph)
    for axis in ("x", "c"):
        half = pooled.shape[1] // 2
        here = lax.axis_index(axis)
        keep = lax.dynamic_slice_in_dim(pooled, here * half, half, 1)
        send = lax.dynamic_slice_in_dim(pooled, (1 - here) * half, half, 1)
        pooled = keep + swap(send, axis, 1)
    share = pooled.shape[1]
    share_pixels = lax.dynamic_slice_in_dim(image_pixels, share_index * share, share, 1)
    pooled_low = to_heads((pooled / share_pixels[..., None]).astype(BF16))
    slope = slopes(ho, hs, coef_join, wph)

    grad_pool, head_rows, head_vec, block, loss_sum, live_count, head_means, head_vars = heads(
        pooled_low, wall, gammas, betas, bias, partner_all, live_all
    )

    grad_pool = grad_pool.astype(BF16).reshape(lax.axis_size("g"), lax.axis_size("p"), images, OUT)
    grad_pool = lax.dynamic_index_in_dim(grad_pool, lax.axis_index("p"), 1, keepdims=False)
    gs = exchange_planes(grad_pool).astype(F32) / image_pixels[..., None]

    sums = add_all(jnp.sum(gs[:, None] * slope, axis=2))
    bo, co, gamma_out = back_coefs(sums[:, 0], sums[:, 1], mean_out, scale_out, a_out, total_out)
    bs, cs, gamma_side = back_coefs(sums[:, 0], sums[:, 2], mean_side, scale_side, a_side, total_out)
    beta_joined = sums[:, 0]
    coef_back = pack([a_out, a_side, b_out + b_side, bo, co, bs, cs])
    d_mid, st, g_out = back_out(
        ho, hs, gs, coef_back, wph, am, xe, wall[ROW_COUT:ROW_SIDE], hm, pack([a_mid, b_mid])
    )
    sums = add_all(st[:, :2])
    bm, cm, gamma_mid = back_coefs(sums[:, 0], sums[:, 1], mean_mid, scale_mid, a_mid, total_out)
    beta_mid = sums[:, 0]
    d_in, d_halo, st, g_mid = back_mid(
        hm, d_mid, pack([a_mid, bm, cm]), cols, w_mid, h, hh, coef_in, wph, whalo
    )
    sums = add_all(st[:, :2])
    bi, ci, gamma_in = back_coefs(sums[:, 0], sums[:, 1], mean_in, scale_in, a_in, total_in)
    beta_in = sums[:, 0]
    g_in = back_in(h, d_in, d_halo, pack([a_in, bi, ci]), wph, whalo, x, x_halo)

    first_plane = (plane == 0).astype(F32)
    trunk_gamma = [jnp.sum(v, axis=0) * first_plane for v in (gamma_in, gamma_mid, gamma_out, gamma_side)]
    trunk_beta = [jnp.sum(v, axis=0) * first_plane for v in (beta_in, beta_mid, beta_joined, beta_joined)]
    vector = jnp.concatenate(trunk_gamma + head_vec[0] + trunk_beta + head_vec[1] + [head_vec[2]])
    vector = jnp.pad(vector, (0, 16 * 2048 - vector.shape[0])).astype(BF16).reshape(16, 2048)
    vector = lax.dynamic_slice_in_dim(vector, block * 256, 256, 1)
    trunk = jnp.concatenate([g_in, g_mid, g_out], axis=1)

    if near:
        head_part = jnp.concatenate(
            [head_rows, vector, jnp.zeros((window_rows * count - ROW_VEC - 16, 256), BF16)], axis=0
        )
        trunk = lax.psum_scatter(trunk, PLANE, scatter_dimension=0, tiled=False)
        part = jnp.concatenate([trunk, head_part], axis=0)
        part = lax.psum_scatter(part, "g", scatter_dimension=0, tiled=True)
        window = lax.all_to_all(part, PLANE, 0, 1, tiled=True)
        new_params, new_first, new_second, new_copy = adam_from_window(
            window, shift, index, count, params, first, second
        )
    else:
        alone = (lax.axis_index("p") < 2).astype(BF16)
        head_part = jnp.concatenate([head_rows, vector], axis=0) * alone
        head_part = lax.dynamic_update_slice(
            jnp.zeros((head_part.shape[0], 2048), BF16), head_part, (jnp.int32(0), (block * 256).astype(jnp.int32))
        )
        trunk = jnp.transpose(trunk, (1, 0, 2)).reshape(-1, 2048)
        flat = jnp.concatenate([trunk, head_part], axis=0).reshape(-1)
        flat = flat[: params.shape[0] * count]
        grad = lax.psum_scatter(flat, ALL, scatter_dimension=0, tiled=True).astype(F32)
        new_params, new_first, new_second = adam(grad, params, first, second)
        new_copy = new_params.astype(BF16)

    head_stats = jnp.stack([jnp.concatenate(head_means), jnp.concatenate(head_vars)])
    scalars = jnp.stack([loss_sum, live_count])
    head_stats = exchange_planes(jnp.broadcast_to(head_stats[None], (micros,) + head_stats.shape))
    scalars = exchange_planes(jnp.broadcast_to(scalars[None], (micros, 2)))
    averages = jnp.concatenate([mean_in, mean_mid, mean_out, mean_side, head_stats[:, 0]], axis=1)
    spreads = jnp.concatenate([var_in, var_mid, var_out, var_side, head_stats[:, 1]], axis=1)
    stats = jnp.stack([averages, spreads], axis=1)
    new_running = running
    for micro in range(micros):
        new_running = (1.0 - MOMENTUM) * new_running + MOMENTUM * stats[micro]
    return (
        scalars[:, 0],
        scalars[:, 1].astype(jnp.int32),
        new_params,
        new_first,
        new_second,
        new_copy,
        new_running,
    )


def solution(mesh):
    img, rows = mesh.shape["img"], mesh.shape["rows"]
    fine = Mesh(mesh.devices.reshape(MB, img // MB, 2, rows // 2), ALL)
    split = P(ALL)
    placed = (
        P(None, ("g", "p"), ("x", "c"), None, None),
        P(None, ("g", "p"), ("x", "c"), None),
        P(None, ALL),
        P(None, ALL),
        split,
        split,
        split,
        P(),
    )
    return jax.shard_map(
        on_device,
        mesh=fine,
        in_specs=placed,
        out_specs=(P(), P(), split, split, split, split, P()),
        check_vma=False,
    )
```

profile of v0, /device:TPU:4, one launch (start us, length us, event | category | flops | bytes accessed | tf_op | source)
XLA Modules:
  0.0 1090.5 jit_solution(12581671156689015764)
XLA Ops:
  11.3 6.0 collective-permute-done.6
  21.7 5.0 slice_bitcast_fusion
  26.7 4.8 collective-permute-start.7
  44.7 68.0 %collective-permute-start.15 = (f32[2,4]{1,0:T(2,128)S(1)}, f32[2,4]{1,0:T(2,128)S(1)}, u32[]{:S(2)}, u32[]{:S(2)}) collective-permute-start(f32[2,4]{1,0:T(2,128)S(1)} %pad_maximum_fusion.8), channel_id=1, source_target_pairs={{0,1},{1,0},{2,3},{3,2},{4,5},{5,4},{6,7},{7,6},{8,9},{9,8},{10,11... | collective-permute-start | bytes 104 | tf_op jit(solution)/shard_map/ppermute | solution.py:790
  116.2 157.7 %all-gather.2.cloned.1.call-done = bf16[10240,2048]{1,0:T(8,128)(2,1)} async-done(((bf16[320,2048]{1,0:T(8,128)(2,1)}), bf16[10240,2048]{1,0:T(8,128)(2,1)}) %all-gather.2.cloned.1.call-update) | async-done | bytes 41943056 | tf_op jit(solution)/shard_map/all_gather | solution.py:961
  276.2 33.7 %shard_map.136 = (f32[4,4,512,512]{3,2,1,0:T(8,128)}, f32[4,2,256,512]{3,2,1,0:T(8,128)}, bf16[4,512,1024]{2,1,0:T(8,128)(2,1)}, f32[4,8,512]{2,1,0:T(8,128)}) custom-call(bf16[4,2048,1024]{2,1,0:T(8,128)(2,1)} %bitcast.251, bf16[4,512,1024]{2,1,0:T(8,128)(2,1)} %bitcast.13.xh_ref, f32[4,2048,1]{2,1,0:T(8,128)} %reshape.1201.w_ref, ...), custom_call_target="tpu_custom_call" | custom-call | flops 10737418240 | bytes 41943040 | tf_op jit(solution)/shard_map/pallas_call | solution.py:206
  325.7 4.8 slice.284.w_ref
  331.9 22.6 %shard_map.138 = (f32[4,512,2048]{2,1,0:T(8,128)}, f32[4,8,2048]{2,1,0:T(8,128)}) custom-call(bf16[4,512,1024]{2,1,0:T(8,128)(2,1)} %get-tuple-element.36.xe_ref, bf16[1024,2048]{1,0:T(8,128)(2,1)} %slice.284.w_ref), custom_call_target="tpu_custom_call" | custom-call | flops 8589934592 | bytes 16777216 | tf_op jit(solution)/shard_map/pallas_call | solution.py:253
  361.6 5.2 slice.281.wide_ref
  367.7 31.3 %shard_map.137 = (bf16[4,512,4608]{2,1,0:T(8,128)(2,1)}, f32[4,512,512]{2,1,0:T(8,128)}, f32[4,8,512]{2,1,0:T(8,128)}, bf16[4608,512]{1,0:T(8,128)(2,1)}) custom-call(f32[4,4,512,512]{3,2,1,0:T(8,128)} %get-tuple-element.31.h_ref, f32[4,2,256,512]{3,2,1,0:T(8,128)} %get-tuple-element.32.hh_ref, f32[4,8,512]{2,1,0:T(8,128)} %pad_maximum_fusion.2.cf_ref, ...), custom_call_target="tpu_custom_call" | custom-call | flops 9663676416 | bytes 52428800 | tf_op jit(solution)/shard_map/pallas_call | solution.py:323
  417.8 4.8 fusion.115
  423.6 11.6 %shard_map.139 = (bf16[4,512,512]{2,1,0:T(8,128)(2,1)}, f32[4,512,2048]{2,1,0:T(8,128)}, f32[4,8,2048]{2,1,0:T(8,128)}) custom-call(f32[4,512,512]{2,1,0:T(8,128)} %get-tuple-element.34.hm_ref, f32[4,8,512]{2,1,0:T(8,128)} %pad_maximum_fusion.1.cf_ref.cm_ref, f32[4,4,512,1]{3,2,1,0:T(8,128)} %copy.164.w_ref, ...), custom_call_target="tpu_custom_call" | custom-call | flops 4294967296 | bytes 18874368 | tf_op jit(solution)/shard_map/pallas_call | solution.py:369
  451.4 4.9 collective-permute-done.30
  457.8 19.6 %shard_map.140 = f32[4,32,2048]{2,1,0:T(8,128)} custom-call(f32[4,512,2048]{2,1,0:T(8,128)} %get-tuple-element.38.ho_ref, f32[4,512,2048]{2,1,0:T(8,128)} %get-tuple-element.39.hs_ref, f32[4,8,2048]{2,1,0:T(8,128)} %stack.41.cf_ref, f32[4,4,512,1]{3,2,1,0:T(8,128)} %copy.164.w_ref), custom_call_target="tpu_custom_call" | custom-call | flops 83886080 | bytes 18874368 | tf_op jit(solution)/shard_map/pallas_call | solution.py:416
  479.4 8.7 collective-permute-done.31
  531.1 23.5 %shard_map.141 = f32[4,3,32,2048]{3,2,1,0:T(8,128)} custom-call(f32[4,512,2048]{2,1,0:T(8,128)} %get-tuple-element.38.ho_ref, f32[4,512,2048]{2,1,0:T(8,128)} %get-tuple-element.39.hs_ref, f32[4,8,2048]{2,1,0:T(8,128)} %stack.41.cf_ref, f32[4,4,512,1]{3,2,1,0:T(8,128)} %copy.164.w_ref), custom_call_target="tpu_custom_call" | custom-call | flops 125829120 | bytes 20971520 | tf_op jit(solution)/shard_map/pallas_call | solution.py:461
  554.7 6.2 fusion.109
  561.0 6.7 fusion.108
  567.8 6.6 fusion.107
  587.2 6.0 fusion.105
  594.4 6.0 fusion.104
  601.6 6.1 fusion.27
  639.6 5.1 collective-permute-done.55
  646.0 53.2 %shard_map.142 = (f32[4,512,512]{2,1,0:T(8,128)}, f32[4,8,512]{2,1,0:T(8,128)}, bf16[8,1536,256]{2,1,0:T(8,128)(2,1)}) custom-call(f32[4,512,2048]{2,1,0:T(8,128)} %get-tuple-element.38.ho_ref, f32[4,512,2048]{2,1,0:T(8,128)} %get-tuple-element.39.hs_ref, f32[4,32,2048]{2,1,0:T(8,128)} %copy-done.6, f32[4,8,2048]{2,1,0:T(8,128)} %copy.193.cf_ref, ...), custom_call_target="tpu_custom_call" | custom-call | flops 17179869184 | bytes 41943040 | tf_op jit(solution)/shard_map/pallas_call | solution.py:554
  719.1 59.9 %shard_map.143 = (bf16[4,4,512,512]{3,2,1,0:T(8,128)(2,1)}, f32[4,2,256,512]{3,2,1,0:T(8,128)}, f32[4,8,512]{2,1,0:T(8,128)}, bf16[8,1152,256]{2,1,0:T(8,128)(2,1)}) custom-call(f32[4,512,512]{2,1,0:T(8,128)} %get-tuple-element.34.hm_ref, f32[4,512,512]{2,1,0:T(8,128)} %get-tuple-element.42.d_ref, f32[4,8,512]{2,1,0:T(8,128)} %stack.88.cm_ref, ...), custom_call_target="tpu_custom_call" | custom-call | flops 19327352832 | bytes 62914560 | tf_op jit(solution)/shard_map/pallas_call | solution.py:675
  798.6 29.9 %shard_map.144 = bf16[8,256,256]{2,1,0:T(8,128)(2,1)} custom-call(f32[4,4,512,512]{3,2,1,0:T(8,128)} %get-tuple-element.31.h_ref, bf16[4,4,512,512]{3,2,1,0:T(8,128)(2,1)} %get-tuple-element.46.din_ref, f32[4,2,256,512]{3,2,1,0:T(8,128)} %get-tuple-element.47.dh_ref, f32[4,8,512]{2,1,0:T(8,128)} %stack.89.cf_ref, f32[4,4,512,1]{3,2,1,0:T(8,128)} %copy.164.w_ref, ...), custom_call_target="tpu_custom_call" | custom-call | flops 10737418240 | bytes 52428800 | tf_op jit(solution)/shard_map/pallas_call | solution.py:761
  828.5 9.2 pad_maximum_fusion
  847.3 79.7 %reduce-scatter.3.cloned.1.call-done = bf16[1,2944,256]{2,1,0:T(8,128)(2,1)} async-done(((bf16[8,2944,256]{2,1,0:T(8,128)(2,1)}), bf16[1,2944,256]{2,1,0:T(8,128)(2,1)}) %reduce-scatter.3.cloned.1.call-update) | async-done | bytes 1507344 | tf_op jit(solution)/shard_map/reduce_scatter | solution.py:1049
  961.6 78.4 %reduce-scatter.5.cloned.1.call-done = bf16[2560,256]{1,0:T(8,128)(2,1)} async-done(((bf16[10240,256]{1,0:T(8,128)(2,1)}), bf16[2560,256]{1,0:T(8,128)(2,1)}) %reduce-scatter.5.cloned.1.call-update) | async-done | bytes 1310736 | tf_op jit(solution)/shard_map/reduce_scatter | solution.py:1051
  1045.1 16.4 %all-to-all-done = bf16[8,320,256]{2,1,0:T(8,128)(2,1)} async-done(((bf16[8,320,256]{2,1,0:T(8,128)(2,1)}), bf16[8,320,256]{2,1,0:T(8,128)(2,1)}, u32[]{:S(2)}, u32[]{:S(2)}) %all-to-all-start) | async-done | bytes 1310752 | tf_op jit(solution)/shard_map/all_to_all | solution.py:1052
  1067.3 6.2 collective-permute-done.66.tail_ref
  1075.3 8.6 shard_map.145
  (606 shorter events, 277.1 us)
Async XLA Ops:
  7.2 266.7 %all-gather.2.cloned.1.call-start = ((), (), s32[]{:S(2)}) async-start(), calls=%async_computation.3 | async-start | bytes 43253760 | tf_op jit(solution)/shard_map/all_gather | solution.py:961
  8.4 8.9 collective-permute-start.6
  21.6 905.4 %reduce-scatter.3.cloned.1.call-start = ((), (), s32[]{:S(2)}) async-start(), calls=%async_computation.4 | async-start | bytes 13565952 | tf_op jit(solution)/shard_map/reduce_scatter | solution.py:1049
  26.7 249.5 %collective-permute-start.7 = (bf16[4,32,16,1024]{3,2,1,0:T(8,128)(2,1)}, bf16[4,32,16,1024]{3,2,1,0:T(8,128)(2,1)}, u32[]{:S(2)}, u32[]{:S(2)}) collective-permute-start(bf16[4,32,16,1024]{3,2,1,0:T(8,128)(2,1)} %slice_bitcast_fusion), channel_id=1, source_target_pairs={{0,1},{1,2},{2,3},{4,5},{5,6},{6,7},{8,9},{9,10},{10,11},{12,13},{... | collective-permute-start | bytes 12582920 | tf_op jit(solution)/shard_map/ppermute | solution.py:955
  31.6 292.7 %collective-permute-start.20 = (s32[4,32,16]{1,2,0:T(8,128)S(1)}, s32[4,32,16]{1,2,0:T(8,128)S(1)}, u32[]{:S(2)}, u32[]{:S(2)}) collective-permute-start(s32[4,32,16]{1,2,0:T(8,128)S(1)} %slice_bitcast_fusion.4), channel_id=1, source_target_pairs={{0,1},{1,2},{2,3},{4,5},{5,6},{6,7},{8,9},{9,10},{10,11},{12,13},{... | collective-permute-start | bytes 24584 | tf_op jit(solution)/shard_map/ppermute | solution.py:957
  36.3 8.3 collective-permute-start.14
  44.7 68.8 %collective-permute-start.15 = (f32[2,4]{1,0:T(2,128)S(1)}, f32[2,4]{1,0:T(2,128)S(1)}, u32[]{:S(2)}, u32[]{:S(2)}) collective-permute-start(f32[2,4]{1,0:T(2,128)S(1)} %pad_maximum_fusion.8), channel_id=1, source_target_pairs={{0,1},{1,0},{2,3},{3,2},{4,5},{5,4},{6,7},{7,6},{8,9},{9,8},{10,11... | collective-permute-start | bytes 104 | tf_op jit(solution)/shard_map/ppermute | solution.py:790
  113.5 197.5 %collective-permute-start.16 = (f32[2,4]{1,0:T(2,128)S(1)}, f32[2,4]{1,0:T(2,128)S(1)}, u32[]{:S(2)}, u32[]{:S(2)}) collective-permute-start(f32[2,4]{1,0:T(2,128)S(1)} %fusion.100), channel_id=1, source_target_pairs={{0,2},{2,0},{1,3},{3,1},{4,6},{6,4},{5,7},{7,5},{8,10},{10,8},{9,1... | collective-permute-start | bytes 104 | tf_op jit(solution)/shard_map/ppermute | solution.py:790
  310.7 12.0 %collective-permute-start.8 = (f32[4,8,512]{2,0,1:T(4,128)S(1)}, f32[4,8,512]{2,0,1:T(4,128)S(1)}, u32[]{:S(2)}, u32[]{:S(2)}) collective-permute-start(f32[4,8,512]{2,0,1:T(4,128)S(1)} %copy.160), channel_id=1, source_target_pairs={{0,1},{1,0},{2,3},{3,2},{4,5},{5,4},{6,7},{7,6},{8,9},{9,8},{10,11... | collective-permute-start | bytes 196616 | tf_op jit(solution)/shard_map/ppermute | solution.py:790
  323.7 6.9 collective-permute-start.9
  330.6 23.9 %collective-permute-start.10 = (f32[4,8,512]{2,0,1:T(4,128)S(1)}, f32[4,8,512]{2,0,1:T(4,128)S(1)}, u32[]{:S(2)}, u32[]{:S(2)}) collective-permute-start(f32[4,8,512]{2,0,1:T(4,128)S(1)} %add.551), channel_id=1, source_target_pairs={{0,4},{4,0},{1,5},{5,1},{2,6},{6,2},{3,7},{7,3},{8,12},{12,8},{9,1... | collective-permute-start | bytes 196616 | tf_op jit(solution)/shard_map/ppermute | solution.py:790
  359.3 7.4 collective-permute-start.12
  415.0 7.6 collective-permute-start.25
  478.5 9.6 collective-permute-start.31
  489.3 11.6 %collective-permute-start.32 = (f32[4,8,2048]{2,1,0:T(8,128)S(1)}, f32[4,8,2048]{2,1,0:T(8,128)S(1)}, u32[]{:S(2)}, u32[]{:S(2)}) collective-permute-start(f32[4,8,2048]{2,1,0:T(8,128)S(1)} %constant_dynamic-slice_fusion.10), channel_id=1, source_target_pairs={{0,1},{1,0},{2,3},{3,2},{4,5},{5,4},{6,7},{7,6},{8,9},{9,8},{10,11... | collective-permute-start | bytes 786440 | tf_op jit(solution)/shard_map/ppermute | solution.py:790
  489.8 8.7 collective-permute-start.2
  498.6 12.2 %collective-permute-start.3 = (s32[1,4,8]{2,1,0:T(4,128)S(1)}, s32[1,4,8]{2,1,0:T(4,128)S(1)}, u32[]{:S(2)}, u32[]{:S(2)}) collective-permute-start(s32[1,4,8]{2,1,0:T(4,128)S(1)} %dynamic_update_slice.87), channel_id=1, source_target_pairs={{0,4},{4,0},{1,5},{5,1},{2,6},{6,2},{3,7},{7,3},{8,12},{12,8},{9,1... | collective-permute-start | bytes 392 | tf_op jit(solution)/shard_map/ppermute | solution.py:790
  499.8 16.2 %collective-permute-start.42 = (s32[1,4,8]{2,1,0:T(4,128)S(1)}, s32[1,4,8]{2,1,0:T(4,128)S(1)}, u32[]{:S(2)}, u32[]{:S(2)}) collective-permute-start(s32[1,4,8]{2,1,0:T(4,128)S(1)} %dynamic_update_slice.95), channel_id=1, source_target_pairs={{0,4},{4,0},{1,5},{5,1},{2,6},{6,2},{3,7},{7,3},{8,12},{12,8},{9,1... | collective-permute-start | bytes 392 | tf_op jit(solution)/shard_map/ppermute | solution.py:790
  516.1 6.6 collective-permute-start.43
  521.0 33.6 %collective-permute-start.38 = (bf16[1,2,2,4,8,2048]{5,4,0,1,2,3:T(8,128)(2,1)S(1)}, bf16[1,2,2,4,8,2048]{5,4,0,1,2,3:T(8,128)(2,1)S(1)}, u32[]{:S(2)}, u32[]{:S(2)}) collective-permute-start(bf16[1,2,2,4,8,2048]{5,4,0,1,2,3:T(8,128)(2,1)S(1)} %maximum_select_fusion.1), channel_id=1, source_target_pairs={{0,1},{1,0},{2,3},{3,2},{4,5},{5,4},{6,7},{7,6},{8,9},{9,8},{10,11... | collective-permute-start | bytes 1572872 | tf_op jit(solution)/shard_map/ppermute | solution.py:790
  607.8 8.3 collective-permute-start.48
  607.8 12.9 %collective-permute-start.49 = (bf16[1,32,2048]{2,1,0:T(8,128)(2,1)S(1)}, bf16[1,32,2048]{2,1,0:T(8,128)(2,1)S(1)}, u32[]{:S(2)}, u32[]{:S(2)}) collective-permute-start(bf16[1,32,2048]{2,1,0:T(8,128)(2,1)S(1)} %get-tuple-element.103), channel_id=1, source_target_pairs={{0,16},{8,24},{16,0},{24,8},{1,17},{9,25},{17,1},{25,9},{2,18},{10... | collective-permute-start | bytes 393224 | tf_op jit(solution)/shard_map/ppermute | solution.py:815
  610.5 10.3 collective-permute-start.50
  837.7 202.3 %reduce-scatter.5.cloned.1.call-start = ((), (), s32[]{:S(2)}) async-start(), calls=%async_computation.5 | async-start | bytes 6553600 | tf_op jit(solution)/shard_map/reduce_scatter | solution.py:1051
  945.5 7.3 collective-permute-start.45
  947.0 8.9 collective-permute-start.46
  949.4 6.6 collective-permute-start.47
  951.0 7.7 collective-permute-start.67
  951.7 8.7 collective-permute-start.68
  952.8 8.2 collective-permute-start.69
  1040.0 21.6 %all-to-all-start = ((bf16[8,320,256]{2,1,0:T(8,128)(2,1)}), bf16[8,320,256]{2,1,0:T(8,128)(2,1)}, u32[]{:S(2)}, u32[]{:S(2)}) async-start(bf16[8,320,256]{2,1,0:T(8,128)(2,1)} %bitcast.256), calls=%async_computation.2 | async-start | bytes 2621440 | tf_op jit(solution)/shard_map/all_to_all | solution.py:1052
  1062.7 10.8 collective-permute-start.66
  (147 other events, 2890.8 us)
Sparse Core Ops, SparseCore 0:
  21.7 252.0 all-gather.1
  837.9 89.0 reduce-scatter.2
  942.6 97.3 reduce-scatter.4
where the time goes:
time: 1100 us; the launch traced here: 1090 us
  waiting for transfers between devices  466 us (42%)
  Pallas kernels  296 us (27%)
  starting transfers between devices  152 us (14%)
  local copies, waits for them, and re-layouts  69.3 us (6%)
  matrix products  58.4 us (5%)
  other arithmetic  31.7 us (3%)
  between operations  17 us (2%)
    all_gather x1, waiting for transfers between devices, on_device(): lax.all_gather(flat_to_window(params, window_rows, shift, index, count),...  158 us
    ppermute x48, starting transfers between devices, swap(): return lax.ppermute(value, axis, [(i, i ^ bit) for i in range(size)])  109 us
    ppermute x48, waiting for transfers between devices, swap(): return lax.ppermute(value, axis, [(i, i ^ bit) for i in range(size)])  104 us
    reduce_scatter x1, waiting for transfers between devices, on_device(): trunk = lax.psum_scatter(trunk, PLANE, scatter_dimension=0, tiled=False)  79.7 us
    reduce_scatter x1, waiting for transfers between devices, on_device(): part = lax.psum_scatter(part, 'g', scatter_dimension=0, tiled=True)  78.4 us
    pallas_call x1, Pallas kernels, back_mid(): pl.pallas_call(back_mid_kernel, grid=(micros,), out_shape=[jax.ShapeDtype...  59.9 us
    pallas_call x1, Pallas kernels, back_out(): pl.pallas_call(back_out_kernel, grid=(micros, OUT // n), out_shape=[jax.S...  53.2 us
    pallas_call x1, Pallas kernels, conv_in(): pl.pallas_call(conv_in_kernel, grid=(micros, parts), out_shape=[jax.Shape...  33.7 us
  transfers between devices with their start and end apart: 74, of which 51 were waited for; matrix products, arithmetic and copies ran while one was open for 5% of the time, Pallas kernels for 7%

commit v1 on v0

--- a/solution.py
+++ b/solution.py
@@ -26,15 +26,22 @@
 ROW_CIN, ROW_CMID, ROW_COUT, ROW_SIDE = 0, 256, 1408, 1920
 ROW_PROJ, ROW_PIN, ROW_POUT, ROW_VEC = 2944, 9088, 9600, 10112
 LANES = 8
+GROUPS, GROUP = 4, 736
+GRAD_OUT, GRAD_MID = 1536, 1152
 ALL = ("g", "p", "x", "c")
 PLANE = ("p", "x", "c")
 F32, BF16 = jnp.float32, jnp.bfloat16
+COST_SHARE = 8
 
 
 def params_of(mib=60, steps=1):
     return pltpu.CompilerParams(
         vmem_limit_bytes=mib << 20, dimension_semantics=("arbitrary",) * steps
     )
+
+
+def cost(flops, moved):
+    return pl.CostEstimate(flops=flops // COST_SHARE, bytes_accessed=moved // COST_SHARE, transcendentals=0)
 
 
 def whole_block(shape):
@@ -68,6 +75,40 @@
         for col in range(4):
             lanes = pl.ds(part * 512 + col * 128, 128)
             scratch[col, pl.ds(part, rows, stride=4), :] = wide_ref[:, lanes].astype(F32)
+    for col in range(4):
+        out_ref[:, col * 128 : (col + 1) * 128] = scratch[col].astype(BF16)
+
+
+def trunk_pieces(start, stop):
+    found = []
+    for group in range(GROUPS):
+        low, high = max(start, group * GROUP), min(stop, (group + 1) * GROUP)
+        if low < high:
+            found.append((group, low - group * GROUP, low - start, high - low))
+    return found
+
+
+def trunk_specs(start, stop):
+    def spec(group):
+        return pl.BlockSpec(
+            (1, LANES, GROUP, 256), lambda *_: (group, 0, 0, 0), pipeline_mode=pl.Buffered(1)
+        )
+
+    return [spec(piece[0]) for piece in trunk_pieces(start, stop)]
+
+
+def join_trunk(refs, start, stop, out_ref):
+    for ref, (_, low, to, rows) in zip(refs, trunk_pieces(start, stop)):
+        for block in range(LANES):
+            out_ref[to : to + rows, block * 256 : block * 256 + 256] = ref[0, block, low : low + rows, :]
+
+
+def unwide_trunk(refs, start, stop, scratch, out_ref):
+    for ref, (_, low, to, rows) in zip(refs, trunk_pieces(start, stop)):
+        for part in range(4):
+            for col in range(4):
+                block, lanes = 2 * part + col // 2, slice((col % 2) * 128, (col % 2) * 128 + 128)
+                scratch[col, pl.ds(part + 4 * to, rows, stride=4), :] = ref[0, block, low : low + rows, lanes].astype(F32)
     for col in range(4):
         out_ref[:, col * 128 : (col + 1) * 128] = scratch[col].astype(BF16)
 
@@ -124,14 +165,16 @@
     co_ref[...] = po_ref[...].astype(BF16)
 
 
-def adam_from_window(window, shift, index, count, params, first, second):
+def tail_rows(shift, count):
+    return -(-shift * (count - 1) // 256) * 16
+
+
+def adam_from_window(window, prev, shift, index, params, first, second):
     own = params.shape[0] // 128
-    rows = window.shape[0]
-    tail = -(-shift * (count - 1) // 256) * 16
+    rows, tail = window.shape[0], prev.shape[0]
     block = 512
     steps = -(-own // block)
     assert steps * block <= rows * 16
-    prev = lax.ppermute(window[rows - tail :], ALL, [(i, i + 1) for i in range(count - 1)])
     off = (tail * 16 - index * shift).astype(jnp.int32)[None]
     spec = pl.BlockSpec((block, 128), lambda i: (i, 0))
     shaped = [v.reshape(own, 128) for v in (params, first, second)]
@@ -147,7 +190,7 @@
     return [v.reshape(-1) for v in outs]
 
 
-def conv_in_kernel(x_ref, xh_ref, w_ref, w2_ref, wide_ref, h_ref, hh_ref, xe_ref, st_ref, wf, wb, hs, xs):
+def conv_in_kernel(x_ref, w_ref, w2_ref, wide_ref, h_ref, xe_ref, st_ref, wb, wf, hs, xs):
     micro, part = pl.program_id(0), pl.program_id(1)
 
     @pl.when((micro == 0) & (part == 0))
@@ -156,10 +199,8 @@
 
     images = x_ref.shape[1] // 64
     h = dot(x_ref[0], wb[...])
-    hh = dot(xh_ref[0], wb[...])
     for col in range(4):
-        hs[col, 0 : images * 64, :] = h[:, col * 128 : (col + 1) * 128]
-        hs[col, images * 64 :, :] = hh[:, col * 128 : (col + 1) * 128]
+        hs[col] = h[:, col * 128 : (col + 1) * 128]
 
     def body(i, carry):
         at = pl.multiple_of(i * 64, 64)
@@ -175,8 +216,6 @@
                 half = hs[col, pl.ds(at + side, 32, stride=2), :].reshape(2, 2, 8, 128)
                 for row in range(2):
                     h_ref[0, 2 * row + side, pl.ds(low, 16), lanes] = half[:, row].reshape(16, 128)
-                hat = pl.multiple_of(i * 8, 8)
-                hh_ref[0, side, pl.ds(hat, 8), lanes] = hs[col, pl.ds(images * 64 + low + side, 8, stride=2), :]
         w = jnp.broadcast_to(w2_ref[0, pl.ds(low, 16), :], (16, 128))
         for col in range(8):
             lanes = slice(col * 128, (col + 1) * 128)
@@ -198,7 +237,7 @@
             st_ref[0, k : k + 1, lanes] += jnp.sum(found[col][k], axis=0, keepdims=True)
 
 
-def conv_in(x, xh, w, w2, wide):
+def conv_in(x, w, w2, wide):
     micros, pixels, _ = x.shape
     images = pixels // 64
     parts = 2
@@ -208,45 +247,72 @@
         grid=(micros, parts),
         out_shape=[
             jax.ShapeDtypeStruct((micros, 4, images * 16, MID), F32),
-            jax.ShapeDtypeStruct((micros, 2, images * 8, MID), F32),
             jax.ShapeDtypeStruct((micros, images * 16, D_IN), BF16),
             jax.ShapeDtypeStruct((micros, 8, MID), F32),
+            jax.ShapeDtypeStruct((D_IN, MID), BF16),
         ],
         in_specs=[
             pl.BlockSpec((1, b * 64, D_IN), lambda m, k: (m, k, 0)),
-            pl.BlockSpec((1, b * 16, D_IN), lambda m, k: (m, k, 0)),
             pl.BlockSpec((1, b * 64, 1), lambda m, k: (m, k, 0)),
             pl.BlockSpec((1, b * 16, 1), lambda m, k: (m, k, 0)),
             whole_block((256, 2048)),
         ],
         out_specs=[
             pl.BlockSpec((1, 4, b * 16, MID), lambda m, k: (m, 0, k, 0)),
-            pl.BlockSpec((1, 2, b * 8, MID), lambda m, k: (m, 0, k, 0)),
             pl.BlockSpec((1, b * 16, D_IN), lambda m, k: (m, k, 0)),
             pl.BlockSpec((1, 8, MID), lambda m, k: (m, 0, 0)),
+            whole_block((D_IN, MID)),
         ],
         scratch_shapes=[
             pltpu.VMEM((4, D_IN, 128), F32),
-            pltpu.VMEM((D_IN, MID), BF16),
-            pltpu.VMEM((4, b * 80, 128), F32),
+            pltpu.VMEM((4, b * 64, 128), F32),
             pltpu.VMEM((8, 32, 128), F32),
         ],
         compiler_params=params_of(56, 2),
-        cost_estimate=pl.CostEstimate(
-            flops=2 * micros * images * 80 * D_IN * MID, bytes_accessed=40 << 20, transcendentals=0
-        ),
-    )(x, xh, w, w2, wide)
-
-
-def side_kernel(xe_ref, w_ref, hs_ref, st_ref):
-    h = dot(xe_ref[0], w_ref[...])
+        cost_estimate=cost(2 * micros * images * 64 * D_IN * MID, 40 << 20),
+    )(x, w, w2, wide)
+
+
+def halo_kernel(xh_ref, wb_ref, hh_ref, hs):
+    h = dot(xh_ref[0], wb_ref[...])
+    rows = hh_ref.shape[2]
+    for col in range(4):
+        lanes = slice(col * 128, (col + 1) * 128)
+        hs[col] = h[:, lanes]
+        for side in range(2):
+            hh_ref[0, side, :, lanes] = hs[col, pl.ds(side, rows, stride=2), :]
+
+
+def conv_in_halo(xh, weight):
+    micros, pixels, _ = xh.shape
+    return pl.pallas_call(
+        halo_kernel,
+        grid=(micros,),
+        out_shape=jax.ShapeDtypeStruct((micros, 2, pixels // 2, MID), F32),
+        in_specs=[pl.BlockSpec((1, pixels, D_IN), lambda m: (m, 0, 0)), whole_block((D_IN, MID))],
+        out_specs=pl.BlockSpec((1, 2, pixels // 2, MID), lambda m: (m, 0, 0, 0)),
+        scratch_shapes=[pltpu.VMEM((4, pixels, 128), F32)],
+        compiler_params=params_of(40),
+        cost_estimate=cost(2 * micros * pixels * D_IN * MID, 9 << 20),
+    )(xh, weight)
+
+
+def side_kernel(xe_ref, *refs):
+    pieces, (hs_ref, st_ref, weight) = refs[:-3], refs[-3:]
+
+    @pl.when((pl.program_id(0) == 0) & (pl.program_id(1) == 0))
+    def _():
+        join_trunk(pieces, ROW_SIDE, ROW_PROJ, weight)
+
+    n = hs_ref.shape[2]
+    h = dot(xe_ref[0], weight[:, pl.ds(pl.multiple_of(pl.program_id(1) * n, n), n)])
     hs_ref[0] = h
     st_ref[...] = jnp.zeros_like(st_ref)
     st_ref[0, 0:1, :] = jnp.sum(h, axis=0, keepdims=True)
     st_ref[0, 1:2, :] = jnp.sum(h * h, axis=0, keepdims=True)
 
 
-def conv_side(xe, weight):
+def conv_side(xe, trunk):
     micros, rows, _ = xe.shape
     cols = 4
     n = OUT // cols
@@ -259,17 +325,16 @@
         ],
         in_specs=[
             pl.BlockSpec((1, rows, D_IN), lambda m, k: (m, 0, 0)),
-            pl.BlockSpec((D_IN, n), lambda m, k: (0, k)),
-        ],
+        ]
+        + trunk_specs(ROW_SIDE, ROW_PROJ),
         out_specs=[
             pl.BlockSpec((1, rows, n), lambda m, k: (m, 0, k)),
             pl.BlockSpec((1, 8, n), lambda m, k: (m, 0, k)),
         ],
+        scratch_shapes=[pltpu.VMEM((D_IN, OUT), BF16)],
         compiler_params=params_of(56, 2),
-        cost_estimate=pl.CostEstimate(
-            flops=2 * micros * rows * D_IN * OUT, bytes_accessed=16 << 20, transcendentals=0
-        ),
-    )(xe, weight)
+        cost_estimate=cost(2 * micros * rows * D_IN * OUT, 16 << 20),
+    )(xe, *[trunk] * len(trunk_pieces(ROW_SIDE, ROW_PROJ)))
 
 
 def shift_right(v):
@@ -282,12 +347,13 @@
     return jnp.where(lax.broadcasted_iota(jnp.int32, v.shape, 1) == 7, 0.0, moved)
 
 
-def conv_mid_kernel(h_ref, hh_ref, cf_ref, w_ref, wh_ref, wide_ref, cols_ref, hm_ref, st_ref, wb, wf):
+def conv_mid_kernel(h_ref, hh_ref, cf_ref, w_ref, wh_ref, *refs):
+    pieces, (cols_ref, hm_ref, st_ref, wb, wf) = refs[:-5], refs[-5:]
     micro = pl.program_id(0)
 
     @pl.when(micro == 0)
     def _():
-        unwide(wide_ref, wf, wb)
+        unwide_trunk(pieces, ROW_CMID, ROW_COUT, wf, wb)
 
     images = h_ref.shape[2] // 16
     scale, shift = cf_ref[0, 0:1, :], cf_ref[0, 1:2, :]
@@ -318,7 +384,7 @@
     st_ref[0, 1:2, :] = jnp.sum(hw * hw, axis=0, keepdims=True)
 
 
-def conv_mid(h, hh, coef, wph, whalo, wide):
+def conv_mid(h, hh, coef, wph, whalo, trunk):
     micros, _, rows, _ = h.shape
     return pl.pallas_call(
         conv_mid_kernel,
@@ -335,8 +401,8 @@
             pl.BlockSpec((1, 8, MID), lambda m: (m, 0, 0)),
             pl.BlockSpec((1, 4, rows, 1), lambda m: (m, 0, 0, 0)),
             pl.BlockSpec((1, 2, rows // 2, 1), lambda m: (m, 0, 0, 0)),
-            whole_block((1152, 2048)),
-        ],
+        ]
+        + trunk_specs(ROW_CMID, ROW_COUT),
         out_specs=[
             pl.BlockSpec((1, rows, 9 * MID), lambda m: (m, 0, 0)),
             pl.BlockSpec((1, rows, MID), lambda m: (m, 0, 0)),
@@ -345,13 +411,17 @@
         ],
         scratch_shapes=[pltpu.VMEM((4, 9 * MID, 128), F32)],
         compiler_params=params_of(60),
-        cost_estimate=pl.CostEstimate(
-            flops=2 * micros * rows * 9 * MID * MID, bytes_accessed=50 << 20, transcendentals=0
-        ),
-    )(h, hh, coef, wph, whalo, wide)
-
-
-def conv_out_kernel(hm_ref, cf_ref, w_ref, weight_ref, am_ref, ho_ref, st_ref):
+        cost_estimate=cost(2 * micros * rows * 9 * MID * MID, 50 << 20),
+    )(h, hh, coef, wph, whalo, *[trunk] * len(trunk_pieces(ROW_CMID, ROW_COUT)))
+
+
+def conv_out_kernel(hm_ref, cf_ref, w_ref, *refs):
+    pieces, (am_ref, ho_ref, st_ref, weight_ref) = refs[:-4], refs[-4:]
+
+    @pl.when(pl.program_id(0) == 0)
+    def _():
+        join_trunk(pieces, ROW_COUT, ROW_SIDE, weight_ref)
+
     v = hm_ref[0] * cf_ref[0, 0:1, :] + cf_ref[0, 1:2, :]
     am = (v * sigmoid(v) * w_ref[0, 0]).astype(BF16)
     am_ref[0] = am
@@ -364,7 +434,7 @@
         st_ref[0, 1:2, lanes] = jnp.sum(h * h, axis=0, keepdims=True)
 
 
-def conv_out(hm, coef, wph, weight):
+def conv_out(hm, coef, wph, trunk):
     micros, rows, _ = hm.shape
     return pl.pallas_call(
         conv_out_kernel,
@@ -373,23 +443,23 @@
             jax.ShapeDtypeStruct((micros, rows, MID), BF16),
             jax.ShapeDtypeStruct((micros, rows, OUT), F32),
             jax.ShapeDtypeStruct((micros, 8, OUT), F32),
+            jax.ShapeDtypeStruct((MID, OUT), BF16),
         ],
         in_specs=[
             pl.BlockSpec((1, rows, MID), lambda m: (m, 0, 0)),
             pl.BlockSpec((1, 8, MID), lambda m: (m, 0, 0)),
             pl.BlockSpec((1, 1, rows, 1), lambda m: (m, 0, 0, 0)),
-            whole_block((MID, OUT)),
-        ],
+        ]
+        + trunk_specs(ROW_COUT, ROW_SIDE),
         out_specs=[
             pl.BlockSpec((1, rows, MID), lambda m: (m, 0, 0)),
             pl.BlockSpec((1, rows, OUT), lambda m: (m, 0, 0)),
             pl.BlockSpec((1, 8, OUT), lambda m: (m, 0, 0)),
+            pl.BlockSpec((MID, OUT), lambda m: (0, 0), pipeline_mode=pl.Buffered(1)),
         ],
         compiler_params=params_of(56),
-        cost_estimate=pl.CostEstimate(
-            flops=2 * micros * rows * MID * OUT, bytes_accessed=18 << 20, transcendentals=0
-        ),
-    )(hm, coef, wph, weight)
+        cost_estimate=cost(2 * micros * rows * MID * OUT, 18 << 20),
+    )(hm, coef, wph, *[trunk] * len(trunk_pieces(ROW_COUT, ROW_SIDE)))
 
 
 def pool_kernel(ho_ref, hs_ref, cf_ref, w_ref, out_ref):
@@ -425,9 +495,7 @@
         ],
         out_specs=pl.BlockSpec((1, images, n), lambda m, k: (m, 0, k)),
         compiler_params=params_of(56, 2),
-        cost_estimate=pl.CostEstimate(
-            flops=20 * micros * rows * OUT, bytes_accessed=18 << 20, transcendentals=micros * rows * OUT
-        ),
+        cost_estimate=cost(20 * micros * rows * OUT, 18 << 20),
     )(ho, hs, coef, wph)
 
 
@@ -470,9 +538,7 @@
         ],
         out_specs=pl.BlockSpec((1, 3, images, n), lambda m, k: (m, 0, 0, k)),
         compiler_params=params_of(56, 2),
-        cost_estimate=pl.CostEstimate(
-            flops=30 * micros * rows * OUT, bytes_accessed=20 << 20, transcendentals=micros * rows * OUT
-        ),
+        cost_estimate=cost(30 * micros * rows * OUT, 20 << 20),
     )(ho, hs, coef, wph)
 
 
@@ -557,7 +623,7 @@
         out_shape=[
             jax.ShapeDtypeStruct((micros, rows, MID), F32),
             jax.ShapeDtypeStruct((micros, 8, MID), F32),
-            jax.ShapeDtypeStruct((LANES, MID + D_IN, 256), BF16),
+            jax.ShapeDtypeStruct((LANES, GRAD_OUT, 256), BF16),
         ],
         in_specs=[
             pl.BlockSpec((1, rows, n), lambda m, k: (m, 0, k)),
@@ -574,7 +640,7 @@
         out_specs=[
             pl.BlockSpec((1, rows, MID), lambda m, k: (m, 0, 0)),
             pl.BlockSpec((1, 8, MID), lambda m, k: (m, 0, 0)),
-            whole_block((LANES, MID + D_IN, 256)),
+            whole_block((LANES, GRAD_OUT, 256)),
         ],
         scratch_shapes=[
             pltpu.VMEM((MID, rows), BF16),
@@ -586,9 +652,7 @@
             pltpu.VMEM((OUT // n, D_IN, n), F32),
         ],
         compiler_params=params_of(60, 2),
-        cost_estimate=pl.CostEstimate(
-            flops=2 * micros * rows * OUT * (2 * MID + D_IN), bytes_accessed=40 << 20, transcendentals=micros * rows * OUT
-        ),
+        cost_estimate=cost(2 * micros * rows * OUT * (2 * MID + D_IN), 40 << 20),
     )(ho, hs, gs, coef, wph, am, xe, weight, hm, coef_mid)
 
 
@@ -666,7 +730,7 @@
     def _():
         for k in range(LANES):
             for half in range(2):
-                found = acc[(k % 2) * 2 + half, pl.ds(k // 2, 9 * MID // 4, stride=4), :]
+                found = acc[(k % 2) * 2 + half, pl.ds(k // 2, GRAD_MID, stride=4), :]
                 gw_ref[k, :, half * 128 : half * 128 + 128] = found.astype(BF16)
 
 
@@ -679,7 +743,7 @@
             jax.ShapeDtypeStruct((micros, 4, rows, MID), BF16),
             jax.ShapeDtypeStruct((micros, 2, rows // 2, MID), F32),
             jax.ShapeDtypeStruct((micros, 8, MID), F32),
-            jax.ShapeDtypeStruct((LANES, 1152, 256), BF16),
+            jax.ShapeDtypeStruct((LANES, GRAD_MID, 256), BF16),
         ],
         in_specs=[
             pl.BlockSpec((1, rows, MID), lambda m: (m, 0, 0)),
@@ -697,16 +761,14 @@
             pl.BlockSpec((1, 4, rows, MID), lambda m: (m, 0, 0, 0)),
             pl.BlockSpec((1, 2, rows // 2, MID), lambda m: (m, 0, 0, 0)),
             pl.BlockSpec((1, 8, MID), lambda m: (m, 0, 0)),
-            pl.BlockSpec((LANES, 1152, 256), lambda m: (0, 0, 0), pipeline_mode=pl.Buffered(1)),
+            pl.BlockSpec((LANES, GRAD_MID, 256), lambda m: (0, 0, 0), pipeline_mode=pl.Buffered(1)),
         ],
         scratch_shapes=[
             pltpu.VMEM((9, rows // 2, MID), F32),
             pltpu.VMEM((4, 9 * MID, 128), F32),
         ],
         compiler_params=params_of(62),
-        cost_estimate=pl.CostEstimate(
-            flops=4 * micros * rows * 9 * MID * MID, bytes_accessed=60 << 20, transcendentals=micros * rows * 5 * MID
-        ),
+        cost_estimate=cost(4 * micros * rows * 9 * MID * MID, 60 << 20),
     )(hm, d, coef_mid, cols, weight, h, hh, coef, wph, whalo)
 
 
@@ -779,9 +841,7 @@
             pltpu.VMEM((4, D_IN, 128), F32),
         ],
         compiler_params=params_of(60, 2),
-        cost_estimate=pl.CostEstimate(
-            flops=2 * micros * rows * 5 * D_IN * MID, bytes_accessed=50 << 20, transcendentals=0
-        ),
+        cost_estimate=cost(2 * micros * rows * 5 * D_IN * MID, 50 << 20),
     )(h, din, dhalo, coef, wph, whalo, x, xh)
 
 
@@ -833,6 +893,63 @@
     order = (3, 2, 1, 0, 4) + tuple(range(5, routed.ndim))
     routed = jnp.transpose(routed, order)
     return routed.reshape((-1,) + value.shape[2:])
+
+
+def halve(value, axis, dim):
+    own = lax.axis_index(axis)
+    keep = lax.dynamic_index_in_dim(value, own, dim, keepdims=False)
+    send = lax.dynamic_index_in_dim(value, 1 - own, dim, keepdims=False)
+    return keep + swap(send, axis, 1)
+
+
+def plane_reduce(value):
+    half = value.shape[1] // 2
+    value = halve(value.reshape((2, 2, 2) + value.shape[1:]), "c", 2)
+    a = halve(halve(value[:, :, :half], "x", 1), "p", 0)
+    b = halve(halve(value[:, :, half:], "p", 0), "x", 0)
+    return jnp.concatenate([a, b], axis=0)
+
+
+def to_first_plane(value):
+    planes = lax.axis_size("g")
+    step = 1
+    while step < planes:
+        value = value + lax.ppermute(value, "g", [(i + step, i) for i in range(0, planes - step, 2 * step)])
+        step *= 2
+    return value
+
+
+def spread_trunk(block, plane, plane_rows):
+    planes = lax.axis_size("g")
+    result = None
+    for target in range(planes):
+        parts = []
+        for source in range(planes):
+            low = max(target * GROUP, source * plane_rows)
+            high = min((target + 1) * GROUP, (source + 1) * plane_rows)
+            if low < high:
+                piece = block[low - source * plane_rows : high - source * plane_rows]
+                parts.append(piece if source == target else lax.ppermute(piece, "g", [(source, target)]))
+        whole = parts[0] if len(parts) == 1 else jnp.concatenate(parts, axis=0)
+        result = whole if result is None else jnp.where(plane == target, whole, result)
+    return result
+
+
+def first_rows_everywhere(block, plane, plane_rows):
+    last = lax.axis_size("g") - 1
+    at = ROW_VEC - last * plane_rows
+    send = jnp.concatenate([block[:ROW_CMID], block[at : at + 16]], axis=0)
+    first, vec = send[:ROW_CMID], send[ROW_CMID:]
+    for target in range(1, last + 1):
+        pairs = [(0, target), (last, last - target)]
+        got = lax.ppermute(send, "g", pairs)
+        first = jnp.where(plane == target, got[:ROW_CMID], first)
+        vec = jnp.where(plane == last - target, got[ROW_CMID:], vec)
+    rows = jnp.concatenate([first, vec], axis=0)
+    for axis in PLANE:
+        rows = gather_axis(rows, axis)
+    rows = jnp.transpose(rows, (3, 2, 1, 0, 4)).reshape(-1, 2048)
+    return rows[:ROW_CMID], rows[ROW_CMID:]
 
 
 def norm_ranges():
@@ -949,49 +1066,74 @@
     out_rows, out_cols = rows // 2, width // 2
     window_rows = -(-own // 256) * 16
     shift = window_rows * 16 - own
-    near = shift * count <= own and window_rows * count % (16 * lax.axis_size("g")) == 0 and lax.axis_size(PLANE) == LANES
-
-    around = [(i, i + 1) for i in range(lax.axis_size(("x", "c")) - 1)]
-    x_halo = lax.ppermute(inputs[:, :, -1], ("x", "c"), around).reshape(micros, images * width, D_IN)
+    plane_rows = window_rows * LANES
+    near = (
+        shift * count <= own
+        and lax.axis_size(PLANE) == LANES
+        and ROW_COUT < plane_rows < ROW_PROJ <= 2 * plane_rows
+        and window_rows - tail_rows(shift, count) < ROW_CMID <= window_rows
+        and ROW_VEC % window_rows + 16 <= window_rows
+        and ROW_VEC >= (lax.axis_size("g") - 1) * plane_rows
+    )
+
+    x = inputs.reshape(micros, images * rows * width, D_IN)
+    x_last, mask_last = inputs[:, :, -1], masks[:, :, -1]
     mask = masks.astype(F32)
-    mask_halo = lax.ppermute(masks[:, :, -1], ("x", "c"), around).astype(F32)
-    x = inputs.reshape(micros, images * rows * width, D_IN)
-
-    if near:
-        wall = lax.all_gather(flat_to_window(params, window_rows, shift, index, count), ALL, axis=0, tiled=True)
-    else:
-        wall = lax.all_gather(params.astype(BF16), ALL, axis=0, tiled=True).reshape(-1, 2048)
-
     w_in = mask.reshape(micros, -1, 1)
     split = mask.reshape(micros, images, out_rows, 2, out_cols, 2)
     wph = jnp.transpose(split, (0, 3, 5, 1, 2, 4)).reshape(micros, 4, -1, 1)
-    whalo = jnp.transpose(mask_halo.reshape(micros, images, out_cols, 2), (0, 3, 1, 2)).reshape(micros, 2, -1, 1)
+    around = [(i, i + 1) for i in range(lax.axis_size(("x", "c")) - 1)]
+    mask_halo = lax.ppermute(mask_last, ("x", "c"), around).astype(F32)
     total_in = jnp.sum(mask, axis=(1, 2, 3))
     image_pixels = jnp.sum(split[:, :, :, 0, :, 0], axis=(2, 3))
+    total_out = jnp.sum(image_pixels, axis=1)
     image_pixels = add_all(image_pixels, ("c", "x"))
-    totals = add_all(
-        jnp.stack([total_in, jnp.sum(image_pixels, axis=1) / lax.axis_size(("x", "c"))]), ("c", "x", "p", "g")
-    )
-    total_in, total_out = totals[0], totals[1]
-    partner_all, live_all = to_heads(partner), to_heads(live)
+    chosen = to_heads(jnp.stack([partner.astype(F32), live.astype(F32)], axis=-1))
+    if near:
+        window = flat_to_window(params, window_rows, shift, index, count)
+        column = lax.all_to_all(window, PLANE, 1, 0, tiled=True)
+        wide_in, vec = first_rows_everywhere(column, plane, plane_rows)
+        trunk = spread_trunk(column, plane, plane_rows)
+        trunk, x_last, wide_in, image_pixels, chosen, mask_halo = lax.optimization_barrier(
+            (trunk, x_last, wide_in, image_pixels, chosen, mask_halo)
+        )
+        h, xe, st, w_first = conv_in(x, w_in, wph[:, 0], wide_in)
+        trunk = lax.all_gather(trunk, ALL, axis=0, tiled=False).reshape(GROUPS, LANES, GROUP, 256)
+    else:
+        wall = lax.all_gather(params.astype(BF16), ALL, axis=0, tiled=True).reshape(-1, 2048)
+        wide_in, vec = wall[:ROW_CMID], wall[ROW_VEC : ROW_VEC + 16]
+        trunk = jnp.transpose(wall[:ROW_PROJ].reshape(GROUPS, GROUP, LANES, 256), (0, 2, 1, 3))
+        h, xe, st, w_first = conv_in(x, w_in, wph[:, 0], wide_in)
+
+    x_halo = lax.ppermute(x_last, ("x", "c"), around).reshape(micros, images * width, D_IN)
+    whalo = jnp.transpose(mask_halo.reshape(micros, images, out_cols, 2), (0, 3, 1, 2)).reshape(micros, 2, -1, 1)
     share_index = lax.axis_index(("x", "c"))
 
-    vec = wall[ROW_VEC : ROW_VEC + 16].astype(F32).reshape(-1)
+    pixels = jnp.broadcast_to(jnp.stack([total_in, total_out], axis=1)[..., None], (micros, 2, 128))
+    sums = add_all(jnp.concatenate([st[:, :2], pixels], axis=2))
+    total_in, total_out = sums[:, 0, MID], sums[:, 1, MID]
+    sums = sums[..., :MID]
+    hh = conv_in_halo(x_halo, w_first)
+    if near:
+        window, trunk, sums, hh, total_in, total_out = lax.optimization_barrier(
+            (window, trunk, sums, hh, total_in, total_out)
+        )
+        wall = lax.all_gather(window, ALL, axis=0, tiled=True)
+
+    vec = vec.astype(F32).reshape(-1)
     ranges = norm_ranges()
     gammas = [vec[start : start + n] for start, n in ranges]
     betas = [vec[NORM + start : NORM + start + n] for start, n in ranges]
     bias = vec[2 * NORM : 2 * NORM + OUT]
 
-    h, hh, xe, st = conv_in(x, x_halo, w_in, wph[:, 0], wall[ROW_CIN:ROW_CMID])
-    sums = add_all(st)
     mean_in, var_in, scale_in, a_in, b_in = norm_coefs(sums, total_in, gammas[0], betas[0])
     coef_in = pack([a_in, b_in])
-    hs, st_side = conv_side(xe, wall[ROW_SIDE:ROW_PROJ])
-    cols, hm, st, w_mid = conv_mid(h, hh, coef_in, wph, whalo, wall[ROW_CMID:ROW_COUT])
+    hs, st_side = conv_side(xe, trunk)
+    cols, hm, st, w_mid = conv_mid(h, hh, coef_in, wph, whalo, trunk)
     sums = add_all(jnp.concatenate([st[:, :2], st_side[:, :2]], axis=2))
     mean_mid, var_mid, scale_mid, a_mid, b_mid = norm_coefs(sums[..., :MID], total_out, gammas[1], betas[1])
     mean_side, var_side, scale_side, a_side, b_side = norm_coefs(sums[..., MID:], total_out, gammas[3], betas[3])
-    am, ho, st = conv_out(hm, pack([a_mid, b_mid]), wph, wall[ROW_COUT:ROW_SIDE])
+    am, ho, st, w_out = conv_out(hm, pack([a_mid, b_mid]), wph, trunk)
     sums = add_all(st[:, :2])
     mean_out, var_out, scale_out, a_out, b_out = norm_coefs(sums, total_out, gammas[2], betas[2])
     coef_join = pack([a_out, a_side, b_out + b_side])
@@ -1006,14 +1148,46 @@
     share_pixels = lax.dynamic_slice_in_dim(image_pixels, share_index * share, share, 1)
     pooled_low = to_heads((pooled / share_pixels[..., None]).astype(BF16))
     slope = slopes(ho, hs, coef_join, wph)
+    pooled_low, slope = lax.optimization_barrier((pooled_low, slope))
 
     grad_pool, head_rows, head_vec, block, loss_sum, live_count, head_means, head_vars = heads(
-        pooled_low, wall, gammas, betas, bias, partner_all, live_all
+        pooled_low, wall, gammas, betas, bias, chosen[:, 0].astype(jnp.int32), chosen[:, 1]
     )
+
+    def vector_rows(gamma, beta, extra):
+        flat, at = jnp.zeros((16 * 2048,), F32), 0
+        for value in gamma + beta + [extra]:
+            flat = flat + jnp.pad(value, (at, flat.shape[0] - at - value.shape[0]))
+            at += value.shape[0]
+        return flat.astype(BF16).reshape(16, 2048)
+
+    none_head = [jnp.zeros((n,), F32) for _, n in ranges[4:]]
+    none_trunk = [jnp.zeros((n,), F32) for _, n in ranges[:4]]
+    head_vector = vector_rows(none_trunk + head_vec[0], none_trunk + head_vec[1], head_vec[2])
+    head_vector = lax.dynamic_slice_in_dim(head_vector, block * 256, 256, 1)
+
+    scalars = jnp.pad(jnp.stack([loss_sum, live_count]), (0, 126))
+    head_stats = jnp.concatenate(head_means + head_vars + [scalars]).reshape(1, -1, 128)
+    head_stats = exchange_planes(jnp.broadcast_to(head_stats, (micros,) + head_stats.shape[1:])).reshape(micros, -1)
+    head_size = NORM - sum(n for _, n in ranges[:4])
+    scalars = head_stats[:, 2 * head_size : 2 * head_size + 2]
 
     grad_pool = grad_pool.astype(BF16).reshape(lax.axis_size("g"), lax.axis_size("p"), images, OUT)
     grad_pool = lax.dynamic_index_in_dim(grad_pool, lax.axis_index("p"), 1, keepdims=False)
-    gs = exchange_planes(grad_pool).astype(F32) / image_pixels[..., None]
+    gs = exchange_planes(grad_pool)
+    if near:
+        head_part = jnp.concatenate(
+            [
+                jnp.zeros((ROW_PROJ, 256), BF16),
+                head_rows,
+                head_vector,
+                jnp.zeros((window_rows * count - ROW_VEC - 16, 256), BF16),
+            ],
+            axis=0,
+        )
+        head_part, gs, head_stats = lax.optimization_barrier((head_part, gs, head_stats))
+        head_part = lax.psum_scatter(head_part, "g", scatter_dimension=0, tiled=True)
+    gs = gs.astype(F32) / image_pixels[..., None]
 
     sums = add_all(jnp.sum(gs[:, None] * slope, axis=2))
     bo, co, gamma_out = back_coefs(sums[:, 0], sums[:, 1], mean_out, scale_out, a_out, total_out)
@@ -1021,44 +1195,65 @@
     beta_joined = sums[:, 0]
     coef_back = pack([a_out, a_side, b_out + b_side, bo, co, bs, cs])
     d_mid, st, g_out = back_out(
-        ho, hs, gs, coef_back, wph, am, xe, wall[ROW_COUT:ROW_SIDE], hm, pack([a_mid, b_mid])
+        ho, hs, gs, coef_back, wph, am, xe, w_out, hm, pack([a_mid, b_mid])
     )
+    if near:
+        head_part, g_out = lax.optimization_barrier((head_part, g_out))
+        g_out = lax.psum_scatter(g_out, PLANE, scatter_dimension=0, tiled=False)
     sums = add_all(st[:, :2])
     bm, cm, gamma_mid = back_coefs(sums[:, 0], sums[:, 1], mean_mid, scale_mid, a_mid, total_out)
     beta_mid = sums[:, 0]
     d_in, d_halo, st, g_mid = back_mid(
         hm, d_mid, pack([a_mid, bm, cm]), cols, w_mid, h, hh, coef_in, wph, whalo
     )
+    if near:
+        g_mid, g_out = lax.optimization_barrier((g_mid, g_out))
+        g_mid = lax.psum_scatter(g_mid, PLANE, scatter_dimension=0, tiled=False)
+        out_first = to_first_plane(g_out[: plane_rows - ROW_COUT])
+        out_second = add_all(g_out[plane_rows - ROW_COUT :], ("g",))
     sums = add_all(st[:, :2])
     bi, ci, gamma_in = back_coefs(sums[:, 0], sums[:, 1], mean_in, scale_in, a_in, total_in)
     beta_in = sums[:, 0]
     g_in = back_in(h, d_in, d_halo, pack([a_in, bi, ci]), wph, whalo, x, x_halo)
 
-    first_plane = (plane == 0).astype(F32)
-    trunk_gamma = [jnp.sum(v, axis=0) * first_plane for v in (gamma_in, gamma_mid, gamma_out, gamma_side)]
-    trunk_beta = [jnp.sum(v, axis=0) * first_plane for v in (beta_in, beta_mid, beta_joined, beta_joined)]
-    vector = jnp.concatenate(trunk_gamma + head_vec[0] + trunk_beta + head_vec[1] + [head_vec[2]])
-    vector = jnp.pad(vector, (0, 16 * 2048 - vector.shape[0])).astype(BF16).reshape(16, 2048)
-    vector = lax.dynamic_slice_in_dim(vector, block * 256, 256, 1)
-    trunk = jnp.concatenate([g_in, g_mid, g_out], axis=1)
-
     if near:
-        head_part = jnp.concatenate(
-            [head_rows, vector, jnp.zeros((window_rows * count - ROW_VEC - 16, 256), BF16)], axis=0
+        g_in, g_mid, out_first, out_second = lax.optimization_barrier(
+            (plane_reduce(g_in), g_mid, out_first, out_second)
         )
-        trunk = lax.psum_scatter(trunk, PLANE, scatter_dimension=0, tiled=False)
-        part = jnp.concatenate([trunk, head_part], axis=0)
-        part = lax.psum_scatter(part, "g", scatter_dimension=0, tiled=True)
+    trunk_gamma = [jnp.sum(v, axis=0) for v in (gamma_in, gamma_mid, gamma_out, gamma_side)]
+    trunk_beta = [jnp.sum(v, axis=0) for v in (beta_in, beta_mid, beta_joined, beta_joined)]
+    trunk_vector = vector_rows(trunk_gamma + none_head, trunk_beta + none_head, jnp.zeros((OUT,), F32))
+
+    if near:
+        def blank(n):
+            return jnp.zeros((n, 256), BF16)
+
+        first_rows = jnp.concatenate([blank(ROW_CMID), to_first_plane(g_mid), out_first], axis=0)
+        second_rows = jnp.concatenate([out_second, blank(plane_rows - out_second.shape[0])], axis=0)
+        part = jnp.where(plane == 0, first_rows, jnp.where(plane == 1, head_part + second_rows, head_part))
         window = lax.all_to_all(part, PLANE, 0, 1, tiled=True)
+        tail = tail_rows(shift, count)
+        prev = lax.ppermute(window[window_rows - tail :], ALL, [(i, i + 1) for i in range(count - 1)])
+        g_in = to_first_plane(g_in)
+        for axis in PLANE:
+            g_in = gather_axis(g_in, axis)
+        g_in = jnp.transpose(g_in, (3, 2, 1, 0, 4)).reshape(ROW_CMID, 2048)
+        window = window.at[:ROW_CMID].add(jnp.where(index == 0, g_in, 0))
+        prev = prev.at[: ROW_CMID - window_rows + tail].add(jnp.where(index == 1, g_in[window_rows - tail :], 0))
+        at = ROW_VEC % window_rows
+        window = window.at[at : at + 16].add(jnp.where(index == ROW_VEC // window_rows, trunk_vector, 0))
         new_params, new_first, new_second, new_copy = adam_from_window(
-            window, shift, index, count, params, first, second
+            window, prev, shift, index, params, first, second
         )
     else:
         alone = (lax.axis_index("p") < 2).astype(BF16)
-        head_part = jnp.concatenate([head_rows, vector], axis=0) * alone
+        head_part = jnp.concatenate([head_rows, head_vector], axis=0) * alone
         head_part = lax.dynamic_update_slice(
             jnp.zeros((head_part.shape[0], 2048), BF16), head_part, (jnp.int32(0), (block * 256).astype(jnp.int32))
         )
+        lone = (index == 0).astype(BF16)
+        head_part = head_part.at[ROW_VEC - ROW_PROJ :].add(trunk_vector * lone)
+        trunk = jnp.concatenate([g_in, g_mid, g_out], axis=1)
         trunk = jnp.transpose(trunk, (1, 0, 2)).reshape(-1, 2048)
         flat = jnp.concatenate([trunk, head_part], axis=0).reshape(-1)
         flat = flat[: params.shape[0] * count]
@@ -1066,12 +1261,8 @@
         new_params, new_first, new_second = adam(grad, params, first, second)
         new_copy = new_params.astype(BF16)
 
-    head_stats = jnp.stack([jnp.concatenate(head_means), jnp.concatenate(head_vars)])
-    scalars = jnp.stack([loss_sum, live_count])
-    head_stats = exchange_planes(jnp.broadcast_to(head_stats[None], (micros,) + head_stats.shape))
-    scalars = exchange_planes(jnp.broadcast_to(scalars[None], (micros, 2)))
-    averages = jnp.concatenate([mean_in, mean_mid, mean_out, mean_side, head_stats[:, 0]], axis=1)
-    spreads = jnp.concatenate([var_in, var_mid, var_out, var_side, head_stats[:, 1]], axis=1)
+    averages = jnp.concatenate([mean_in, mean_mid, mean_out, mean_side, head_stats[:, :head_size]], axis=1)
+    spreads = jnp.concatenate([var_in, var_mid, var_out, var_side, head_stats[:, head_size : 2 * head_size]], axis=1)
     stats = jnp.stack([averages, spreads], axis=1)
     new_running = running
     for micro in range(micros):

time: 1100 us -> 946 us (0.86)
  waiting for transfers between devices: 466 us -> 324 us
  starting transfers between devices: 152 us -> 122 us
  other arithmetic: 31.7 us -> 47.3 us
    reduce_scatter x2 -> x3, waiting for transfers between devices: 158 us -> 3.93 us  [the longest x1 3.89 us: on_device(): lax.psum_scatter(head_part, 'g', scatter_dimension=0, tiled=True)]
    all_gather x1 -> x2, waiting for transfers between devices: 158 us -> 50.9 us  [the longest x1 36.5 us: on_device(): lax.all_gather(trunk, ALL, axis=0, tiled=False)]
    ppermute x48 -> x53, waiting for transfers between devices: 104 us -> 184 us  [swap(): return lax.ppermute(value, axis, [(i, i ^ bit) for i in range(size)])]
    ppermute x48 -> x53, starting transfers between devices: 109 us -> 51.7 us  [swap(): return lax.ppermute(value, axis, [(i, i ^ bit) for i in range(size)])]
    ppermute x3 -> x16, waiting for transfers between devices: 6.2 us -> 45.6 us  [the longest x6 36.2 us: to_first_plane(): lax.ppermute(value, 'g', [(i + step, i) for i in range(0, planes - step,...]
    ppermute x3 -> x16, starting transfers between devices: 9.2 us -> 37.5 us  [the longest x4 15.1 us: spread_trunk(): lax.ppermute(piece, 'g', [(source, target)])]
    all_to_all x0 -> x1, waiting for transfers between devices: none -> 13.9 us  [on_device(): column = lax.all_to_all(window, PLANE, 1, 0, tiled=True)]
    ppermute x18 -> x12, starting transfers between devices: 26 us -> 17.9 us  [exchange_planes(): lax.ppermute(block, 'g', [(i, (i + step) % planes) for i in range(planes)])]
  transfers between devices with their start and end apart: 74 -> 89, of which waited for: 51 -> 58; matrix products, arithmetic and copies ran while one was open for 5% -> 12% of each run, Pallas kernels for 7% -> 31%
where the time goes in v1:
time: 946 us; the launch traced here: 935 us
  waiting for transfers between devices  324 us (34%)
  Pallas kernels  296 us (31%)
  starting transfers between devices  122 us (13%)
  local copies, waits for them, and re-layouts  68.4 us (7%)
  matrix products  59.1 us (6%)
  other arithmetic  47.3 us (5%)
  between operations  17.7 us (2%)
    ppermute x53, waiting for transfers between devices, swap(): return lax.ppermute(value, axis, [(i, i ^ bit) for i in range(size)])  184 us
    pallas_call x1, Pallas kernels, back_mid(): pl.pallas_call(back_mid_kernel, grid=(micros,), out_shape=[jax.ShapeDtype...  59.6 us
    pallas_call x1, Pallas kernels, back_out(): pl.pallas_call(back_out_kernel, grid=(micros, OUT // n), out_shape=[jax.S...  53.3 us
    ppermute x53, starting transfers between devices, swap(): return lax.ppermute(value, axis, [(i, i ^ bit) for i in range(size)])  51.7 us
    all_gather x1, waiting for transfers between devices, on_device(): lax.all_gather(trunk, ALL, axis=0, tiled=False)  36.5 us
    ppermute x6, waiting for transfers between devices, to_first_plane(): lax.ppermute(value, 'g', [(i + step, i) for i in range(0, planes - step,...  36.2 us
    pallas_call x1, Pallas kernels, conv_mid(): pl.pallas_call(conv_mid_kernel, grid=(micros,), out_shape=[jax.ShapeDtype...  31.5 us
    pallas_call x1, Pallas kernels, back_in(): pl.pallas_call(back_in_kernel, grid=(micros, parts), out_shape=jax.ShapeD...  29.9 us
  transfers between devices with their start and end apart: 89, of which 58 were waited for; matrix products, arithmetic and copies ran while one was open for 12% of the time, Pallas kernels for 31%

profile of v1, /device:TPU:4, one launch (start us, length us, event | category | flops | bytes accessed | tf_op | source)
XLA Modules:
  0.0 935.0 jit_solution(3948456170855803867)
XLA Ops:
  24.0 6.5 all-to-all-start
  33.4 13.9 %all-to-all-done = bf16[320,8,256]{2,0,1:T(8,128)(2,1)S(1)} async-done(((bf16[320,8,256]{2,0,1:T(8,128)(2,1)}), bf16[320,8,256]{2,0,1:T(8,128)(2,1)S(1)}, u32[]{:S(2)}, u32[]{:S(2)}) %all-to-all-start) | async-done | bytes 1310752 | tf_op jit(solution)/shard_map/all_to_all | solution.py:1094
  83.1 6.8 collective-permute-start.1
  113.3 28.8 %shard_map.136 = (f32[4,4,512,512]{3,2,1,0:T(8,128)}, bf16[4,512,1024]{2,1,0:T(8,128)(2,1)}, f32[4,8,512]{2,1,0:T(8,128)}, bf16[1024,512]{1,0:T(8,128)(2,1)}) custom-call(bf16[4,2048,1024]{2,1,0:T(8,128)(2,1)} %bitcast.298, f32[4,2048,1]{2,1,0:T(8,128)} %reshape.1314.w_ref, f32[4,512,1]{2,1,0:T(8,128)} %squeeze.150.w2_ref, bf16[256,2048]{1,0:T(8,128)(2,1)} %slice.344.wide_ref), custom_call_target="tpu_custom_call" | custom-call | flops 1073741824 | bytes 5242880 | tf_op jit(solution)/shard_map/pallas_call | solution.py:245
  169.2 36.5 %all-gather.6.cloned.1.call-done = bf16[23552,256]{1,0:T(8,128)(2,1)} async-done(((bf16[736,256]{1,0:T(8,128)(2,1)}), bf16[23552,256]{1,0:T(8,128)(2,1)}) %all-gather.6.cloned.1.call-update) | async-done | bytes 12058640 | tf_op jit(solution)/shard_map/all_gather | solution.py:1101
  210.3 20.7 %shard_map.139 = (f32[4,512,2048]{2,1,0:T(8,128)}, f32[4,8,2048]{2,1,0:T(8,128)}) custom-call(bf16[4,512,1024]{2,1,0:T(8,128)(2,1)} %get-tuple-element.106.xe_ref, bf16[4,8,736,256]{3,2,1,0:T(8,128)(2,1)} %bitcast.292, bf16[4,8,736,256]{3,2,1,0:T(8,128)(2,1)} %bitcast.293), custom_call_target="tpu_custom_call" | custom-call | flops 1073741824 | bytes 2097152 | tf_op jit(solution)/shard_map/pallas_call | solution.py:319
  233.1 31.5 %shard_map.138 = (bf16[4,512,4608]{2,1,0:T(8,128)(2,1)}, f32[4,512,512]{2,1,0:T(8,128)}, f32[4,8,512]{2,1,0:T(8,128)}, bf16[4608,512]{1,0:T(8,128)(2,1)}) custom-call(f32[4,4,512,512]{3,2,1,0:T(8,128)} %get-tuple-element.94.h_ref, f32[4,2,256,512]{3,2,1,0:T(8,128)} %copy-done, f32[4,8,512]{2,1,0:T(8,128)} %pad_maximum_fusion.4.cf_ref, ...), custom_call_target="tpu_custom_call" | custom-call | flops 1207959552 | bytes 6553600 | tf_op jit(solution)/shard_map/pallas_call | solution.py:389
  267.0 6.8 collective-permute-done.27
  279.5 10.6 %collective-permute-done.29 = f32[4,2,2560]{2,0,1:T(4,128)S(1)} collective-permute-done((f32[4,2,2560]{2,0,1:T(4,128)S(1)}, f32[4,2,2560]{2,0,1:T(4,128)S(1)}, u32[]{:S(2)}, u32[]{:S(2)}) %collective-permute-start.29) | collective-permute-done | bytes 81952 | tf_op jit(solution)/shard_map/ppermute | solution.py:850
  290.2 10.0 %collective-permute-done.30 = f32[4,2,2560]{2,0,1:T(4,128)S(1)} collective-permute-done((f32[4,2,2560]{2,0,1:T(4,128)S(1)}, f32[4,2,2560]{2,0,1:T(4,128)S(1)}, u32[]{:S(2)}, u32[]{:S(2)}) %collective-permute-start.30) | collective-permute-done | bytes 81952 | tf_op jit(solution)/shard_map/ppermute | solution.py:850
  301.2 12.8 %shard_map.140 = (bf16[4,512,512]{2,1,0:T(8,128)(2,1)}, f32[4,512,2048]{2,1,0:T(8,128)}, f32[4,8,2048]{2,1,0:T(8,128)}, bf16[512,2048]{1,0:T(8,128)(2,1)}) custom-call(f32[4,512,512]{2,1,0:T(8,128)} %get-tuple-element.104.hm_ref, f32[4,8,512]{2,1,0:T(8,128)} %pad_maximum_fusion.3.cf_ref.cm_ref, f32[4,4,512,1]{3,2,1,0:T(8,128)} %copy.231.w_ref, ...), custom_call_target="tpu_custom_call" | custom-call | flops 536870912 | bytes 2359296 | tf_op jit(solution)/shard_map/pallas_call | solution.py:439
  332.2 7.0 collective-permute-done.35
  341.9 19.9 %shard_map.141 = f32[4,32,2048]{2,1,0:T(8,128)} custom-call(f32[4,512,2048]{2,1,0:T(8,128)} %get-tuple-element.109.ho_ref, f32[4,512,2048]{2,1,0:T(8,128)} %get-tuple-element.110.hs_ref, f32[4,8,2048]{2,1,0:T(8,128)} %stack.89.cf_ref, f32[4,4,512,1]{3,2,1,0:T(8,128)} %copy.231.w_ref), custom_call_target="tpu_custom_call" | custom-call | flops 10485760 | bytes 2359296 | tf_op jit(solution)/shard_map/pallas_call | solution.py:486
  362.9 6.9 collective-permute-start.36
  369.8 21.0 %collective-permute-done.36 = f32[4,16,2048]{2,1,0:T(8,128)S(1)} collective-permute-done((f32[4,16,2048]{2,1,0:T(8,128)S(1)}, f32[4,16,2048]{2,1,0:T(8,128)S(1)}, u32[]{:S(2)}, u32[]{:S(2)}) %collective-permute-start.36) | collective-permute-done | bytes 524320 | tf_op jit(solution)/shard_map/ppermute | solution.py:850
  411.5 6.1 collective-permute-done.42
  420.2 23.7 %shard_map.142 = f32[4,3,32,2048]{3,2,1,0:T(8,128)} custom-call(f32[4,512,2048]{2,1,0:T(8,128)} %get-tuple-element.109.ho_ref, f32[4,512,2048]{2,1,0:T(8,128)} %get-tuple-element.110.hs_ref, f32[4,8,2048]{2,1,0:T(8,128)} %stack.89.cf_ref, f32[4,4,512,1]{3,2,1,0:T(8,128)} %copy.231.w_ref), custom_call_target="tpu_custom_call" | custom-call | flops 15728640 | bytes 2621440 | tf_op jit(solution)/shard_map/pallas_call | solution.py:529
  444.0 14.3 %all-gather.4.cloned.1.call-done = bf16[10240,2048]{1,0:T(8,128)(2,1)} async-done(((bf16[320,2048]{1,0:T(8,128)(2,1)}), bf16[10240,2048]{1,0:T(8,128)(2,1)}) %all-gather.4.cloned.1.call-update) | async-done | bytes 41943056 | tf_op jit(solution)/shard_map/all_gather | solution.py:1121
  468.9 6.1 multiply_reduce_fusion.8
  475.7 6.1 multiply_reduce_fusion.7
  525.8 6.1 fusion.27
  579.5 9.5 %collective-permute-done.53 = f32[4,3,2048]{2,0,1:T(4,128)S(1)} collective-permute-done((f32[4,3,2048]{2,0,1:T(4,128)S(1)}, f32[4,3,2048]{2,0,1:T(4,128)S(1)}, u32[]{:S(2)}, u32[]{:S(2)}) %collective-permute-start.53) | collective-permute-done | bytes 98336 | tf_op jit(solution)/shard_map/ppermute | solution.py:850
  590.4 13.2 %collective-permute-done.54 = f32[4,3,2048]{2,0,1:T(4,128)S(1)} collective-permute-done((f32[4,3,2048]{2,0,1:T(4,128)S(1)}, f32[4,3,2048]{2,0,1:T(4,128)S(1)}, u32[]{:S(2)}, u32[]{:S(2)}) %collective-permute-start.54) | collective-permute-done | bytes 98336 | tf_op jit(solution)/shard_map/ppermute | solution.py:850
  605.0 53.3 %shard_map.143 = (f32[4,512,512]{2,1,0:T(8,128)}, f32[4,8,512]{2,1,0:T(8,128)}, bf16[8,1536,256]{2,1,0:T(8,128)(2,1)}) custom-call(f32[4,512,2048]{2,1,0:T(8,128)} %get-tuple-element.109.ho_ref, f32[4,512,2048]{2,1,0:T(8,128)} %get-tuple-element.110.hs_ref, f32[4,32,2048]{2,1,0:T(8,128)} %copy-done.6, f32[4,8,2048]{2,1,0:T(8,128)} %copy.252.cf_ref, ...), custom_call_target="tpu_custom_call" | custom-call | flops 2147483648 | bytes 5242880 | tf_op jit(solution)/shard_map/pallas_call | solution.py:620
  681.0 59.6 %shard_map.144 = (bf16[4,4,512,512]{3,2,1,0:T(8,128)(2,1)}, f32[4,2,256,512]{3,2,1,0:T(8,128)}, f32[4,8,512]{2,1,0:T(8,128)}, bf16[8,1152,256]{2,1,0:T(8,128)(2,1)}) custom-call(f32[4,512,512]{2,1,0:T(8,128)} %get-tuple-element.104.hm_ref, f32[4,512,512]{2,1,0:T(8,128)} %get-tuple-element.120.d_ref, f32[4,8,512]{2,1,0:T(8,128)} %stack.94.cm_ref, ...), custom_call_target="tpu_custom_call" | custom-call | flops 2415919104 | bytes 7864320 | tf_op jit(solution)/shard_map/pallas_call | solution.py:739
  760.2 29.9 %shard_map.145 = bf16[8,256,256]{2,1,0:T(8,128)(2,1)} custom-call(f32[4,4,512,512]{3,2,1,0:T(8,128)} %get-tuple-element.94.h_ref, bf16[4,4,512,512]{3,2,1,0:T(8,128)(2,1)} %get-tuple-element.124.din_ref, f32[4,2,256,512]{3,2,1,0:T(8,128)} %get-tuple-element.125.dh_ref, f32[4,8,512]{2,1,0:T(8,128)} %stack.95.cf_ref, f32[4,4,512,1]{3,2,1,0:T(8,128)} %copy.231.w_ref, ...), custom_call_target="tpu_custom_call" | custom-call | flops 1342177280 | bytes 6553600 | tf_op jit(solution)/shard_map/pallas_call | solution.py:823
  805.2 11.0 %collective-permute-done.70 = bf16[1152,256]{1,0:T(8,128)(2,1)S(1)} collective-permute-done((bf16[1152,256]{1,0:T(8,128)(2,1)S(1)}, bf16[1152,256]{1,0:T(8,128)(2,1)S(1)}, u32[]{:S(2)}, u32[]{:S(2)}) %collective-permute-start.70) | collective-permute-done | bytes 589856 | tf_op jit(solution)/shard_map/ppermute | solution.py:917
  822.7 17.9 %collective-permute-done.73 = bf16[384,256]{1,0:T(8,128)(2,1)S(1)} collective-permute-done((bf16[384,256]{1,0:T(8,128)(2,1)S(1)}, bf16[384,256]{1,0:T(8,128)(2,1)S(1)}, u32[]{:S(2)}, u32[]{:S(2)}) %collective-permute-start.73) | collective-permute-done | bytes 196640 | tf_op jit(solution)/shard_map/ppermute | solution.py:850
  868.8 12.0 %collective-permute-done.75 = bf16[1152,256]{1,0:T(8,128)(2,1)S(1)} collective-permute-done((bf16[1152,256]{1,0:T(8,128)(2,1)S(1)}, bf16[1152,256]{1,0:T(8,128)(2,1)S(1)}, u32[]{:S(2)}, u32[]{:S(2)}) %collective-permute-start.75) | collective-permute-done | bytes 589856 | tf_op jit(solution)/shard_map/ppermute | solution.py:917
  897.1 10.7 %all-to-all-done.1 = bf16[8,320,256]{2,1,0:T(8,128)(2,1)S(1)} async-done(((bf16[8,320,256]{2,1,0:T(8,128)(2,1)}), bf16[8,320,256]{2,1,0:T(8,128)(2,1)S(1)}, u32[]{:S(2)}, u32[]{:S(2)}) %all-to-all-start.1) | async-done | bytes 1310752 | tf_op jit(solution)/shard_map/all_to_all | solution.py:1234
  910.9 8.3 collective-permute-done.76
  919.3 8.7 shard_map.146
  (693 shorter events, 381.0 us)
Async XLA Ops:
  24.0 23.3 %all-to-all-start = ((bf16[320,8,256]{2,0,1:T(8,128)(2,1)}), bf16[320,8,256]{2,0,1:T(8,128)(2,1)S(1)}, u32[]{:S(2)}, u32[]{:S(2)}) async-start(bf16[320,8,256]{2,0,1:T(8,128)(2,1)} %bitcast.286), calls=%async_computation | async-start | bytes 2621440 | tf_op jit(solution)/shard_map/all_to_all | solution.py:1094
  30.5 175.1 %all-gather.6.cloned.1.call-start = ((), (), s32[]{:S(2)}) async-start(), calls=%async_computation.9 | async-start | bytes 12435456 | tf_op jit(solution)/shard_map/all_gather | solution.py:1101
  30.6 24.1 %collective-permute-start.13 = (f32[1,8,2]{1,0,2:T(1,128)S(1)}, f32[1,8,2]{1,0,2:T(1,128)S(1)}, u32[]{:S(2)}, u32[]{:S(2)}) collective-permute-start(f32[1,8,2]{1,0,2:T(1,128)S(1)} %get-tuple-element.262), channel_id=1, source_target_pairs={{0,8},{8,16},{16,24},{24,0},{1,9},{9,17},{17,25},{25,1},{2,10},{10... | collective-permute-start | bytes 200 | tf_op jit(solution)/shard_map/ppermute | solution.py:875
  32.2 24.2 %collective-permute-start.14 = (f32[1,8,2]{1,0,2:T(1,128)S(1)}, f32[1,8,2]{1,0,2:T(1,128)S(1)}, u32[]{:S(2)}, u32[]{:S(2)}) collective-permute-start(f32[1,8,2]{1,0,2:T(1,128)S(1)} %get-tuple-element.263), channel_id=1, source_target_pairs={{0,16},{8,24},{16,0},{24,8},{1,17},{9,25},{17,1},{25,9},{2,18},{10... | collective-permute-start | bytes 200 | tf_op jit(solution)/shard_map/ppermute | solution.py:875
  47.3 16.6 %collective-permute-start.5 = (bf16[272,256]{1,0:T(8,128)(2,1)S(1)}, bf16[272,256]{1,0:T(8,128)(2,1)S(1)}, u32[]{:S(2)}, u32[]{:S(2)}) collective-permute-start(bf16[272,256]{1,0:T(8,128)(2,1)S(1)} %pad_maximum_fusion), channel_id=1, source_target_pairs={{0,24},{24,0},{1,25},{25,1},{2,26},{26,2},{3,27},{27,3},{4,28},{28... | collective-permute-start | bytes 417800 | tf_op jit(solution)/shard_map/ppermute | solution.py:945
  62.1 27.9 %collective-permute-start.19 = (s32[4,32,16]{1,2,0:T(8,128)S(1)}, s32[4,32,16]{1,2,0:T(8,128)}, u32[]{:S(2)}, u32[]{:S(2)}) collective-permute-start(s32[4,32,16]{1,2,0:T(8,128)S(1)} %slice_bitcast_fusion.3), channel_id=1, source_target_pairs={{0,1},{1,2},{2,3},{4,5},{5,6},{6,7},{8,9},{9,10},{10,11},{12,13},{... | collective-permute-start | bytes 24584 | tf_op jit(solution)/shard_map/ppermute | solution.py:1086
  73.2 25.6 %collective-permute-start.3 = (bf16[736,256]{1,0:T(8,128)(2,1)}, bf16[736,256]{1,0:T(8,128)(2,1)}, u32[]{:S(2)}, u32[]{:S(2)}) collective-permute-start(bf16[736,256]{1,0:T(8,128)(2,1)} %get-tuple-element.187), channel_id=1, source_target_pairs={{0,16},{1,17},{2,18},{3,19},{4,20},{5,21},{6,22},{7,23}} | collective-permute-start | bytes 1130504 | tf_op jit(solution)/shard_map/ppermute | solution.py:932
  80.3 18.5 %collective-permute-start.4 = (bf16[736,256]{1,0:T(8,128)(2,1)S(1)}, bf16[736,256]{1,0:T(8,128)(2,1)}, u32[]{:S(2)}, u32[]{:S(2)}) collective-permute-start(bf16[736,256]{1,0:T(8,128)(2,1)S(1)} %get-tuple-element.186), channel_id=1, source_target_pairs={{0,8},{1,9},{2,10},{3,11},{4,12},{5,13},{6,14},{7,15}} | collective-permute-start | bytes 1130504 | tf_op jit(solution)/shard_map/ppermute | solution.py:932
  82.4 16.3 %collective-permute-start.2 = (bf16[384,256]{1,0:T(8,128)(2,1)S(1)}, bf16[384,256]{1,0:T(8,128)(2,1)S(1)}, u32[]{:S(2)}, u32[]{:S(2)}) collective-permute-start(bf16[384,256]{1,0:T(8,128)(2,1)S(1)} %slice.417), channel_id=1, source_target_pairs={{8,24},{9,25},{10,26},{11,27},{12,28},{13,29},{14,30},{15,31}} | collective-permute-start | bytes 589832 | tf_op jit(solution)/shard_map/ppermute | solution.py:932
  83.1 15.6 %collective-permute-start.1 = (bf16[352,256]{1,0:T(8,128)(2,1)}, bf16[352,256]{1,0:T(8,128)(2,1)}, u32[]{:S(2)}, u32[]{:S(2)}) collective-permute-start(bf16[352,256]{1,0:T(8,128)(2,1)} %slice.416), channel_id=1, source_target_pairs={{0,24},{1,25},{2,26},{3,27},{4,28},{5,29},{6,30},{7,31}} | collective-permute-start | bytes 540680 | tf_op jit(solution)/shard_map/ppermute | solution.py:932
  103.7 354.7 %all-gather.4.cloned.1.call-start = ((), (), s32[]{:S(2)}) async-start(), calls=%async_computation.5 | async-start | bytes 43253760 | tf_op jit(solution)/shard_map/all_gather | solution.py:1121
  103.7 57.1 %collective-permute-start.25 = (bf16[4,32,16,1024]{3,2,1,0:T(8,128)(2,1)}, bf16[4,32,16,1024]{3,2,1,0:T(8,128)(2,1)}, u32[]{:S(2)}, u32[]{:S(2)}) collective-permute-start(bf16[4,32,16,1024]{3,2,1,0:T(8,128)(2,1)} %slice_bitcast_fusion), channel_id=1, source_target_pairs={{0,1},{1,2},{2,3},{4,5},{5,6},{6,7},{8,9},{9,10},{10,11},{12,13},{... | collective-permute-start | bytes 12582920 | tf_op jit(solution)/shard_map/ppermute | solution.py:1108
  205.7 456.4 %reduce-scatter.4.cloned.1.call-start = ((), (), s32[]{:S(2)}) async-start(), calls=%async_computation.6 | async-start | bytes 6553600 | tf_op jit(solution)/shard_map/reduce_scatter | solution.py:1189
  362.9 27.9 %collective-permute-start.36 = (f32[4,16,2048]{2,1,0:T(8,128)S(1)}, f32[4,16,2048]{2,1,0:T(8,128)S(1)}, u32[]{:S(2)}, u32[]{:S(2)}) collective-permute-start(f32[4,16,2048]{2,1,0:T(8,128)S(1)} %constant_dynamic-slice_fusion.11), channel_id=1, source_target_pairs={{0,2},{2,0},{1,3},{3,1},{4,6},{6,4},{5,7},{7,5},{8,10},{10,8},{9,1... | collective-permute-start | bytes 1572872 | tf_op jit(solution)/shard_map/ppermute | solution.py:850
  417.6 26.3 %collective-permute-start.43 = (bf16[1,2,2,4,8,2048]{5,4,0,1,2,3:T(8,128)(2,1)S(1)}, bf16[1,2,2,4,8,2048]{5,4,0,1,2,3:T(8,128)(2,1)S(1)}, u32[]{:S(2)}, u32[]{:S(2)}) collective-permute-start(bf16[1,2,2,4,8,2048]{5,4,0,1,2,3:T(8,128)(2,1)S(1)} %maximum_select_fusion.4), channel_id=1, source_target_pairs={{0,1},{1,0},{2,3},{3,2},{4,5},{5,4},{6,7},{7,6},{8,9},{9,8},{10,11... | collective-permute-start | bytes 1572872 | tf_op jit(solution)/shard_map/ppermute | solution.py:850
  498.2 58.7 %collective-permute-start.44 = (f32[1,105,128]{2,1,0:T(8,128)}, f32[1,105,128]{2,1,0:T(8,128)}, u32[]{:S(2)}, u32[]{:S(2)}) collective-permute-start(f32[1,105,128]{2,1,0:T(8,128)} %bitcast.51), channel_id=1, source_target_pairs={{0,8},{8,16},{16,24},{24,0},{1,9},{9,17},{17,25},{25,1},{2,10},{10... | collective-permute-start | bytes 161288 | tf_op jit(solution)/shard_map/ppermute | solution.py:875
  498.2 62.4 %collective-permute-start.45 = (f32[1,105,128]{2,1,0:T(8,128)}, f32[1,105,128]{2,1,0:T(8,128)}, u32[]{:S(2)}, u32[]{:S(2)}) collective-permute-start(f32[1,105,128]{2,1,0:T(8,128)} %bitcast.51), channel_id=1, source_target_pairs={{0,16},{8,24},{16,0},{24,8},{1,17},{9,25},{17,1},{25,9},{2,18},{10... | collective-permute-start | bytes 161288 | tf_op jit(solution)/shard_map/ppermute | solution.py:875
  500.3 61.1 %collective-permute-start.46 = (f32[1,105,128]{2,1,0:T(8,128)}, f32[1,105,128]{2,1,0:T(8,128)}, u32[]{:S(2)}, u32[]{:S(2)}) collective-permute-start(f32[1,105,128]{2,1,0:T(8,128)} %bitcast.51), channel_id=1, source_target_pairs={{0,24},{8,0},{16,8},{24,16},{1,25},{9,1},{17,9},{25,17},{2,26},{10... | collective-permute-start | bytes 161288 | tf_op jit(solution)/shard_map/ppermute | solution.py:875
  533.7 28.6 %collective-permute-start.47 = (bf16[1,32,2048]{2,1,0:T(8,128)(2,1)}, bf16[1,32,2048]{2,1,0:T(8,128)(2,1)}, u32[]{:S(2)}, u32[]{:S(2)}) collective-permute-start(bf16[1,32,2048]{2,1,0:T(8,128)(2,1)} %get-tuple-element.190), channel_id=1, source_target_pairs={{0,8},{8,16},{16,24},{24,0},{1,9},{9,17},{17,25},{25,1},{2,10},{10... | collective-permute-start | bytes 393224 | tf_op jit(solution)/shard_map/ppermute | solution.py:875
  534.3 28.9 %collective-permute-start.48 = (bf16[1,32,2048]{2,1,0:T(8,128)(2,1)}, bf16[1,32,2048]{2,1,0:T(8,128)(2,1)}, u32[]{:S(2)}, u32[]{:S(2)}) collective-permute-start(bf16[1,32,2048]{2,1,0:T(8,128)(2,1)} %get-tuple-element.189), channel_id=1, source_target_pairs={{0,16},{8,24},{16,0},{24,8},{1,17},{9,25},{17,1},{25,9},{2,18},{10... | collective-permute-start | bytes 393224 | tf_op jit(solution)/shard_map/ppermute | solution.py:875
  565.0 175.6 %reduce-scatter.6.cloned.1.call-start = ((), (), s32[]{:S(2)}) async-start(), calls=%async_computation.7 | async-start | bytes 7077888 | tf_op jit(solution)/shard_map/reduce_scatter | solution.py:1202
  662.2 178.6 %reduce-scatter.8.cloned.1.call-start = ((), (), s32[]{:S(2)}) async-start(), calls=%async_computation.8 | async-start | bytes 5308416 | tf_op jit(solution)/shard_map/reduce_scatter | solution.py:1211
  798.0 18.1 %collective-permute-start.70 = (bf16[1152,256]{1,0:T(8,128)(2,1)S(1)}, bf16[1152,256]{1,0:T(8,128)(2,1)S(1)}, u32[]{:S(2)}, u32[]{:S(2)}) collective-permute-start(bf16[1152,256]{1,0:T(8,128)(2,1)S(1)} %slice.400), channel_id=1, source_target_pairs={{8,0},{24,16},{9,1},{25,17},{10,2},{26,18},{11,3},{27,19},{12,4},{... | collective-permute-start | bytes 1769480 | tf_op jit(solution)/shard_map/ppermute | solution.py:917
  800.6 16.9 %collective-permute-start.67 = (bf16[128,256]{1,0:T(8,128)(2,1)S(1)}, bf16[128,256]{1,0:T(8,128)(2,1)S(1)}, u32[]{:S(2)}, u32[]{:S(2)}) collective-permute-start(bf16[128,256]{1,0:T(8,128)(2,1)S(1)} %dynamic-slice_bitcast_fusion.7), channel_id=1, source_target_pairs={{0,4},{4,0},{1,5},{5,1},{2,6},{6,2},{3,7},{7,3},{8,12},{12,8},{9,1... | collective-permute-start | bytes 196616 | tf_op jit(solution)/shard_map/ppermute | solution.py:850
  803.0 19.6 %collective-permute-start.69 = (bf16[128,256]{1,0:T(8,128)(2,1)S(1)}, bf16[128,256]{1,0:T(8,128)(2,1)S(1)}, u32[]{:S(2)}, u32[]{:S(2)}) collective-permute-start(bf16[128,256]{1,0:T(8,128)(2,1)S(1)} %dynamic-slice_bitcast_fusion.6), channel_id=1, source_target_pairs={{0,2},{2,0},{1,3},{3,1},{4,6},{6,4},{5,7},{7,5},{8,10},{10,8},{9,1... | collective-permute-start | bytes 196616 | tf_op jit(solution)/shard_map/ppermute | solution.py:850
  803.7 15.5 %collective-permute-start.72 = (bf16[384,256]{1,0:T(8,128)(2,1)S(1)}, bf16[384,256]{1,0:T(8,128)(2,1)S(1)}, u32[]{:S(2)}, u32[]{:S(2)}) collective-permute-start(bf16[384,256]{1,0:T(8,128)(2,1)S(1)} %slice.401), channel_id=1, source_target_pairs={{0,8},{8,0},{16,24},{24,16},{1,9},{9,1},{17,25},{25,17},{2,10},{10... | collective-permute-start | bytes 589832 | tf_op jit(solution)/shard_map/ppermute | solution.py:850
  816.2 24.5 %collective-permute-start.71 = (bf16[1152,256]{1,0:T(8,128)(2,1)S(1)}, bf16[1152,256]{1,0:T(8,128)(2,1)S(1)}, u32[]{:S(2)}, u32[]{:S(2)}) collective-permute-start(bf16[1152,256]{1,0:T(8,128)(2,1)S(1)} %slice_add_fusion.6), channel_id=1, source_target_pairs={{16,0},{17,1},{18,2},{19,3},{20,4},{21,5},{22,6},{23,7}} | collective-permute-start | bytes 1769480 | tf_op jit(solution)/shard_map/ppermute | solution.py:917
  819.3 21.3 %collective-permute-start.73 = (bf16[384,256]{1,0:T(8,128)(2,1)S(1)}, bf16[384,256]{1,0:T(8,128)(2,1)S(1)}, u32[]{:S(2)}, u32[]{:S(2)}) collective-permute-start(bf16[384,256]{1,0:T(8,128)(2,1)S(1)} %slice_add_fusion.5), channel_id=1, source_target_pairs={{0,16},{8,24},{16,0},{24,8},{1,17},{9,25},{17,1},{25,9},{2,18},{10... | collective-permute-start | bytes 589832 | tf_op jit(solution)/shard_map/ppermute | solution.py:850
  849.9 15.5 %collective-permute-start.74 = (bf16[1152,256]{1,0:T(8,128)(2,1)}, bf16[1152,256]{1,0:T(8,128)(2,1)S(1)}, u32[]{:S(2)}, u32[]{:S(2)}) collective-permute-start(bf16[1152,256]{1,0:T(8,128)(2,1)} %bitcast.329), channel_id=1, source_target_pairs={{8,0},{24,16},{9,1},{25,17},{10,2},{26,18},{11,3},{27,19},{12,4},{... | collective-permute-start | bytes 1769480 | tf_op jit(solution)/shard_map/ppermute | solution.py:917
  865.6 15.2 %collective-permute-start.75 = (bf16[1152,256]{1,0:T(8,128)(2,1)S(1)}, bf16[1152,256]{1,0:T(8,128)(2,1)S(1)}, u32[]{:S(2)}, u32[]{:S(2)}) collective-permute-start(bf16[1152,256]{1,0:T(8,128)(2,1)S(1)} %add.855), channel_id=1, source_target_pairs={{16,0},{17,1},{18,2},{19,3},{20,4},{21,5},{22,6},{23,7}} | collective-permute-start | bytes 1769480 | tf_op jit(solution)/shard_map/ppermute | solution.py:917
  868.7 23.3 %collective-permute-start.81 = (bf16[1,2,2,256,256]{4,3,2,1,0:T(8,128)(2,1)S(1)}, bf16[1,2,2,256,256]{4,3,2,1,0:T(8,128)(2,1)S(1)}, u32[]{:S(2)}, u32[]{:S(2)}) collective-permute-start(bf16[1,2,2,256,256]{4,3,2,1,0:T(8,128)(2,1)S(1)} %maximum_select_fusion.5), channel_id=1, source_target_pairs={{0,1},{1,0},{2,3},{3,2},{4,5},{5,4},{6,7},{7,6},{8,9},{9,8},{10,11... | collective-permute-start | bytes 1572872 | tf_op jit(solution)/shard_map/ppermute | solution.py:850
  885.9 21.9 %all-to-all-start.1 = ((bf16[8,320,256]{2,1,0:T(8,128)(2,1)}), bf16[8,320,256]{2,1,0:T(8,128)(2,1)S(1)}, u32[]{:S(2)}, u32[]{:S(2)}) async-start(bf16[8,320,256]{2,1,0:T(8,128)(2,1)} %bitcast.73), calls=%async_computation.4 | async-start | bytes 2621440 | tf_op jit(solution)/shard_map/all_to_all | solution.py:1234
  (186 other events, 2536.0 us)
Sparse Core Ops, SparseCore 0:
  103.8 101.8 all-gather.5
  209.1 249.2 all-gather.3
  565.2 96.9 reduce-scatter.3
  665.4 62.1 reduce-scatter.5
  740.9 54.4 reduce-scatter.7

commit v2 on v1

--- a/solution.py
+++ b/solution.py
@@ -190,7 +190,7 @@
     return [v.reshape(-1) for v in outs]
 
 
-def conv_in_kernel(x_ref, w_ref, w2_ref, wide_ref, h_ref, xe_ref, st_ref, wb, wf, hs, xs):
+def conv_in_kernel(x_ref, w_ref, wide_ref, h_ref, xe_ref, st_ref, wb, wf, hs, xs):
     micro, part = pl.program_id(0), pl.program_id(1)
 
     @pl.when((micro == 0) & (part == 0))
@@ -205,18 +205,19 @@
     def body(i, carry):
         at = pl.multiple_of(i * 64, 64)
         low = pl.multiple_of(i * 16, 16)
-        w = jnp.broadcast_to(w_ref[0, pl.ds(at, 64), :], (64, 128))
+        w = [jnp.broadcast_to(w_ref[0, k, pl.ds(low, 16), :], (16, 128)) for k in range(4)]
         new = []
         for col in range(4):
             lanes = slice(col * 128, (col + 1) * 128)
-            h = hs[col, pl.ds(at, 64), :] * w
-            new.append((carry[col][0] + fold(h), carry[col][1] + fold(h * h)))
-            hs[col, pl.ds(at, 64), :] = h
+            total, square = carry[col]
             for side in range(2):
                 half = hs[col, pl.ds(at + side, 32, stride=2), :].reshape(2, 2, 8, 128)
                 for row in range(2):
-                    h_ref[0, 2 * row + side, pl.ds(low, 16), lanes] = half[:, row].reshape(16, 128)
-        w = jnp.broadcast_to(w2_ref[0, pl.ds(low, 16), :], (16, 128))
+                    h = half[:, row].reshape(16, 128) * w[2 * row + side]
+                    total, square = total + fold(h), square + fold(h * h)
+                    h_ref[0, 2 * row + side, pl.ds(low, 16), lanes] = h
+            new.append((total, square))
+        w = w[0]
         for col in range(8):
             lanes = slice(col * 128, (col + 1) * 128)
             for row in range(2):
@@ -237,7 +238,7 @@
             st_ref[0, k : k + 1, lanes] += jnp.sum(found[col][k], axis=0, keepdims=True)
 
 
-def conv_in(x, w, w2, wide):
+def conv_in(x, wph, wide):
     micros, pixels, _ = x.shape
     images = pixels // 64
     parts = 2
@@ -253,8 +254,7 @@
         ],
         in_specs=[
             pl.BlockSpec((1, b * 64, D_IN), lambda m, k: (m, k, 0)),
-            pl.BlockSpec((1, b * 64, 1), lambda m, k: (m, k, 0)),
-            pl.BlockSpec((1, b * 16, 1), lambda m, k: (m, k, 0)),
+            pl.BlockSpec((1, 4, b * 16, 1), lambda m, k: (m, 0, k, 0)),
             whole_block((256, 2048)),
         ],
         out_specs=[
@@ -270,7 +270,7 @@
         ],
         compiler_params=params_of(56, 2),
         cost_estimate=cost(2 * micros * images * 64 * D_IN * MID, 40 << 20),
-    )(x, w, w2, wide)
+    )(x, wph, wide)
 
 
 def halo_kernel(xh_ref, wb_ref, hh_ref, hs):
@@ -910,12 +910,10 @@
     return jnp.concatenate([a, b], axis=0)
 
 
-def to_first_plane(value):
-    planes = lax.axis_size("g")
-    step = 1
-    while step < planes:
-        value = value + lax.ppermute(value, "g", [(i + step, i) for i in range(0, planes - step, 2 * step)])
-        step *= 2
+def to_plane(value, first, steps=(1, 2)):
+    for step in steps:
+        pairs = [(i ^ step, i) for i in range(GROUPS) if step == 1 and i % 2 == first or i == first]
+        value = value + lax.ppermute(value, "g", pairs)
     return value
 
 
@@ -1037,6 +1035,14 @@
     return grad_act, jnp.concatenate(rows, axis=0), vector, block, loss_sum, live_count, means, variances
 
 
+def place(values, size):
+    flat, at = jnp.zeros((size,), F32), 0
+    for value in values:
+        flat = flat + jnp.pad(value, (at, size - at - value.shape[0]))
+        at += value.shape[0]
+    return flat
+
+
 def norm_coefs(sums, total, gamma, beta):
     mean = sums[:, 0] / total[:, None]
     variance = sums[:, 1] / total[:, None] - mean * mean
@@ -1069,6 +1075,7 @@
     plane_rows = window_rows * LANES
     near = (
         shift * count <= own
+        and lax.axis_size("g") == GROUPS
         and lax.axis_size(PLANE) == LANES
         and ROW_COUT < plane_rows < ROW_PROJ <= 2 * plane_rows
         and window_rows - tail_rows(shift, count) < ROW_CMID <= window_rows
@@ -1079,33 +1086,32 @@
     x = inputs.reshape(micros, images * rows * width, D_IN)
     x_last, mask_last = inputs[:, :, -1], masks[:, :, -1]
     mask = masks.astype(F32)
-    w_in = mask.reshape(micros, -1, 1)
     split = mask.reshape(micros, images, out_rows, 2, out_cols, 2)
     wph = jnp.transpose(split, (0, 3, 5, 1, 2, 4)).reshape(micros, 4, -1, 1)
     around = [(i, i + 1) for i in range(lax.axis_size(("x", "c")) - 1)]
-    mask_halo = lax.ppermute(mask_last, ("x", "c"), around).astype(F32)
     total_in = jnp.sum(mask, axis=(1, 2, 3))
     image_pixels = jnp.sum(split[:, :, :, 0, :, 0], axis=(2, 3))
     total_out = jnp.sum(image_pixels, axis=1)
-    image_pixels = add_all(image_pixels, ("c", "x"))
-    chosen = to_heads(jnp.stack([partner.astype(F32), live.astype(F32)], axis=-1))
+    chosen = jnp.stack([partner.astype(F32), live.astype(F32)], axis=-1)
     if near:
         window = flat_to_window(params, window_rows, shift, index, count)
         column = lax.all_to_all(window, PLANE, 1, 0, tiled=True)
         wide_in, vec = first_rows_everywhere(column, plane, plane_rows)
         trunk = spread_trunk(column, plane, plane_rows)
-        trunk, x_last, wide_in, image_pixels, chosen, mask_halo = lax.optimization_barrier(
-            (trunk, x_last, wide_in, image_pixels, chosen, mask_halo)
-        )
-        h, xe, st, w_first = conv_in(x, w_in, wph[:, 0], wide_in)
+        trunk, x_last, wide_in = lax.optimization_barrier((trunk, x_last, wide_in))
+        h, xe, st, w_first = conv_in(x, wph, wide_in)
         trunk = lax.all_gather(trunk, ALL, axis=0, tiled=False).reshape(GROUPS, LANES, GROUP, 256)
+        st, image_pixels, chosen, mask_last = lax.optimization_barrier((st, image_pixels, chosen, mask_last))
     else:
         wall = lax.all_gather(params.astype(BF16), ALL, axis=0, tiled=True).reshape(-1, 2048)
         wide_in, vec = wall[:ROW_CMID], wall[ROW_VEC : ROW_VEC + 16]
         trunk = jnp.transpose(wall[:ROW_PROJ].reshape(GROUPS, GROUP, LANES, 256), (0, 2, 1, 3))
-        h, xe, st, w_first = conv_in(x, w_in, wph[:, 0], wide_in)
+        h, xe, st, w_first = conv_in(x, wph, wide_in)
 
     x_halo = lax.ppermute(x_last, ("x", "c"), around).reshape(micros, images * width, D_IN)
+    mask_halo = lax.ppermute(mask_last, ("x", "c"), around).astype(F32)
+    image_pixels = add_all(image_pixels, ("c", "x"))
+    chosen = to_heads(chosen)
     whalo = jnp.transpose(mask_halo.reshape(micros, images, out_cols, 2), (0, 3, 1, 2)).reshape(micros, 2, -1, 1)
     share_index = lax.axis_index(("x", "c"))
 
@@ -1115,8 +1121,8 @@
     sums = sums[..., :MID]
     hh = conv_in_halo(x_halo, w_first)
     if near:
-        window, trunk, sums, hh, total_in, total_out = lax.optimization_barrier(
-            (window, trunk, sums, hh, total_in, total_out)
+        window, trunk, sums, hh, total_in, total_out, whalo, image_pixels, chosen = lax.optimization_barrier(
+            (window, trunk, sums, hh, total_in, total_out, whalo, image_pixels, chosen)
         )
         wall = lax.all_gather(window, ALL, axis=0, tiled=True)
 
@@ -1155,19 +1161,14 @@
     )
 
     def vector_rows(gamma, beta, extra):
-        flat, at = jnp.zeros((16 * 2048,), F32), 0
-        for value in gamma + beta + [extra]:
-            flat = flat + jnp.pad(value, (at, flat.shape[0] - at - value.shape[0]))
-            at += value.shape[0]
-        return flat.astype(BF16).reshape(16, 2048)
+        return place(gamma + beta + [extra], 16 * 2048).astype(BF16).reshape(16, 2048)
 
     none_head = [jnp.zeros((n,), F32) for _, n in ranges[4:]]
     none_trunk = [jnp.zeros((n,), F32) for _, n in ranges[:4]]
     head_vector = vector_rows(none_trunk + head_vec[0], none_trunk + head_vec[1], head_vec[2])
     head_vector = lax.dynamic_slice_in_dim(head_vector, block * 256, 256, 1)
 
-    scalars = jnp.pad(jnp.stack([loss_sum, live_count]), (0, 126))
-    head_stats = jnp.concatenate(head_means + head_vars + [scalars]).reshape(1, -1, 128)
+    head_stats = place(head_means + head_vars + [loss_sum[None], live_count[None]], 106 * 128).reshape(1, -1, 128)
     head_stats = exchange_planes(jnp.broadcast_to(head_stats, (micros,) + head_stats.shape[1:])).reshape(micros, -1)
     head_size = NORM - sum(n for _, n in ranges[:4])
     scalars = head_stats[:, 2 * head_size : 2 * head_size + 2]
@@ -1209,11 +1210,14 @@
     if near:
         g_mid, g_out = lax.optimization_barrier((g_mid, g_out))
         g_mid = lax.psum_scatter(g_mid, PLANE, scatter_dimension=0, tiled=False)
-        out_first = to_first_plane(g_out[: plane_rows - ROW_COUT])
-        out_second = add_all(g_out[plane_rows - ROW_COUT :], ("g",))
+        out_first = to_plane(g_out[: plane_rows - ROW_COUT], 0, (1,))
+        out_second = to_plane(g_out[plane_rows - ROW_COUT :], 1, (1,))
     sums = add_all(st[:, :2])
     bi, ci, gamma_in = back_coefs(sums[:, 0], sums[:, 1], mean_in, scale_in, a_in, total_in)
     beta_in = sums[:, 0]
+    if near:
+        bi, ci, out_first, out_second = lax.optimization_barrier((bi, ci, out_first, out_second))
+        out_first, out_second = to_plane(out_first, 0, (2,)), to_plane(out_second, 1, (2,))
     g_in = back_in(h, d_in, d_halo, pack([a_in, bi, ci]), wph, whalo, x, x_halo)
 
     if near:
@@ -1228,13 +1232,13 @@
         def blank(n):
             return jnp.zeros((n, 256), BF16)
 
-        first_rows = jnp.concatenate([blank(ROW_CMID), to_first_plane(g_mid), out_first], axis=0)
+        first_rows = jnp.concatenate([blank(ROW_CMID), to_plane(g_mid, 0), out_first], axis=0)
         second_rows = jnp.concatenate([out_second, blank(plane_rows - out_second.shape[0])], axis=0)
         part = jnp.where(plane == 0, first_rows, jnp.where(plane == 1, head_part + second_rows, head_part))
         window = lax.all_to_all(part, PLANE, 0, 1, tiled=True)
         tail = tail_rows(shift, count)
         prev = lax.ppermute(window[window_rows - tail :], ALL, [(i, i + 1) for i in range(count - 1)])
-        g_in = to_first_plane(g_in)
+        g_in = to_plane(g_in, 0)
         for axis in PLANE:
             g_in = gather_axis(g_in, axis)
         g_in = jnp.transpose(g_in, (3, 2, 1, 0, 4)).reshape(ROW_CMID, 2048)

time: 946 us -> 926 us (0.979)
  waiting for transfers between devices: 324 us -> 281 us
  blocking collectives: 0 us -> 23 us
  starting transfers between devices: 122 us -> 134 us
    ppermute x53 -> x51, waiting for transfers between devices: 184 us -> 157 us  [swap(): return lax.ppermute(value, axis, [(i, i ^ bit) for i in range(size)])]
    all_gather x1, waiting for transfers between devices: 36.5 us -> 11.4 us  [on_device(): lax.all_gather(trunk, ALL, axis=0, tiled=False)]
    all_to_all x0 -> x1, blocking collectives: none -> 23 us  [on_device(): column = lax.all_to_all(window, PLANE, 1, 0, tiled=True)]
    ppermute x53 -> x51, starting transfers between devices: 51.7 us -> 70 us  [swap(): return lax.ppermute(value, axis, [(i, i ^ bit) for i in range(size)])]
    all_to_all x1 -> x0, waiting for transfers between devices: 13.9 us -> none  [on_device(): column = lax.all_to_all(window, PLANE, 1, 0, tiled=True)]
    ppermute x6 -> x8, waiting for transfers between devices: 36.2 us -> 49.7 us  [to_plane(): value = value + lax.ppermute(value, 'g', pairs)]
  transfers between devices with their start and end apart: 89 -> 88, of which waited for: 58 -> 59; matrix products, arithmetic and copies ran while one was open for 12% -> 12% of each run, Pallas kernels for 31% -> 31%
where the time goes in v2:
time: 926 us; the launch traced here: 913 us
  Pallas kernels  295 us (32%)
  waiting for transfers between devices  281 us (30%)
  starting transfers between devices  134 us (14%)
  local copies, waits for them, and re-layouts  63 us (7%)
  matrix products  60.4 us (7%)
  other arithmetic  39.2 us (4%)
  blocking collectives  23 us (2%)
  between operations  17.8 us (2%)
    ppermute x51, waiting for transfers between devices, swap(): return lax.ppermute(value, axis, [(i, i ^ bit) for i in range(size)])  157 us
    ppermute x51, starting transfers between devices, swap(): return lax.ppermute(value, axis, [(i, i ^ bit) for i in range(size)])  70 us
    pallas_call x1, Pallas kernels, back_mid(): pl.pallas_call(back_mid_kernel, grid=(micros,), out_shape=[jax.ShapeDtype...  59.8 us
    pallas_call x1, Pallas kernels, back_out(): pl.pallas_call(back_out_kernel, grid=(micros, OUT // n), out_shape=[jax.S...  53.2 us
    ppermute x8, waiting for transfers between devices, to_plane(): value = value + lax.ppermute(value, 'g', pairs)  49.7 us
    pallas_call x1, Pallas kernels, conv_mid(): pl.pallas_call(conv_mid_kernel, grid=(micros,), out_shape=[jax.ShapeDtype...  31.5 us
    pallas_call x1, Pallas kernels, back_in(): pl.pallas_call(back_in_kernel, grid=(micros, parts), out_shape=jax.ShapeD...  30.1 us
    pallas_call x1, Pallas kernels, conv_in(): pl.pallas_call(conv_in_kernel, grid=(micros, parts), out_shape=[jax.Shape...  27.2 us
  transfers between devices with their start and end apart: 88, of which 59 were waited for; matrix products, arithmetic and copies ran while one was open for 12% of the time, Pallas kernels for 31%

profile of v2, /device:TPU:4, one launch (start us, length us, event | category | flops | bytes accessed | tf_op | source)
XLA Modules:
  0.0 913.3 jit_solution(14393022845669115890)
XLA Ops:
  11.3 6.0 collective-permute-done
  23.0 23.0 %all_to_all.38 = bf16[320,8,256]{2,0,1:T(8,128)(2,1)S(1)} all-to-all(bf16[320,8,256]{2,0,1:T(8,128)(2,1)S(1)} %bitcast.321), channel_id=1, replica_groups=mesh['g'=4,'p'=2,'x'=2,'c'=2] {'p','x','c'}, dimensions={1} | all-to-all | bytes 2621440 | tf_op jit(solution)/shard_map/all_to_all | solution.py:1098
  80.0 7.2 collective-permute-done.1
  98.9 27.2 %shard_map.136 = (f32[4,4,512,512]{3,2,1,0:T(8,128)}, bf16[4,512,1024]{2,1,0:T(8,128)(2,1)}, f32[4,8,512]{2,1,0:T(8,128)}, bf16[1024,512]{1,0:T(8,128)(2,1)}) custom-call(bf16[4,2048,1024]{2,1,0:T(8,128)(2,1)} %bitcast.308, f32[4,4,512,1]{3,2,1,0:T(8,128)} %reshape.1274.w_ref, bf16[256,2048]{1,0:T(8,128)(2,1)} %slice.340.wide_ref), custom_call_target="tpu_custom_call" | custom-call | flops 1073741824 | bytes 5242880 | tf_op jit(solution)/shard_map/pallas_call | solution.py:246
  145.7 14.5 %collective-permute-start.25 = (f32[1,2,2,4,8,2]{4,3,5,2,1,0:T(4,128)S(1)}, f32[1,2,2,4,8,2]{4,3,5,2,1,0:T(4,128)S(1)}, u32[]{:S(2)}, u32[]{:S(2)}) collective-permute-start(f32[1,2,2,4,8,2]{4,3,5,2,1,0:T(4,128)S(1)} %maximum_select_fusion.10), channel_id=1, source_target_pairs={{0,1},{1,0},{2,3},{3,2},{4,5},{5,4},{6,7},{7,6},{8,9},{9,8},{10,11... | collective-permute-start | bytes 3080 | tf_op jit(solution)/shard_map/ppermute | solution.py:850
  164.6 6.0 collective-permute-start.15
  182.9 11.4 %all-gather.6.cloned.1.call-done = bf16[23552,256]{1,0:T(8,128)(2,1)} async-done(((bf16[736,256]{1,0:T(8,128)(2,1)}), bf16[23552,256]{1,0:T(8,128)(2,1)}) %all-gather.6.cloned.1.call-update) | async-done | bytes 12058640 | tf_op jit(solution)/shard_map/all_gather | solution.py:1103
  194.9 20.7 %shard_map.139 = (f32[4,512,2048]{2,1,0:T(8,128)}, f32[4,8,2048]{2,1,0:T(8,128)}) custom-call(bf16[4,512,1024]{2,1,0:T(8,128)(2,1)} %get-tuple-element.118.xe_ref, bf16[4,8,736,256]{3,2,1,0:T(8,128)(2,1)} %bitcast.302, bf16[4,8,736,256]{3,2,1,0:T(8,128)(2,1)} %bitcast.303), custom_call_target="tpu_custom_call" | custom-call | flops 1073741824 | bytes 2097152 | tf_op jit(solution)/shard_map/pallas_call | solution.py:319
  219.0 31.5 %shard_map.138 = (bf16[4,512,4608]{2,1,0:T(8,128)(2,1)}, f32[4,512,512]{2,1,0:T(8,128)}, f32[4,8,512]{2,1,0:T(8,128)}, bf16[4608,512]{1,0:T(8,128)(2,1)}) custom-call(f32[4,4,512,512]{3,2,1,0:T(8,128)} %get-tuple-element.102.h_ref, f32[4,2,256,512]{3,2,1,0:T(8,128)} %copy-done, f32[4,8,512]{2,1,0:T(8,128)} %pad_maximum_fusion.4.cf_ref, ...), custom_call_target="tpu_custom_call" | custom-call | flops 1207959552 | bytes 6553600 | tf_op jit(solution)/shard_map/pallas_call | solution.py:389
  253.1 6.5 collective-permute-done.27
  267.4 11.0 %collective-permute-done.29 = f32[4,2,2560]{2,0,1:T(4,128)S(1)} collective-permute-done((f32[4,2,2560]{2,0,1:T(4,128)S(1)}, f32[4,2,2560]{2,0,1:T(4,128)S(1)}, u32[]{:S(2)}, u32[]{:S(2)}) %collective-permute-start.29) | collective-permute-done | bytes 81952 | tf_op jit(solution)/shard_map/ppermute | solution.py:850
  278.5 10.5 %collective-permute-done.30 = f32[4,2,2560]{2,0,1:T(4,128)S(1)} collective-permute-done((f32[4,2,2560]{2,0,1:T(4,128)S(1)}, f32[4,2,2560]{2,0,1:T(4,128)S(1)}, u32[]{:S(2)}, u32[]{:S(2)}) %collective-permute-start.30) | collective-permute-done | bytes 81952 | tf_op jit(solution)/shard_map/ppermute | solution.py:850
  289.9 12.8 %shard_map.140 = (bf16[4,512,512]{2,1,0:T(8,128)(2,1)}, f32[4,512,2048]{2,1,0:T(8,128)}, f32[4,8,2048]{2,1,0:T(8,128)}, bf16[512,2048]{1,0:T(8,128)(2,1)}) custom-call(f32[4,512,512]{2,1,0:T(8,128)} %get-tuple-element.116.hm_ref, f32[4,8,512]{2,1,0:T(8,128)} %pad_maximum_fusion.3.cf_ref.cm_ref, f32[4,4,512,1]{3,2,1,0:T(8,128)} %reshape.1274.w_ref, ...), custom_call_target="tpu_custom_call" | custom-call | flops 536870912 | bytes 2359296 | tf_op jit(solution)/shard_map/pallas_call | solution.py:439
  315.0 6.3 collective-permute-done.34
  330.1 19.8 %shard_map.141 = f32[4,32,2048]{2,1,0:T(8,128)} custom-call(f32[4,512,2048]{2,1,0:T(8,128)} %get-tuple-element.121.ho_ref, f32[4,512,2048]{2,1,0:T(8,128)} %get-tuple-element.122.hs_ref, f32[4,8,2048]{2,1,0:T(8,128)} %stack.84.cf_ref, f32[4,4,512,1]{3,2,1,0:T(8,128)} %reshape.1274.w_ref), custom_call_target="tpu_custom_call" | custom-call | flops 10485760 | bytes 2359296 | tf_op jit(solution)/shard_map/pallas_call | solution.py:486
  351.1 9.0 collective-permute-start.36
  360.0 20.5 %collective-permute-done.36 = f32[4,16,2048]{2,1,0:T(8,128)S(1)} collective-permute-done((f32[4,16,2048]{2,1,0:T(8,128)S(1)}, f32[4,16,2048]{2,1,0:T(8,128)S(1)}, u32[]{:S(2)}, u32[]{:S(2)}) %collective-permute-start.36) | collective-permute-done | bytes 524320 | tf_op jit(solution)/shard_map/ppermute | solution.py:850
  400.4 7.1 collective-permute-done.42
  410.1 24.2 %shard_map.142 = f32[4,3,32,2048]{3,2,1,0:T(8,128)} custom-call(f32[4,512,2048]{2,1,0:T(8,128)} %get-tuple-element.121.ho_ref, f32[4,512,2048]{2,1,0:T(8,128)} %get-tuple-element.122.hs_ref, f32[4,8,2048]{2,1,0:T(8,128)} %stack.84.cf_ref, f32[4,4,512,1]{3,2,1,0:T(8,128)} %reshape.1274.w_ref), custom_call_target="tpu_custom_call" | custom-call | flops 15728640 | bytes 2621440 | tf_op jit(solution)/shard_map/pallas_call | solution.py:529
  434.5 12.1 %all-gather.4.cloned.1.call-done = bf16[10240,2048]{1,0:T(8,128)(2,1)} async-done(((bf16[320,2048]{1,0:T(8,128)(2,1)}), bf16[10240,2048]{1,0:T(8,128)(2,1)}) %all-gather.4.cloned.1.call-update) | async-done | bytes 41943056 | tf_op jit(solution)/shard_map/all_gather | solution.py:1127
  514.0 6.1 fusion.27
  567.6 8.5 collective-permute-done.53
  577.7 13.3 %collective-permute-done.54 = f32[4,3,2048]{2,0,1:T(4,128)S(1)} collective-permute-done((f32[4,3,2048]{2,0,1:T(4,128)S(1)}, f32[4,3,2048]{2,0,1:T(4,128)S(1)}, u32[]{:S(2)}, u32[]{:S(2)}) %collective-permute-start.54) | collective-permute-done | bytes 98336 | tf_op jit(solution)/shard_map/ppermute | solution.py:850
  592.3 53.2 %shard_map.143 = (f32[4,512,512]{2,1,0:T(8,128)}, f32[4,8,512]{2,1,0:T(8,128)}, bf16[8,1536,256]{2,1,0:T(8,128)(2,1)}) custom-call(f32[4,512,2048]{2,1,0:T(8,128)} %get-tuple-element.121.ho_ref, f32[4,512,2048]{2,1,0:T(8,128)} %get-tuple-element.122.hs_ref, f32[4,32,2048]{2,1,0:T(8,128)} %copy-done.6, f32[4,8,2048]{2,1,0:T(8,128)} %copy.242.cf_ref, ...), custom_call_target="tpu_custom_call" | custom-call | flops 2147483648 | bytes 5242880 | tf_op jit(solution)/shard_map/pallas_call | solution.py:620
  668.9 59.8 %shard_map.144 = (bf16[4,4,512,512]{3,2,1,0:T(8,128)(2,1)}, f32[4,2,256,512]{3,2,1,0:T(8,128)}, f32[4,8,512]{2,1,0:T(8,128)}, bf16[8,1152,256]{2,1,0:T(8,128)(2,1)}) custom-call(f32[4,512,512]{2,1,0:T(8,128)} %get-tuple-element.116.hm_ref, f32[4,512,512]{2,1,0:T(8,128)} %get-tuple-element.132.d_ref, f32[4,8,512]{2,1,0:T(8,128)} %stack.86.cm_ref, ...), custom_call_target="tpu_custom_call" | custom-call | flops 2415919104 | bytes 7864320 | tf_op jit(solution)/shard_map/pallas_call | solution.py:739
  761.1 30.1 %shard_map.145 = bf16[8,256,256]{2,1,0:T(8,128)(2,1)} custom-call(f32[4,4,512,512]{3,2,1,0:T(8,128)} %get-tuple-element.102.h_ref, bf16[4,4,512,512]{3,2,1,0:T(8,128)(2,1)} %get-tuple-element.136.din_ref, f32[4,2,256,512]{3,2,1,0:T(8,128)} %get-tuple-element.137.dh_ref, f32[4,8,512]{2,1,0:T(8,128)} %stack.89.cf_ref, f32[4,4,512,1]{3,2,1,0:T(8,128)} %reshape.1274.w_ref, ...), custom_call_target="tpu_custom_call" | custom-call | flops 1342177280 | bytes 6553600 | tf_op jit(solution)/shard_map/pallas_call | solution.py:823
  800.6 15.4 %collective-permute-done.72 = bf16[1152,256]{1,0:T(8,128)(2,1)S(1)} collective-permute-done((bf16[1152,256]{1,0:T(8,128)(2,1)S(1)}, bf16[1152,256]{1,0:T(8,128)(2,1)S(1)}, u32[]{:S(2)}, u32[]{:S(2)}) %collective-permute-start.72) | collective-permute-done | bytes 589856 | tf_op jit(solution)/shard_map/ppermute | solution.py:916
  831.4 6.2 collective-permute-done.78
  847.2 12.7 %collective-permute-done.75 = bf16[1152,256]{1,0:T(8,128)(2,1)S(1)} collective-permute-done((bf16[1152,256]{1,0:T(8,128)(2,1)S(1)}, bf16[1152,256]{1,0:T(8,128)(2,1)S(1)}, u32[]{:S(2)}, u32[]{:S(2)}) %collective-permute-start.75) | collective-permute-done | bytes 589856 | tf_op jit(solution)/shard_map/ppermute | solution.py:916
  876.5 9.6 %all-to-all-done.1 = bf16[8,320,256]{2,1,0:T(8,128)(2,1)S(1)} async-done(((bf16[8,320,256]{2,1,0:T(8,128)(2,1)}), bf16[8,320,256]{2,1,0:T(8,128)(2,1)S(1)}, u32[]{:S(2)}, u32[]{:S(2)}) %all-to-all-start.1) | async-done | bytes 1310752 | tf_op jit(solution)/shard_map/all_to_all | solution.py:1238
  889.2 8.3 collective-permute-done.76
  897.7 8.7 shard_map.146
  (689 shorter events, 375.9 us)
Async XLA Ops:
  7.2 187.1 %all-gather.6.cloned.1.call-start = ((), (), s32[]{:S(2)}) async-start(), calls=%async_computation.9 | async-start | bytes 12435456 | tf_op jit(solution)/shard_map/all_gather | solution.py:1103
  63.2 11.7 %collective-permute-start.9 = (bf16[1,2,272,256]{3,2,1,0:T(8,128)(2,1)S(1)}, bf16[1,2,272,256]{3,2,1,0:T(8,128)(2,1)S(1)}, u32[]{:S(2)}, u32[]{:S(2)}) collective-permute-start(bf16[1,2,272,256]{3,2,1,0:T(8,128)(2,1)S(1)} %maximum_select_fusion.6), channel_id=1, source_target_pairs={{0,2},{2,0},{1,3},{3,1},{4,6},{6,4},{5,7},{7,5},{8,10},{10,8},{9,1... | collective-permute-start | bytes 835592 | tf_op jit(solution)/shard_map/ppermute | solution.py:850
  64.5 22.8 %collective-permute-start.3 = (bf16[736,256]{1,0:T(8,128)(2,1)S(1)}, bf16[736,256]{1,0:T(8,128)(2,1)S(1)}, u32[]{:S(2)}, u32[]{:S(2)}) collective-permute-start(bf16[736,256]{1,0:T(8,128)(2,1)S(1)} %get-tuple-element.213), channel_id=1, source_target_pairs={{0,16},{1,17},{2,18},{3,19},{4,20},{5,21},{6,22},{7,23}} | collective-permute-start | bytes 1130504 | tf_op jit(solution)/shard_map/ppermute | solution.py:930
  69.5 17.7 %collective-permute-start.4 = (bf16[736,256]{1,0:T(8,128)(2,1)S(1)}, bf16[736,256]{1,0:T(8,128)(2,1)}, u32[]{:S(2)}, u32[]{:S(2)}) collective-permute-start(bf16[736,256]{1,0:T(8,128)(2,1)S(1)} %get-tuple-element.212), channel_id=1, source_target_pairs={{0,8},{1,9},{2,10},{3,11},{4,12},{5,13},{6,14},{7,15}} | collective-permute-start | bytes 1130504 | tf_op jit(solution)/shard_map/ppermute | solution.py:930
  71.5 15.7 %collective-permute-start.2 = (bf16[384,256]{1,0:T(8,128)(2,1)}, bf16[384,256]{1,0:T(8,128)(2,1)}, u32[]{:S(2)}, u32[]{:S(2)}) collective-permute-start(bf16[384,256]{1,0:T(8,128)(2,1)} %slice.412), channel_id=1, source_target_pairs={{8,24},{9,25},{10,26},{11,27},{12,28},{13,29},{14,30},{15,31}} | collective-permute-start | bytes 589832 | tf_op jit(solution)/shard_map/ppermute | solution.py:930
  72.9 14.3 %collective-permute-start.1 = (bf16[352,256]{1,0:T(8,128)(2,1)}, bf16[352,256]{1,0:T(8,128)(2,1)}, u32[]{:S(2)}, u32[]{:S(2)}) collective-permute-start(bf16[352,256]{1,0:T(8,128)(2,1)} %slice.411), channel_id=1, source_target_pairs={{0,24},{1,25},{2,26},{3,27},{4,28},{5,29},{6,30},{7,31}} | collective-permute-start | bytes 540680 | tf_op jit(solution)/shard_map/ppermute | solution.py:930
  75.0 14.2 %collective-permute-start.10 = (bf16[1,2,2,272,256]{4,3,2,1,0:T(8,128)(2,1)S(1)}, bf16[1,2,2,272,256]{4,3,2,1,0:T(8,128)(2,1)S(1)}, u32[]{:S(2)}, u32[]{:S(2)}) collective-permute-start(bf16[1,2,2,272,256]{4,3,2,1,0:T(8,128)(2,1)S(1)} %maximum_select_fusion.3), channel_id=1, source_target_pairs={{0,1},{1,0},{2,3},{3,2},{4,5},{5,4},{6,7},{7,6},{8,9},{9,8},{10,11... | collective-permute-start | bytes 1671176 | tf_op jit(solution)/shard_map/ppermute | solution.py:850
  92.2 354.4 %all-gather.4.cloned.1.call-start = ((), (), s32[]{:S(2)}) async-start(), calls=%async_computation.5 | async-start | bytes 43253760 | tf_op jit(solution)/shard_map/all_gather | solution.py:1127
  92.2 82.4 %collective-permute-start.16 = (bf16[4,32,16,1024]{3,2,1,0:T(8,128)(2,1)}, bf16[4,32,16,1024]{3,2,1,0:T(8,128)(2,1)}, u32[]{:S(2)}, u32[]{:S(2)}) collective-permute-start(bf16[4,32,16,1024]{3,2,1,0:T(8,128)(2,1)} %slice_bitcast_fusion), channel_id=1, source_target_pairs={{0,1},{1,2},{2,3},{4,5},{5,6},{6,7},{8,9},{9,10},{10,11},{12,13},{... | collective-permute-start | bytes 12582920 | tf_op jit(solution)/shard_map/ppermute | solution.py:1111
  133.2 27.0 %collective-permute-start.18 = (f32[4,32]{1,0:T(4,128)S(1)}, f32[4,32]{1,0:T(4,128)S(1)}, u32[]{:S(2)}, u32[]{:S(2)}) collective-permute-start(f32[4,32]{1,0:T(4,128)S(1)} %get-tuple-element.109), channel_id=1, source_target_pairs={{0,1},{1,0},{2,3},{3,2},{4,5},{5,4},{6,7},{7,6},{8,9},{9,8},{10,11... | collective-permute-start | bytes 1544 | tf_op jit(solution)/shard_map/ppermute | solution.py:850
  145.6 19.0 %collective-permute-start.14 = (f32[4,2,640]{2,0,1:T(4,128)S(1)}, f32[4,2,640]{2,0,1:T(4,128)S(1)}, u32[]{:S(2)}, u32[]{:S(2)}) collective-permute-start(f32[4,2,640]{2,0,1:T(4,128)S(1)} %add.787), channel_id=1, source_target_pairs={{0,8},{8,0},{16,24},{24,16},{1,9},{9,1},{17,25},{25,17},{2,10},{10... | collective-permute-start | bytes 61448 | tf_op jit(solution)/shard_map/ppermute | solution.py:850
  145.7 25.0 %collective-permute-start.25 = (f32[1,2,2,4,8,2]{4,3,5,2,1,0:T(4,128)S(1)}, f32[1,2,2,4,8,2]{4,3,5,2,1,0:T(4,128)S(1)}, u32[]{:S(2)}, u32[]{:S(2)}) collective-permute-start(f32[1,2,2,4,8,2]{4,3,5,2,1,0:T(4,128)S(1)} %maximum_select_fusion.10), channel_id=1, source_target_pairs={{0,1},{1,0},{2,3},{3,2},{4,5},{5,4},{6,7},{7,6},{8,9},{9,8},{10,11... | collective-permute-start | bytes 3080 | tf_op jit(solution)/shard_map/ppermute | solution.py:850
  194.3 455.1 %reduce-scatter.4.cloned.1.call-start = ((), (), s32[]{:S(2)}) async-start(), calls=%async_computation.6 | async-start | bytes 6553600 | tf_op jit(solution)/shard_map/reduce_scatter | solution.py:1190
  265.8 12.6 %collective-permute-start.29 = (f32[4,2,2560]{2,0,1:T(4,128)S(1)}, f32[4,2,2560]{2,0,1:T(4,128)S(1)}, u32[]{:S(2)}, u32[]{:S(2)}) collective-permute-start(f32[4,2,2560]{2,0,1:T(4,128)S(1)} %add.804), channel_id=1, source_target_pairs={{0,8},{8,0},{16,24},{24,16},{1,9},{9,1},{17,25},{25,17},{2,10},{10... | collective-permute-start | bytes 245768 | tf_op jit(solution)/shard_map/ppermute | solution.py:850
  351.1 29.5 %collective-permute-start.36 = (f32[4,16,2048]{2,1,0:T(8,128)S(1)}, f32[4,16,2048]{2,1,0:T(8,128)S(1)}, u32[]{:S(2)}, u32[]{:S(2)}) collective-permute-start(f32[4,16,2048]{2,1,0:T(8,128)S(1)} %constant_dynamic-slice_fusion.7), channel_id=1, source_target_pairs={{0,2},{2,0},{1,3},{3,1},{4,6},{6,4},{5,7},{7,5},{8,10},{10,8},{9,1... | collective-permute-start | bytes 1572872 | tf_op jit(solution)/shard_map/ppermute | solution.py:850
  407.5 26.8 %collective-permute-start.43 = (bf16[1,2,2,4,8,2048]{5,4,0,1,2,3:T(8,128)(2,1)S(1)}, bf16[1,2,2,4,8,2048]{5,4,0,1,2,3:T(8,128)(2,1)S(1)}, u32[]{:S(2)}, u32[]{:S(2)}) collective-permute-start(bf16[1,2,2,4,8,2048]{5,4,0,1,2,3:T(8,128)(2,1)S(1)} %maximum_select_fusion.4), channel_id=1, source_target_pairs={{0,1},{1,0},{2,3},{3,2},{4,5},{5,4},{6,7},{7,6},{8,9},{9,8},{10,11... | collective-permute-start | bytes 1572872 | tf_op jit(solution)/shard_map/ppermute | solution.py:850
  485.6 58.6 %collective-permute-start.44 = (f32[1,106,128]{2,1,0:T(8,128)}, f32[1,106,128]{2,1,0:T(8,128)}, u32[]{:S(2)}, u32[]{:S(2)}) collective-permute-start(f32[1,106,128]{2,1,0:T(8,128)} %add_bitcast_fusion), channel_id=1, source_target_pairs={{0,8},{8,16},{16,24},{24,0},{1,9},{9,17},{17,25},{25,1},{2,10},{10... | collective-permute-start | bytes 162824 | tf_op jit(solution)/shard_map/ppermute | solution.py:875
  485.6 62.3 %collective-permute-start.45 = (f32[1,106,128]{2,1,0:T(8,128)}, f32[1,106,128]{2,1,0:T(8,128)}, u32[]{:S(2)}, u32[]{:S(2)}) collective-permute-start(f32[1,106,128]{2,1,0:T(8,128)} %add_bitcast_fusion), channel_id=1, source_target_pairs={{0,16},{8,24},{16,0},{24,8},{1,17},{9,25},{17,1},{25,9},{2,18},{10... | collective-permute-start | bytes 162824 | tf_op jit(solution)/shard_map/ppermute | solution.py:875
  487.5 61.3 %collective-permute-start.46 = (f32[1,106,128]{2,1,0:T(8,128)}, f32[1,106,128]{2,1,0:T(8,128)}, u32[]{:S(2)}, u32[]{:S(2)}) collective-permute-start(f32[1,106,128]{2,1,0:T(8,128)} %add_bitcast_fusion), channel_id=1, source_target_pairs={{0,24},{8,0},{16,8},{24,16},{1,25},{9,1},{17,9},{25,17},{2,26},{10... | collective-permute-start | bytes 162824 | tf_op jit(solution)/shard_map/ppermute | solution.py:875
  521.9 27.8 %collective-permute-start.47 = (bf16[1,32,2048]{2,1,0:T(8,128)(2,1)}, bf16[1,32,2048]{2,1,0:T(8,128)(2,1)}, u32[]{:S(2)}, u32[]{:S(2)}) collective-permute-start(bf16[1,32,2048]{2,1,0:T(8,128)(2,1)} %get-tuple-element.216), channel_id=1, source_target_pairs={{0,8},{8,16},{16,24},{24,0},{1,9},{9,17},{17,25},{25,1},{2,10},{10... | collective-permute-start | bytes 393224 | tf_op jit(solution)/shard_map/ppermute | solution.py:875
  522.1 28.5 %collective-permute-start.48 = (bf16[1,32,2048]{2,1,0:T(8,128)(2,1)}, bf16[1,32,2048]{2,1,0:T(8,128)(2,1)}, u32[]{:S(2)}, u32[]{:S(2)}) collective-permute-start(bf16[1,32,2048]{2,1,0:T(8,128)(2,1)} %get-tuple-element.215), channel_id=1, source_target_pairs={{0,16},{8,24},{16,0},{24,8},{1,17},{9,25},{17,1},{25,9},{2,18},{10... | collective-permute-start | bytes 393224 | tf_op jit(solution)/shard_map/ppermute | solution.py:875
  552.4 176.4 %reduce-scatter.6.cloned.1.call-start = ((), (), s32[]{:S(2)}) async-start(), calls=%async_computation.7 | async-start | bytes 7077888 | tf_op jit(solution)/shard_map/reduce_scatter | solution.py:1203
  576.2 14.7 %collective-permute-start.54 = (f32[4,3,2048]{2,0,1:T(4,128)S(1)}, f32[4,3,2048]{2,0,1:T(4,128)S(1)}, u32[]{:S(2)}, u32[]{:S(2)}) collective-permute-start(f32[4,3,2048]{2,0,1:T(4,128)S(1)} %add.881), channel_id=1, source_target_pairs={{0,16},{8,24},{16,0},{24,8},{1,17},{9,25},{17,1},{25,9},{2,18},{10... | collective-permute-start | bytes 294920 | tf_op jit(solution)/shard_map/ppermute | solution.py:850
  649.5 171.8 %reduce-scatter.8.cloned.1.call-start = ((), (), s32[]{:S(2)}) async-start(), calls=%async_computation.8 | async-start | bytes 5308416 | tf_op jit(solution)/shard_map/reduce_scatter | solution.py:1212
  747.3 13.0 %collective-permute-start.65 = (bf16[1152,256]{1,0:T(8,128)(2,1)S(1)}, bf16[1152,256]{1,0:T(8,128)(2,1)S(1)}, u32[]{:S(2)}, u32[]{:S(2)}) collective-permute-start(bf16[1152,256]{1,0:T(8,128)(2,1)S(1)} %slice.394), channel_id=1, source_target_pairs={{8,0},{24,16},{9,1},{25,17},{10,2},{26,18},{11,3},{27,19},{12,4},{... | collective-permute-start | bytes 1769480 | tf_op jit(solution)/shard_map/ppermute | solution.py:916
  795.3 20.8 %collective-permute-start.72 = (bf16[1152,256]{1,0:T(8,128)(2,1)S(1)}, bf16[1152,256]{1,0:T(8,128)(2,1)S(1)}, u32[]{:S(2)}, u32[]{:S(2)}) collective-permute-start(bf16[1152,256]{1,0:T(8,128)(2,1)S(1)} %slice_add_fusion.6), channel_id=1, source_target_pairs={{16,0},{17,1},{18,2},{19,3},{20,4},{21,5},{22,6},{23,7}} | collective-permute-start | bytes 1769480 | tf_op jit(solution)/shard_map/ppermute | solution.py:916
  797.8 18.5 %collective-permute-start.68 = (bf16[2,128,256]{2,1,0:T(8,128)(2,1)S(1)}, bf16[2,128,256]{2,1,0:T(8,128)(2,1)S(1)}, u32[]{:S(2)}, u32[]{:S(2)}) collective-permute-start(bf16[2,128,256]{2,1,0:T(8,128)(2,1)S(1)} %dynamic-slice_bitcast_fusion.2), channel_id=1, source_target_pairs={{0,2},{2,0},{1,3},{3,1},{4,6},{6,4},{5,7},{7,5},{8,10},{10,8},{9,1... | collective-permute-start | bytes 393224 | tf_op jit(solution)/shard_map/ppermute | solution.py:850
  800.0 16.9 %collective-permute-start.70 = (bf16[2,128,256]{2,1,0:T(8,128)(2,1)S(1)}, bf16[2,128,256]{2,1,0:T(8,128)(2,1)S(1)}, u32[]{:S(2)}, u32[]{:S(2)}) collective-permute-start(bf16[2,128,256]{2,1,0:T(8,128)(2,1)S(1)} %dynamic-slice_bitcast_fusion.1), channel_id=1, source_target_pairs={{0,4},{4,0},{1,5},{5,1},{2,6},{6,2},{3,7},{7,3},{8,12},{12,8},{9,1... | collective-permute-start | bytes 393224 | tf_op jit(solution)/shard_map/ppermute | solution.py:850
  822.9 20.5 %collective-permute-start.74 = (bf16[1152,256]{1,0:T(8,128)(2,1)}, bf16[1152,256]{1,0:T(8,128)(2,1)S(1)}, u32[]{:S(2)}, u32[]{:S(2)}) collective-permute-start(bf16[1152,256]{1,0:T(8,128)(2,1)} %bitcast.340), channel_id=1, source_target_pairs={{8,0},{24,16},{9,1},{25,17},{10,2},{26,18},{11,3},{27,19},{12,4},{... | collective-permute-start | bytes 1769480 | tf_op jit(solution)/shard_map/ppermute | solution.py:916
  843.5 16.3 %collective-permute-start.75 = (bf16[1152,256]{1,0:T(8,128)(2,1)S(1)}, bf16[1152,256]{1,0:T(8,128)(2,1)S(1)}, u32[]{:S(2)}, u32[]{:S(2)}) collective-permute-start(bf16[1152,256]{1,0:T(8,128)(2,1)S(1)} %add.908), channel_id=1, source_target_pairs={{16,0},{17,1},{18,2},{19,3},{20,4},{21,5},{22,6},{23,7}} | collective-permute-start | bytes 1769480 | tf_op jit(solution)/shard_map/ppermute | solution.py:916
  845.8 23.6 %collective-permute-start.80 = (bf16[1,2,256,256]{3,2,1,0:T(8,128)(2,1)S(1)}, bf16[1,2,256,256]{3,2,1,0:T(8,128)(2,1)S(1)}, u32[]{:S(2)}, u32[]{:S(2)}) collective-permute-start(bf16[1,2,256,256]{3,2,1,0:T(8,128)(2,1)S(1)} %maximum_select_fusion.8), channel_id=1, source_target_pairs={{0,2},{2,0},{1,3},{3,1},{4,6},{6,4},{5,7},{7,5},{8,10},{10,8},{9,1... | collective-permute-start | bytes 786440 | tf_op jit(solution)/shard_map/ppermute | solution.py:850
  864.9 21.2 %all-to-all-start.1 = ((bf16[8,320,256]{2,1,0:T(8,128)(2,1)}), bf16[8,320,256]{2,1,0:T(8,128)(2,1)S(1)}, u32[]{:S(2)}, u32[]{:S(2)}) async-start(bf16[8,320,256]{2,1,0:T(8,128)(2,1)} %bitcast.79), calls=%async_computation.4 | async-start | bytes 2621440 | tf_op jit(solution)/shard_map/all_to_all | solution.py:1238
  (184 other events, 2212.9 us)
Sparse Core Ops, SparseCore 0:
  92.3 101.9 all-gather.5
  197.7 248.8 all-gather.3
  552.5 96.9 reduce-scatter.3
  652.7 62.0 reduce-scatter.5
  729.0 54.6 reduce-scatter.7

commit v3 on v2

--- a/solution.py
+++ b/solution.py
@@ -816,8 +816,8 @@
                 gw_ref[k, :, half * 128 : half * 128 + 128] = found.astype(BF16)
 
 
-def back_in(h, din, dhalo, coef, wph, whalo, x, xh):
-    micros, _, rows, _ = h.shape
+def back_in(h, din, dhalo, coef, wph, whalo, x, xh, first, micros):
+    rows = h.shape[2]
     parts = 2
     r = rows // parts
     return pl.pallas_call(
@@ -825,14 +825,14 @@
         grid=(micros, parts),
         out_shape=jax.ShapeDtypeStruct((LANES, 256, 256), BF16),
         in_specs=[
-            pl.BlockSpec((1, 4, r, MID), lambda m, k: (m, 0, k, 0)),
-            pl.BlockSpec((1, 4, r, MID), lambda m, k: (m, 0, k, 0)),
-            pl.BlockSpec((1, 2, r // 2, MID), lambda m, k: (m, 0, k, 0)),
-            pl.BlockSpec((1, 8, MID), lambda m, k: (m, 0, 0)),
-            pl.BlockSpec((1, 4, r, 1), lambda m, k: (m, 0, k, 0)),
-            pl.BlockSpec((1, 2, r // 2, 1), lambda m, k: (m, 0, k, 0)),
-            pl.BlockSpec((1, r * 4, D_IN), lambda m, k: (m, k, 0)),
-            pl.BlockSpec((1, r, D_IN), lambda m, k: (m, k, 0)),
+            pl.BlockSpec((1, 4, r, MID), lambda m, k: (m + first, 0, k, 0)),
+            pl.BlockSpec((1, 4, r, MID), lambda m, k: (m + first, 0, k, 0)),
+            pl.BlockSpec((1, 2, r // 2, MID), lambda m, k: (m + first, 0, k, 0)),
+            pl.BlockSpec((1, 8, MID), lambda m, k: (m + first, 0, 0)),
+            pl.BlockSpec((1, 4, r, 1), lambda m, k: (m + first, 0, k, 0)),
+            pl.BlockSpec((1, 2, r // 2, 1), lambda m, k: (m + first, 0, k, 0)),
+            pl.BlockSpec((1, r * 4, D_IN), lambda m, k: (m + first, k, 0)),
+            pl.BlockSpec((1, r, D_IN), lambda m, k: (m + first, k, 0)),
         ],
         out_specs=whole_block((LANES, 256, 256)),
         scratch_shapes=[
@@ -1208,22 +1208,28 @@
         hm, d_mid, pack([a_mid, bm, cm]), cols, w_mid, h, hh, coef_in, wph, whalo
     )
     if near:
-        g_mid, g_out = lax.optimization_barrier((g_mid, g_out))
-        g_mid = lax.psum_scatter(g_mid, PLANE, scatter_dimension=0, tiled=False)
+        g_mid = halve(g_mid.reshape(2, 2, 2, GRAD_MID, 256), "c", 2)
         out_first = to_plane(g_out[: plane_rows - ROW_COUT], 0, (1,))
         out_second = to_plane(g_out[plane_rows - ROW_COUT :], 1, (1,))
     sums = add_all(st[:, :2])
     bi, ci, gamma_in = back_coefs(sums[:, 0], sums[:, 1], mean_in, scale_in, a_in, total_in)
     beta_in = sums[:, 0]
+    half = micros // 2
     if near:
-        bi, ci, out_first, out_second = lax.optimization_barrier((bi, ci, out_first, out_second))
+        bi, ci, g_mid = lax.optimization_barrier((bi, ci, g_mid))
+        coef = pack([a_in, bi, ci])
+        g_in = back_in(h, d_in, d_halo, coef, wph, whalo, x, x_halo, 0, half)
+        upper, lower = halve(g_mid[:, :, : GRAD_MID // 2], "x", 1), halve(g_mid[:, :, GRAD_MID // 2 :], "p", 0)
+        g_in, coef, upper, lower, out_first, out_second = lax.optimization_barrier(
+            (g_in, coef, upper, lower, out_first, out_second)
+        )
         out_first, out_second = to_plane(out_first, 0, (2,)), to_plane(out_second, 1, (2,))
-    g_in = back_in(h, d_in, d_halo, pack([a_in, bi, ci]), wph, whalo, x, x_halo)
-
-    if near:
-        g_in, g_mid, out_first, out_second = lax.optimization_barrier(
-            (plane_reduce(g_in), g_mid, out_first, out_second)
-        )
+        g_in = g_in + back_in(h, d_in, d_halo, coef, wph, whalo, x, x_halo, half, micros - half)
+        g_mid = jnp.concatenate([halve(upper, "p", 0), halve(lower, "x", 0)], axis=0)
+        g_in = plane_reduce(g_in)
+    else:
+        g_in = back_in(h, d_in, d_halo, pack([a_in, bi, ci]), wph, whalo, x, x_halo, 0, micros)
+
     trunk_gamma = [jnp.sum(v, axis=0) for v in (gamma_in, gamma_mid, gamma_out, gamma_side)]
     trunk_beta = [jnp.sum(v, axis=0) for v in (beta_in, beta_mid, beta_joined, beta_joined)]
     trunk_vector = vector_rows(trunk_gamma + none_head, trunk_beta + none_head, jnp.zeros((OUT,), F32))

time: 926 us -> 937 us (1.012)
    ppermute x51 -> x56, waiting for transfers between devices: 157 us -> 181 us  [swap(): return lax.ppermute(value, axis, [(i, i ^ bit) for i in range(size)])]
    ppermute x8, waiting for transfers between devices: 49.7 us -> 28 us  [to_plane(): value = value + lax.ppermute(value, 'g', pairs)]
    ppermute x51 -> x56, starting transfers between devices: 70 us -> 63.4 us  [swap(): return lax.ppermute(value, axis, [(i, i ^ bit) for i in range(size)])]
    pallas_call x1 -> x2, Pallas kernels: 30.1 us -> 34.5 us  [back_in(): pl.pallas_call(back_in_kernel, grid=(micros, parts), out_shape=jax.ShapeD...]
  transfers between devices with their start and end apart: 88 -> 92, of which waited for: 59 -> 62; matrix products, arithmetic and copies ran while one was open for 12% -> 12% of each run, Pallas kernels for 31% -> 29%
where the time goes in v3:
time: 937 us; the launch traced here: 927 us
  Pallas kernels  300 us (32%)
  waiting for transfers between devices  286 us (31%)
  starting transfers between devices  129 us (14%)
  local copies, waits for them, and re-layouts  69.2 us (7%)
  matrix products  60.5 us (6%)
  other arithmetic  41.6 us (4%)
  blocking collectives  23 us (2%)
  between operations  17.6 us (2%)
    ppermute x56, waiting for transfers between devices, swap(): return lax.ppermute(value, axis, [(i, i ^ bit) for i in range(size)])  181 us
    ppermute x56, starting transfers between devices, swap(): return lax.ppermute(value, axis, [(i, i ^ bit) for i in range(size)])  63.4 us
    pallas_call x1, Pallas kernels, back_mid(): pl.pallas_call(back_mid_kernel, grid=(micros,), out_shape=[jax.ShapeDtype...  60.1 us
    pallas_call x1, Pallas kernels, back_out(): pl.pallas_call(back_out_kernel, grid=(micros, OUT // n), out_shape=[jax.S...  53.1 us
    pallas_call x2, Pallas kernels, back_in(): pl.pallas_call(back_in_kernel, grid=(micros, parts), out_shape=jax.ShapeD...  34.5 us
    pallas_call x1, Pallas kernels, conv_mid(): pl.pallas_call(conv_mid_kernel, grid=(micros,), out_shape=[jax.ShapeDtype...  31.5 us
    ppermute x8, waiting for transfers between devices, to_plane(): value = value + lax.ppermute(value, 'g', pairs)  28 us
    pallas_call x1, Pallas kernels, conv_in(): pl.pallas_call(conv_in_kernel, grid=(micros, parts), out_shape=[jax.Shape...  27.2 us
  transfers between devices with their start and end apart: 92, of which 62 were waited for; matrix products, arithmetic and copies ran while one was open for 12% of the time, Pallas kernels for 29%

profile of v3, /device:TPU:4, one launch (start us, length us, event | category | flops | bytes accessed | tf_op | source)
XLA Modules:
  0.0 926.6 jit_solution(12429845909254963745)
XLA Ops:
  11.3 6.0 collective-permute-done
  23.0 23.0 %all_to_all.38 = bf16[320,8,256]{2,0,1:T(8,128)(2,1)S(1)} all-to-all(bf16[320,8,256]{2,0,1:T(8,128)(2,1)S(1)} %bitcast.349), channel_id=1, replica_groups=mesh['g'=4,'p'=2,'x'=2,'c'=2] {'p','x','c'}, dimensions={1} | all-to-all | bytes 2621440 | tf_op jit(solution)/shard_map/all_to_all | solution.py:1098
  80.1 7.1 collective-permute-done.1
  99.0 27.2 %shard_map.136 = (f32[4,4,512,512]{3,2,1,0:T(8,128)}, bf16[4,512,1024]{2,1,0:T(8,128)(2,1)}, f32[4,8,512]{2,1,0:T(8,128)}, bf16[1024,512]{1,0:T(8,128)(2,1)}) custom-call(bf16[4,2048,1024]{2,1,0:T(8,128)(2,1)} %bitcast.335, f32[4,4,512,1]{3,2,1,0:T(8,128)} %reshape.1280.w_ref, bf16[256,2048]{1,0:T(8,128)(2,1)} %slice.352.wide_ref), custom_call_target="tpu_custom_call" | custom-call | flops 1073741824 | bytes 5242880 | tf_op jit(solution)/shard_map/pallas_call | solution.py:246
  145.7 14.7 %collective-permute-start.25 = (f32[1,2,2,4,8,2]{4,3,5,2,1,0:T(4,128)S(1)}, f32[1,2,2,4,8,2]{4,3,5,2,1,0:T(4,128)S(1)}, u32[]{:S(2)}, u32[]{:S(2)}) collective-permute-start(f32[1,2,2,4,8,2]{4,3,5,2,1,0:T(4,128)S(1)} %maximum_select_fusion.10), channel_id=1, source_target_pairs={{0,1},{1,0},{2,3},{3,2},{4,5},{5,4},{6,7},{7,6},{8,9},{9,8},{10,11... | collective-permute-start | bytes 3080 | tf_op jit(solution)/shard_map/ppermute | solution.py:850
  182.9 11.3 %all-gather.6.cloned.1.call-done = bf16[23552,256]{1,0:T(8,128)(2,1)} async-done(((bf16[736,256]{1,0:T(8,128)(2,1)}), bf16[23552,256]{1,0:T(8,128)(2,1)}) %all-gather.6.cloned.1.call-update) | async-done | bytes 12058640 | tf_op jit(solution)/shard_map/all_gather | solution.py:1103
  194.8 20.5 %shard_map.139 = (f32[4,512,2048]{2,1,0:T(8,128)}, f32[4,8,2048]{2,1,0:T(8,128)}) custom-call(bf16[4,512,1024]{2,1,0:T(8,128)(2,1)} %get-tuple-element.117.xe_ref, bf16[4,8,736,256]{3,2,1,0:T(8,128)(2,1)} %bitcast.329, bf16[4,8,736,256]{3,2,1,0:T(8,128)(2,1)} %bitcast.330), custom_call_target="tpu_custom_call" | custom-call | flops 1073741824 | bytes 2097152 | tf_op jit(solution)/shard_map/pallas_call | solution.py:319
  218.6 31.5 %shard_map.138 = (bf16[4,512,4608]{2,1,0:T(8,128)(2,1)}, f32[4,512,512]{2,1,0:T(8,128)}, f32[4,8,512]{2,1,0:T(8,128)}, bf16[4608,512]{1,0:T(8,128)(2,1)}) custom-call(f32[4,4,512,512]{3,2,1,0:T(8,128)} %get-tuple-element.101.h_ref, f32[4,2,256,512]{3,2,1,0:T(8,128)} %copy-done, f32[4,8,512]{2,1,0:T(8,128)} %pad_maximum_fusion.5.cf_ref, ...), custom_call_target="tpu_custom_call" | custom-call | flops 1207959552 | bytes 6553600 | tf_op jit(solution)/shard_map/pallas_call | solution.py:389
  252.9 6.4 collective-permute-done.27
  267.2 11.1 %collective-permute-done.29 = f32[4,2,2560]{2,0,1:T(4,128)S(1)} collective-permute-done((f32[4,2,2560]{2,0,1:T(4,128)S(1)}, f32[4,2,2560]{2,0,1:T(4,128)S(1)}, u32[]{:S(2)}, u32[]{:S(2)}) %collective-permute-start.29) | collective-permute-done | bytes 81952 | tf_op jit(solution)/shard_map/ppermute | solution.py:850
  278.4 10.4 %collective-permute-done.30 = f32[4,2,2560]{2,0,1:T(4,128)S(1)} collective-permute-done((f32[4,2,2560]{2,0,1:T(4,128)S(1)}, f32[4,2,2560]{2,0,1:T(4,128)S(1)}, u32[]{:S(2)}, u32[]{:S(2)}) %collective-permute-start.30) | collective-permute-done | bytes 81952 | tf_op jit(solution)/shard_map/ppermute | solution.py:850
  289.8 12.8 %shard_map.140 = (bf16[4,512,512]{2,1,0:T(8,128)(2,1)}, f32[4,512,2048]{2,1,0:T(8,128)}, f32[4,8,2048]{2,1,0:T(8,128)}, bf16[512,2048]{1,0:T(8,128)(2,1)}) custom-call(f32[4,512,512]{2,1,0:T(8,128)} %get-tuple-element.115.hm_ref, f32[4,8,512]{2,1,0:T(8,128)} %pad_maximum_fusion.4.cf_ref.cm_ref, f32[4,4,512,1]{3,2,1,0:T(8,128)} %reshape.1280.w_ref, ...), custom_call_target="tpu_custom_call" | custom-call | flops 536870912 | bytes 2359296 | tf_op jit(solution)/shard_map/pallas_call | solution.py:439
  314.7 6.3 collective-permute-done.34
  330.1 19.7 %shard_map.141 = f32[4,32,2048]{2,1,0:T(8,128)} custom-call(f32[4,512,2048]{2,1,0:T(8,128)} %get-tuple-element.120.ho_ref, f32[4,512,2048]{2,1,0:T(8,128)} %get-tuple-element.121.hs_ref, f32[4,8,2048]{2,1,0:T(8,128)} %stack.84.cf_ref, f32[4,4,512,1]{3,2,1,0:T(8,128)} %reshape.1280.w_ref), custom_call_target="tpu_custom_call" | custom-call | flops 10485760 | bytes 2359296 | tf_op jit(solution)/shard_map/pallas_call | solution.py:486
  351.6 24.3 %collective-permute-done.36 = f32[4,16,2048]{2,1,0:T(8,128)S(1)} collective-permute-done((f32[4,16,2048]{2,1,0:T(8,128)S(1)}, f32[4,16,2048]{2,1,0:T(8,128)S(1)}, u32[]{:S(2)}, u32[]{:S(2)}) %collective-permute-start.36) | collective-permute-done | bytes 524320 | tf_op jit(solution)/shard_map/ppermute | solution.py:850
  386.3 6.3 collective-permute-done.39
  399.8 6.6 collective-permute-done.42
  409.1 24.3 %shard_map.142 = f32[4,3,32,2048]{3,2,1,0:T(8,128)} custom-call(f32[4,512,2048]{2,1,0:T(8,128)} %get-tuple-element.120.ho_ref, f32[4,512,2048]{2,1,0:T(8,128)} %get-tuple-element.121.hs_ref, f32[4,8,2048]{2,1,0:T(8,128)} %stack.84.cf_ref, f32[4,4,512,1]{3,2,1,0:T(8,128)} %reshape.1280.w_ref), custom_call_target="tpu_custom_call" | custom-call | flops 15728640 | bytes 2621440 | tf_op jit(solution)/shard_map/pallas_call | solution.py:529
  433.5 14.4 %all-gather.4.cloned.1.call-done = bf16[10240,2048]{1,0:T(8,128)(2,1)} async-done(((bf16[320,2048]{1,0:T(8,128)(2,1)}), bf16[10240,2048]{1,0:T(8,128)(2,1)}) %all-gather.4.cloned.1.call-update) | async-done | bytes 41943056 | tf_op jit(solution)/shard_map/all_gather | solution.py:1127
  514.3 6.1 fusion.27
  567.9 9.6 %collective-permute-done.53 = f32[4,3,2048]{2,0,1:T(4,128)S(1)} collective-permute-done((f32[4,3,2048]{2,0,1:T(4,128)S(1)}, f32[4,3,2048]{2,0,1:T(4,128)S(1)}, u32[]{:S(2)}, u32[]{:S(2)}) %collective-permute-start.53) | collective-permute-done | bytes 98336 | tf_op jit(solution)/shard_map/ppermute | solution.py:850
  578.8 13.2 %collective-permute-done.54 = f32[4,3,2048]{2,0,1:T(4,128)S(1)} collective-permute-done((f32[4,3,2048]{2,0,1:T(4,128)S(1)}, f32[4,3,2048]{2,0,1:T(4,128)S(1)}, u32[]{:S(2)}, u32[]{:S(2)}) %collective-permute-start.54) | collective-permute-done | bytes 98336 | tf_op jit(solution)/shard_map/ppermute | solution.py:850
  593.4 53.1 %shard_map.143 = (f32[4,512,512]{2,1,0:T(8,128)}, f32[4,8,512]{2,1,0:T(8,128)}, bf16[8,1536,256]{2,1,0:T(8,128)(2,1)}) custom-call(f32[4,512,2048]{2,1,0:T(8,128)} %get-tuple-element.120.ho_ref, f32[4,512,2048]{2,1,0:T(8,128)} %get-tuple-element.121.hs_ref, f32[4,32,2048]{2,1,0:T(8,128)} %copy-done.6, f32[4,8,2048]{2,1,0:T(8,128)} %copy.248.cf_ref, ...), custom_call_target="tpu_custom_call" | custom-call | flops 2147483648 | bytes 5242880 | tf_op jit(solution)/shard_map/pallas_call | solution.py:620
  670.1 60.1 %shard_map.144 = (bf16[4,4,512,512]{3,2,1,0:T(8,128)(2,1)}, f32[4,2,256,512]{3,2,1,0:T(8,128)}, f32[4,8,512]{2,1,0:T(8,128)}, bf16[8,1152,256]{2,1,0:T(8,128)(2,1)}) custom-call(f32[4,512,512]{2,1,0:T(8,128)} %get-tuple-element.115.hm_ref, f32[4,512,512]{2,1,0:T(8,128)} %get-tuple-element.131.d_ref, f32[4,8,512]{2,1,0:T(8,128)} %stack.86.cm_ref, ...), custom_call_target="tpu_custom_call" | custom-call | flops 2415919104 | bytes 7864320 | tf_op jit(solution)/shard_map/pallas_call | solution.py:739
  762.8 17.2 %shard_map.145 = bf16[8,256,256]{2,1,0:T(8,128)(2,1)} custom-call(f32[4,4,512,512]{3,2,1,0:T(8,128)} %get-tuple-element.101.h_ref, bf16[4,4,512,512]{3,2,1,0:T(8,128)(2,1)} %get-tuple-element.135.din_ref, f32[4,2,256,512]{3,2,1,0:T(8,128)} %get-tuple-element.136.dh_ref, f32[4,8,512]{2,1,0:T(8,128)} %stack.89.cf_ref, f32[4,4,512,1]{3,2,1,0:T(8,128)} %reshape.1280.w_ref, ...), custom_call_target="tpu_custom_call" | custom-call | flops 671088640 | bytes 6553600 | tf_op jit(solution)/shard_map/pallas_call | solution.py:823
  795.1 17.3 %shard_map.146 = bf16[8,256,256]{2,1,0:T(8,128)(2,1)} custom-call(f32[4,4,512,512]{3,2,1,0:T(8,128)} %get-tuple-element.101.h_ref, bf16[4,4,512,512]{3,2,1,0:T(8,128)(2,1)} %get-tuple-element.135.din_ref, f32[4,2,256,512]{3,2,1,0:T(8,128)} %get-tuple-element.136.dh_ref, f32[4,8,512]{2,1,0:T(8,128)} %stack.89.cf_ref, f32[4,4,512,1]{3,2,1,0:T(8,128)} %reshape.1280.w_ref, ...), custom_call_target="tpu_custom_call" | custom-call | flops 671088640 | bytes 6553600 | tf_op jit(solution)/shard_map/pallas_call | solution.py:823
  816.4 7.2 collective-permute-done.70
  840.9 9.4 %collective-permute-done.82 = bf16[256,256]{1,0:T(8,128)(2,1)S(1)} collective-permute-done((bf16[256,256]{1,0:T(8,128)(2,1)S(1)}, bf16[256,256]{1,0:T(8,128)(2,1)S(1)}, u32[]{:S(2)}, u32[]{:S(2)}) %collective-permute-start.82) | collective-permute-done | bytes 131104 | tf_op jit(solution)/shard_map/ppermute | solution.py:916
  853.1 12.1 %collective-permute-done.83 = bf16[256,256]{1,0:T(8,128)(2,1)S(1)} collective-permute-done((bf16[256,256]{1,0:T(8,128)(2,1)S(1)}, bf16[256,256]{1,0:T(8,128)(2,1)S(1)}, u32[]{:S(2)}, u32[]{:S(2)}) %collective-permute-start.83) | collective-permute-done | bytes 131104 | tf_op jit(solution)/shard_map/ppermute | solution.py:916
  890.1 9.6 %all-to-all-done.1 = bf16[8,320,256]{2,1,0:T(8,128)(2,1)S(1)} async-done(((bf16[8,320,256]{2,1,0:T(8,128)(2,1)}), bf16[8,320,256]{2,1,0:T(8,128)(2,1)S(1)}, u32[]{:S(2)}, u32[]{:S(2)}) %all-to-all-start.1) | async-done | bytes 1310752 | tf_op jit(solution)/shard_map/all_to_all | solution.py:1244
  902.8 8.3 collective-permute-done.76
  911.2 8.7 shard_map.147
  (716 shorter events, 392.9 us)
Async XLA Ops:
  7.2 187.1 %all-gather.6.cloned.1.call-start = ((), (), s32[]{:S(2)}) async-start(), calls=%async_computation.7 | async-start | bytes 12435456 | tf_op jit(solution)/shard_map/all_gather | solution.py:1103
  64.5 22.8 %collective-permute-start.3 = (bf16[736,256]{1,0:T(8,128)(2,1)S(1)}, bf16[736,256]{1,0:T(8,128)(2,1)S(1)}, u32[]{:S(2)}, u32[]{:S(2)}) collective-permute-start(bf16[736,256]{1,0:T(8,128)(2,1)S(1)} %get-tuple-element.213), channel_id=1, source_target_pairs={{0,16},{1,17},{2,18},{3,19},{4,20},{5,21},{6,22},{7,23}} | collective-permute-start | bytes 1130504 | tf_op jit(solution)/shard_map/ppermute | solution.py:930
  69.5 17.7 %collective-permute-start.4 = (bf16[736,256]{1,0:T(8,128)(2,1)S(1)}, bf16[736,256]{1,0:T(8,128)(2,1)}, u32[]{:S(2)}, u32[]{:S(2)}) collective-permute-start(bf16[736,256]{1,0:T(8,128)(2,1)S(1)} %get-tuple-element.212), channel_id=1, source_target_pairs={{0,8},{1,9},{2,10},{3,11},{4,12},{5,13},{6,14},{7,15}} | collective-permute-start | bytes 1130504 | tf_op jit(solution)/shard_map/ppermute | solution.py:930
  71.6 15.7 %collective-permute-start.2 = (bf16[384,256]{1,0:T(8,128)(2,1)}, bf16[384,256]{1,0:T(8,128)(2,1)}, u32[]{:S(2)}, u32[]{:S(2)}) collective-permute-start(bf16[384,256]{1,0:T(8,128)(2,1)} %slice.428), channel_id=1, source_target_pairs={{8,24},{9,25},{10,26},{11,27},{12,28},{13,29},{14,30},{15,31}} | collective-permute-start | bytes 589832 | tf_op jit(solution)/shard_map/ppermute | solution.py:930
  72.9 14.3 %collective-permute-start.1 = (bf16[352,256]{1,0:T(8,128)(2,1)}, bf16[352,256]{1,0:T(8,128)(2,1)}, u32[]{:S(2)}, u32[]{:S(2)}) collective-permute-start(bf16[352,256]{1,0:T(8,128)(2,1)} %slice.427), channel_id=1, source_target_pairs={{0,24},{1,25},{2,26},{3,27},{4,28},{5,29},{6,30},{7,31}} | collective-permute-start | bytes 540680 | tf_op jit(solution)/shard_map/ppermute | solution.py:930
  75.0 14.2 %collective-permute-start.10 = (bf16[1,2,2,272,256]{4,3,2,1,0:T(8,128)(2,1)S(1)}, bf16[1,2,2,272,256]{4,3,2,1,0:T(8,128)(2,1)S(1)}, u32[]{:S(2)}, u32[]{:S(2)}) collective-permute-start(bf16[1,2,2,272,256]{4,3,2,1,0:T(8,128)(2,1)S(1)} %maximum_select_fusion.3), channel_id=1, source_target_pairs={{0,1},{1,0},{2,3},{3,2},{4,5},{5,4},{6,7},{7,6},{8,9},{9,8},{10,11... | collective-permute-start | bytes 1671176 | tf_op jit(solution)/shard_map/ppermute | solution.py:850
  92.2 355.7 %all-gather.4.cloned.1.call-start = ((), (), s32[]{:S(2)}) async-start(), calls=%async_computation.4 | async-start | bytes 43253760 | tf_op jit(solution)/shard_map/all_gather | solution.py:1127
  92.2 82.4 %collective-permute-start.16 = (bf16[4,32,16,1024]{3,2,1,0:T(8,128)(2,1)}, bf16[4,32,16,1024]{3,2,1,0:T(8,128)(2,1)}, u32[]{:S(2)}, u32[]{:S(2)}) collective-permute-start(bf16[4,32,16,1024]{3,2,1,0:T(8,128)(2,1)} %slice_bitcast_fusion), channel_id=1, source_target_pairs={{0,1},{1,2},{2,3},{4,5},{5,6},{6,7},{8,9},{9,10},{10,11},{12,13},{... | collective-permute-start | bytes 12582920 | tf_op jit(solution)/shard_map/ppermute | solution.py:1111
  133.2 27.1 %collective-permute-start.18 = (f32[4,32]{1,0:T(4,128)S(1)}, f32[4,32]{1,0:T(4,128)S(1)}, u32[]{:S(2)}, u32[]{:S(2)}) collective-permute-start(f32[4,32]{1,0:T(4,128)S(1)} %get-tuple-element.108), channel_id=1, source_target_pairs={{0,1},{1,0},{2,3},{3,2},{4,5},{5,4},{6,7},{7,6},{8,9},{9,8},{10,11... | collective-permute-start | bytes 1544 | tf_op jit(solution)/shard_map/ppermute | solution.py:850
  145.6 19.2 %collective-permute-start.14 = (f32[4,2,640]{2,0,1:T(4,128)S(1)}, f32[4,2,640]{2,0,1:T(4,128)S(1)}, u32[]{:S(2)}, u32[]{:S(2)}) collective-permute-start(f32[4,2,640]{2,0,1:T(4,128)S(1)} %add.817), channel_id=1, source_target_pairs={{0,8},{8,0},{16,24},{24,16},{1,9},{9,1},{17,25},{25,17},{2,10},{10... | collective-permute-start | bytes 61448 | tf_op jit(solution)/shard_map/ppermute | solution.py:850
  145.7 25.2 %collective-permute-start.25 = (f32[1,2,2,4,8,2]{4,3,5,2,1,0:T(4,128)S(1)}, f32[1,2,2,4,8,2]{4,3,5,2,1,0:T(4,128)S(1)}, u32[]{:S(2)}, u32[]{:S(2)}) collective-permute-start(f32[1,2,2,4,8,2]{4,3,5,2,1,0:T(4,128)S(1)} %maximum_select_fusion.10), channel_id=1, source_target_pairs={{0,1},{1,0},{2,3},{3,2},{4,5},{5,4},{6,7},{7,6},{8,9},{9,8},{10,11... | collective-permute-start | bytes 3080 | tf_op jit(solution)/shard_map/ppermute | solution.py:850
  194.3 456.4 %reduce-scatter.3.cloned.1.call-start = ((), (), s32[]{:S(2)}) async-start(), calls=%async_computation.5 | async-start | bytes 6553600 | tf_op jit(solution)/shard_map/reduce_scatter | solution.py:1190
  350.9 24.9 %collective-permute-start.36 = (f32[4,16,2048]{2,1,0:T(8,128)S(1)}, f32[4,16,2048]{2,1,0:T(8,128)S(1)}, u32[]{:S(2)}, u32[]{:S(2)}) collective-permute-start(f32[4,16,2048]{2,1,0:T(8,128)S(1)} %constant_dynamic-slice_fusion.7), channel_id=1, source_target_pairs={{0,2},{2,0},{1,3},{3,1},{4,6},{6,4},{5,7},{7,5},{8,10},{10,8},{9,1... | collective-permute-start | bytes 1572872 | tf_op jit(solution)/shard_map/ppermute | solution.py:850
  406.5 26.9 %collective-permute-start.43 = (bf16[1,2,2,4,8,2048]{5,4,0,1,2,3:T(8,128)(2,1)S(1)}, bf16[1,2,2,4,8,2048]{5,4,0,1,2,3:T(8,128)(2,1)S(1)}, u32[]{:S(2)}, u32[]{:S(2)}) collective-permute-start(bf16[1,2,2,4,8,2048]{5,4,0,1,2,3:T(8,128)(2,1)S(1)} %maximum_select_fusion.4), channel_id=1, source_target_pairs={{0,1},{1,0},{2,3},{3,2},{4,5},{5,4},{6,7},{7,6},{8,9},{9,8},{10,11... | collective-permute-start | bytes 1572872 | tf_op jit(solution)/shard_map/ppermute | solution.py:850
  486.8 58.6 %collective-permute-start.44 = (f32[1,106,128]{2,1,0:T(8,128)}, f32[1,106,128]{2,1,0:T(8,128)}, u32[]{:S(2)}, u32[]{:S(2)}) collective-permute-start(f32[1,106,128]{2,1,0:T(8,128)} %add_bitcast_fusion), channel_id=1, source_target_pairs={{0,8},{8,16},{16,24},{24,0},{1,9},{9,17},{17,25},{25,1},{2,10},{10... | collective-permute-start | bytes 162824 | tf_op jit(solution)/shard_map/ppermute | solution.py:875
  486.8 62.3 %collective-permute-start.45 = (f32[1,106,128]{2,1,0:T(8,128)}, f32[1,106,128]{2,1,0:T(8,128)}, u32[]{:S(2)}, u32[]{:S(2)}) collective-permute-start(f32[1,106,128]{2,1,0:T(8,128)} %add_bitcast_fusion), channel_id=1, source_target_pairs={{0,16},{8,24},{16,0},{24,8},{1,17},{9,25},{17,1},{25,9},{2,18},{10... | collective-permute-start | bytes 162824 | tf_op jit(solution)/shard_map/ppermute | solution.py:875
  488.7 61.2 %collective-permute-start.46 = (f32[1,106,128]{2,1,0:T(8,128)}, f32[1,106,128]{2,1,0:T(8,128)}, u32[]{:S(2)}, u32[]{:S(2)}) collective-permute-start(f32[1,106,128]{2,1,0:T(8,128)} %add_bitcast_fusion), channel_id=1, source_target_pairs={{0,24},{8,0},{16,8},{24,16},{1,25},{9,1},{17,9},{25,17},{2,26},{10... | collective-permute-start | bytes 162824 | tf_op jit(solution)/shard_map/ppermute | solution.py:875
  522.1 28.7 %collective-permute-start.47 = (bf16[1,32,2048]{2,1,0:T(8,128)(2,1)}, bf16[1,32,2048]{2,1,0:T(8,128)(2,1)}, u32[]{:S(2)}, u32[]{:S(2)}) collective-permute-start(bf16[1,32,2048]{2,1,0:T(8,128)(2,1)} %get-tuple-element.216), channel_id=1, source_target_pairs={{0,8},{8,16},{16,24},{24,0},{1,9},{9,17},{17,25},{25,1},{2,10},{10... | collective-permute-start | bytes 393224 | tf_op jit(solution)/shard_map/ppermute | solution.py:875
  522.9 28.9 %collective-permute-start.48 = (bf16[1,32,2048]{2,1,0:T(8,128)(2,1)}, bf16[1,32,2048]{2,1,0:T(8,128)(2,1)}, u32[]{:S(2)}, u32[]{:S(2)}) collective-permute-start(bf16[1,32,2048]{2,1,0:T(8,128)(2,1)} %get-tuple-element.215), channel_id=1, source_target_pairs={{0,16},{8,24},{16,0},{24,8},{1,17},{9,25},{17,1},{25,9},{2,18},{10... | collective-permute-start | bytes 393224 | tf_op jit(solution)/shard_map/ppermute | solution.py:875
  553.5 227.7 %reduce-scatter.5.cloned.1.call-start = ((), (), s32[]{:S(2)}) async-start(), calls=%async_computation.6 | async-start | bytes 7077888 | tf_op jit(solution)/shard_map/reduce_scatter | solution.py:1203
  577.5 14.6 %collective-permute-start.54 = (f32[4,3,2048]{2,0,1:T(4,128)S(1)}, f32[4,3,2048]{2,0,1:T(4,128)S(1)}, u32[]{:S(2)}, u32[]{:S(2)}) collective-permute-start(f32[4,3,2048]{2,0,1:T(4,128)S(1)} %add.911), channel_id=1, source_target_pairs={{0,16},{8,24},{16,0},{24,8},{1,17},{9,25},{17,1},{25,9},{2,18},{10... | collective-permute-start | bytes 294920 | tf_op jit(solution)/shard_map/ppermute | solution.py:850
  733.5 21.9 %collective-permute-start.65 = (bf16[2,2,1152,256]{3,2,1,0:T(8,128)(2,1)}, bf16[2,2,1152,256]{3,2,1,0:T(8,128)(2,1)S(1)}, u32[]{:S(2)}, u32[]{:S(2)}) collective-permute-start(bf16[2,2,1152,256]{3,2,1,0:T(8,128)(2,1)} %dynamic-slice_bitcast_fusion), channel_id=1, source_target_pairs={{0,1},{1,0},{2,3},{3,2},{4,5},{5,4},{6,7},{7,6},{8,9},{9,8},{10,11... | collective-permute-start | bytes 7077896 | tf_op jit(solution)/shard_map/ppermute | solution.py:850
  757.6 22.5 %collective-permute-start.67 = (bf16[2,576,256]{2,1,0:T(8,128)(2,1)S(1)}, bf16[2,576,256]{2,1,0:T(8,128)(2,1)}, u32[]{:S(2)}, u32[]{:S(2)}) collective-permute-start(bf16[2,576,256]{2,1,0:T(8,128)(2,1)S(1)} %dynamic-slice_bitcast_fusion.1), channel_id=1, source_target_pairs={{0,4},{4,0},{1,5},{5,1},{2,6},{6,2},{3,7},{7,3},{8,12},{12,8},{9,1... | collective-permute-start | bytes 1769480 | tf_op jit(solution)/shard_map/ppermute | solution.py:850
  760.7 28.9 %collective-permute-start.66 = (bf16[2,576,256]{2,1,0:T(8,128)(2,1)}, bf16[2,576,256]{2,1,0:T(8,128)(2,1)}, u32[]{:S(2)}, u32[]{:S(2)}) collective-permute-start(bf16[2,576,256]{2,1,0:T(8,128)(2,1)} %dynamic-slice_bitcast_fusion.2), channel_id=1, source_target_pairs={{0,2},{2,0},{1,3},{3,1},{4,6},{6,4},{5,7},{7,5},{8,10},{10,8},{9,1... | collective-permute-start | bytes 1769480 | tf_op jit(solution)/shard_map/ppermute | solution.py:850
  825.8 25.8 %collective-permute-start.72 = (bf16[1152,256]{1,0:T(8,128)(2,1)S(1)}, bf16[1152,256]{1,0:T(8,128)(2,1)S(1)}, u32[]{:S(2)}, u32[]{:S(2)}) collective-permute-start(bf16[1152,256]{1,0:T(8,128)(2,1)S(1)} %pad_maximum_fusion), channel_id=1, source_target_pairs={{8,0},{24,16},{9,1},{25,17},{10,2},{26,18},{11,3},{27,19},{12,4},{... | collective-permute-start | bytes 1769480 | tf_op jit(solution)/shard_map/ppermute | solution.py:916
  837.3 13.0 %collective-permute-start.82 = (bf16[256,256]{1,0:T(8,128)(2,1)S(1)}, bf16[256,256]{1,0:T(8,128)(2,1)S(1)}, u32[]{:S(2)}, u32[]{:S(2)}) collective-permute-start(bf16[256,256]{1,0:T(8,128)(2,1)S(1)} %pad_maximum_fusion.3), channel_id=1, source_target_pairs={{8,0},{24,16},{9,1},{25,17},{10,2},{26,18},{11,3},{27,19},{12,4},{... | collective-permute-start | bytes 393224 | tf_op jit(solution)/shard_map/ppermute | solution.py:916
  838.9 27.9 %collective-permute-start.75 = (bf16[384,256]{1,0:T(8,128)(2,1)S(1)}, bf16[384,256]{1,0:T(8,128)(2,1)S(1)}, u32[]{:S(2)}, u32[]{:S(2)}) collective-permute-start(bf16[384,256]{1,0:T(8,128)(2,1)S(1)} %fusion.114), channel_id=1, source_target_pairs={{24,8},{25,9},{26,10},{27,11},{28,12},{29,13},{30,14},{31,15}} | collective-permute-start | bytes 589832 | tf_op jit(solution)/shard_map/ppermute | solution.py:916
  839.5 27.3 %collective-permute-start.74 = (bf16[1152,256]{1,0:T(8,128)(2,1)S(1)}, bf16[1152,256]{1,0:T(8,128)(2,1)S(1)}, u32[]{:S(2)}, u32[]{:S(2)}) collective-permute-start(bf16[1152,256]{1,0:T(8,128)(2,1)S(1)} %fusion.117), channel_id=1, source_target_pairs={{16,0},{17,1},{18,2},{19,3},{20,4},{21,5},{22,6},{23,7}} | collective-permute-start | bytes 1769480 | tf_op jit(solution)/shard_map/ppermute | solution.py:916
  850.3 14.9 %collective-permute-start.83 = (bf16[256,256]{1,0:T(8,128)(2,1)S(1)}, bf16[256,256]{1,0:T(8,128)(2,1)S(1)}, u32[]{:S(2)}, u32[]{:S(2)}) collective-permute-start(bf16[256,256]{1,0:T(8,128)(2,1)S(1)} %fusion.116), channel_id=1, source_target_pairs={{16,0},{17,1},{18,2},{19,3},{20,4},{21,5},{22,6},{23,7}} | collective-permute-start | bytes 393224 | tf_op jit(solution)/shard_map/ppermute | solution.py:916
  851.8 22.1 %collective-permute-start.73 = (bf16[1152,256]{1,0:T(8,128)(2,1)S(1)}, bf16[1152,256]{1,0:T(8,128)(2,1)S(1)}, u32[]{:S(2)}, u32[]{:S(2)}) collective-permute-start(bf16[1152,256]{1,0:T(8,128)(2,1)S(1)} %fusion.118), channel_id=1, source_target_pairs={{16,0},{17,1},{18,2},{19,3},{20,4},{21,5},{22,6},{23,7}} | collective-permute-start | bytes 1769480 | tf_op jit(solution)/shard_map/ppermute | solution.py:916
  870.2 12.7 %collective-permute-start.85 = (bf16[1,2,256,256]{3,2,1,0:T(8,128)(2,1)S(1)}, bf16[1,2,256,256]{3,2,1,0:T(8,128)(2,1)S(1)}, u32[]{:S(2)}, u32[]{:S(2)}) collective-permute-start(bf16[1,2,256,256]{3,2,1,0:T(8,128)(2,1)S(1)} %maximum_select_fusion.8), channel_id=1, source_target_pairs={{0,2},{2,0},{1,3},{3,1},{4,6},{6,4},{5,7},{7,5},{8,10},{10,8},{9,1... | collective-permute-start | bytes 786440 | tf_op jit(solution)/shard_map/ppermute | solution.py:850
  878.9 20.8 %all-to-all-start.1 = ((bf16[8,320,256]{2,1,0:T(8,128)(2,1)}), bf16[8,320,256]{2,1,0:T(8,128)(2,1)S(1)}, u32[]{:S(2)}, u32[]{:S(2)}) async-start(bf16[8,320,256]{2,1,0:T(8,128)(2,1)} %bitcast.79), calls=%async_computation.3 | async-start | bytes 2621440 | tf_op jit(solution)/shard_map/all_to_all | solution.py:1244
  (191 other events, 2204.5 us)
Sparse Core Ops, SparseCore 0:
  92.3 101.8 all-gather.5
  197.6 250.2 all-gather.3
  553.6 96.9 reduce-scatter.2
  653.9 62.1 reduce-scatter.4

commit v4 on v2

--- a/solution.py
+++ b/solution.py
@@ -1096,9 +1096,10 @@
     if near:
         window = flat_to_window(params, window_rows, shift, index, count)
         column = lax.all_to_all(window, PLANE, 1, 0, tiled=True)
+        trunk = spread_trunk(column, plane, plane_rows)
+        trunk, column = lax.optimization_barrier((trunk, column))
         wide_in, vec = first_rows_everywhere(column, plane, plane_rows)
-        trunk = spread_trunk(column, plane, plane_rows)
-        trunk, x_last, wide_in = lax.optimization_barrier((trunk, x_last, wide_in))
+        x_last, wide_in = lax.optimization_barrier((x_last, wide_in))
         h, xe, st, w_first = conv_in(x, wph, wide_in)
         trunk = lax.all_gather(trunk, ALL, axis=0, tiled=False).reshape(GROUPS, LANES, GROUP, 256)
         st, image_pixels, chosen, mask_last = lax.optimization_barrier((st, image_pixels, chosen, mask_last))

time: 926 us -> 934 us (level)
    all_gather x1, waiting for transfers between devices: 11.4 us -> 0.01 us  [on_device(): lax.all_gather(trunk, ALL, axis=0, tiled=False)]
  transfers between devices with their start and end apart: 88 -> 88, of which waited for: 59 -> 59; matrix products, arithmetic and copies ran while one was open for 12% -> 11% of each run, Pallas kernels for 31% -> 31%
where the time goes in v4:
time: 934 us; the launch traced here: 924 us
  Pallas kernels  295 us (32%)
  waiting for transfers between devices  288 us (31%)
  starting transfers between devices  138 us (15%)
  local copies, waits for them, and re-layouts  61.7 us (7%)
  matrix products  60.5 us (6%)
  other arithmetic  39.1 us (4%)
  blocking collectives  23 us (2%)
  between operations  17.9 us (2%)
    ppermute x51, waiting for transfers between devices, swap(): return lax.ppermute(value, axis, [(i, i ^ bit) for i in range(size)])  162 us
    ppermute x51, starting transfers between devices, swap(): return lax.ppermute(value, axis, [(i, i ^ bit) for i in range(size)])  72.7 us
    pallas_call x1, Pallas kernels, back_mid(): pl.pallas_call(back_mid_kernel, grid=(micros,), out_shape=[jax.ShapeDtype...  59.8 us
    pallas_call x1, Pallas kernels, back_out(): pl.pallas_call(back_out_kernel, grid=(micros, OUT // n), out_shape=[jax.S...  53.2 us
    ppermute x8, waiting for transfers between devices, to_plane(): value = value + lax.ppermute(value, 'g', pairs)  49.6 us
    pallas_call x1, Pallas kernels, conv_mid(): pl.pallas_call(conv_mid_kernel, grid=(micros,), out_shape=[jax.ShapeDtype...  31.6 us
    pallas_call x1, Pallas kernels, back_in(): pl.pallas_call(back_in_kernel, grid=(micros, parts), out_shape=jax.ShapeD...  30.1 us
    pallas_call x1, Pallas kernels, conv_in(): pl.pallas_call(conv_in_kernel, grid=(micros, parts), out_shape=[jax.Shape...  27.5 us
  transfers between devices with their start and end apart: 88, of which 59 were waited for; matrix products, arithmetic and copies ran while one was open for 11% of the time, Pallas kernels for 31%

profile of v4, /device:TPU:4, one launch (start us, length us, event | category | flops | bytes accessed | tf_op | source)
XLA Modules:
  0.0 923.9 jit_solution(15046927035944574263)
XLA Ops:
  11.3 6.0 collective-permute-done
  23.0 23.0 %all_to_all.38 = bf16[320,8,256]{2,0,1:T(8,128)(2,1)S(1)} all-to-all(bf16[320,8,256]{2,0,1:T(8,128)(2,1)S(1)} %bitcast.321), channel_id=1, replica_groups=mesh['g'=4,'p'=2,'x'=2,'c'=2] {'p','x','c'}, dimensions={1} | all-to-all | bytes 2621440 | tf_op jit(solution)/shard_map/all_to_all | solution.py:1098
  54.6 15.3 %collective-permute-done.1 = bf16[352,256]{1,0:T(8,128)(2,1)} collective-permute-done((bf16[352,256]{1,0:T(8,128)(2,1)S(1)}, bf16[352,256]{1,0:T(8,128)(2,1)}, u32[]{:S(2)}, u32[]{:S(2)}) %collective-permute-start.1) | collective-permute-done | bytes 180256 | tf_op jit(solution)/shard_map/ppermute | solution.py:930
  71.9 6.3 collective-permute-start.5
  118.5 27.5 %shard_map.136 = (f32[4,4,512,512]{3,2,1,0:T(8,128)}, bf16[4,512,1024]{2,1,0:T(8,128)(2,1)}, f32[4,8,512]{2,1,0:T(8,128)}, bf16[1024,512]{1,0:T(8,128)(2,1)}) custom-call(bf16[4,2048,1024]{2,1,0:T(8,128)(2,1)} %bitcast.308, f32[4,4,512,1]{3,2,1,0:T(8,128)} %reshape.1274.w_ref, bf16[256,2048]{1,0:T(8,128)(2,1)} %slice.340.wide_ref), custom_call_target="tpu_custom_call" | custom-call | flops 1073741824 | bytes 5242880 | tf_op jit(solution)/shard_map/pallas_call | solution.py:246
  168.1 23.5 %collective-permute-start.25 = (f32[1,2,2,4,8,2]{4,3,5,2,1,0:T(4,128)S(1)}, f32[1,2,2,4,8,2]{4,3,5,2,1,0:T(4,128)S(1)}, u32[]{:S(2)}, u32[]{:S(2)}) collective-permute-start(f32[1,2,2,4,8,2]{4,3,5,2,1,0:T(4,128)S(1)} %maximum_select_fusion.10), channel_id=1, source_target_pairs={{0,1},{1,0},{2,3},{3,2},{4,5},{5,4},{6,7},{7,6},{8,9},{9,8},{10,11... | collective-permute-start | bytes 3080 | tf_op jit(solution)/shard_map/ppermute | solution.py:850
  209.4 20.9 %shard_map.139 = (f32[4,512,2048]{2,1,0:T(8,128)}, f32[4,8,2048]{2,1,0:T(8,128)}) custom-call(bf16[4,512,1024]{2,1,0:T(8,128)(2,1)} %get-tuple-element.120.xe_ref, bf16[4,8,736,256]{3,2,1,0:T(8,128)(2,1)} %bitcast.302, bf16[4,8,736,256]{3,2,1,0:T(8,128)(2,1)} %bitcast.303), custom_call_target="tpu_custom_call" | custom-call | flops 1073741824 | bytes 2097152 | tf_op jit(solution)/shard_map/pallas_call | solution.py:319
  233.7 31.6 %shard_map.138 = (bf16[4,512,4608]{2,1,0:T(8,128)(2,1)}, f32[4,512,512]{2,1,0:T(8,128)}, f32[4,8,512]{2,1,0:T(8,128)}, bf16[4608,512]{1,0:T(8,128)(2,1)}) custom-call(f32[4,4,512,512]{3,2,1,0:T(8,128)} %get-tuple-element.104.h_ref, f32[4,2,256,512]{3,2,1,0:T(8,128)} %copy-done, f32[4,8,512]{2,1,0:T(8,128)} %pad_maximum_fusion.4.cf_ref, ...), custom_call_target="tpu_custom_call" | custom-call | flops 1207959552 | bytes 6553600 | tf_op jit(solution)/shard_map/pallas_call | solution.py:389
  279.1 10.1 %collective-permute-done.29 = f32[4,2,2560]{2,0,1:T(4,128)S(1)} collective-permute-done((f32[4,2,2560]{2,0,1:T(4,128)S(1)}, f32[4,2,2560]{2,0,1:T(4,128)S(1)}, u32[]{:S(2)}, u32[]{:S(2)}) %collective-permute-start.29) | collective-permute-done | bytes 81952 | tf_op jit(solution)/shard_map/ppermute | solution.py:850
  289.3 9.6 %collective-permute-done.30 = f32[4,2,2560]{2,0,1:T(4,128)S(1)} collective-permute-done((f32[4,2,2560]{2,0,1:T(4,128)S(1)}, f32[4,2,2560]{2,0,1:T(4,128)S(1)}, u32[]{:S(2)}, u32[]{:S(2)}) %collective-permute-start.30) | collective-permute-done | bytes 81952 | tf_op jit(solution)/shard_map/ppermute | solution.py:850
  300.0 12.8 %shard_map.140 = (bf16[4,512,512]{2,1,0:T(8,128)(2,1)}, f32[4,512,2048]{2,1,0:T(8,128)}, f32[4,8,2048]{2,1,0:T(8,128)}, bf16[512,2048]{1,0:T(8,128)(2,1)}) custom-call(f32[4,512,512]{2,1,0:T(8,128)} %get-tuple-element.118.hm_ref, f32[4,8,512]{2,1,0:T(8,128)} %pad_maximum_fusion.3.cf_ref.cm_ref, f32[4,4,512,1]{3,2,1,0:T(8,128)} %reshape.1274.w_ref, ...), custom_call_target="tpu_custom_call" | custom-call | flops 536870912 | bytes 2359296 | tf_op jit(solution)/shard_map/pallas_call | solution.py:439
  331.4 11.8 %collective-permute-done.35 = f32[4,2,2048]{2,0,1:T(4,128)S(1)} collective-permute-done((f32[4,2,2048]{2,0,1:T(4,128)S(1)}, f32[4,2,2048]{2,0,1:T(4,128)S(1)}, u32[]{:S(2)}, u32[]{:S(2)}) %collective-permute-start.35) | collective-permute-done | bytes 65568 | tf_op jit(solution)/shard_map/ppermute | solution.py:850
  345.2 19.8 %shard_map.141 = f32[4,32,2048]{2,1,0:T(8,128)} custom-call(f32[4,512,2048]{2,1,0:T(8,128)} %get-tuple-element.123.ho_ref, f32[4,512,2048]{2,1,0:T(8,128)} %get-tuple-element.124.hs_ref, f32[4,8,2048]{2,1,0:T(8,128)} %stack.84.cf_ref, f32[4,4,512,1]{3,2,1,0:T(8,128)} %reshape.1274.w_ref), custom_call_target="tpu_custom_call" | custom-call | flops 10485760 | bytes 2359296 | tf_op jit(solution)/shard_map/pallas_call | solution.py:486
  368.2 21.0 %collective-permute-done.36 = f32[4,16,2048]{2,1,0:T(8,128)S(1)} collective-permute-done((f32[4,16,2048]{2,1,0:T(8,128)S(1)}, f32[4,16,2048]{2,1,0:T(8,128)S(1)}, u32[]{:S(2)}, u32[]{:S(2)}) %collective-permute-start.36) | collective-permute-done | bytes 524320 | tf_op jit(solution)/shard_map/ppermute | solution.py:850
  410.3 6.1 collective-permute-done.42
  419.0 24.0 %shard_map.142 = f32[4,3,32,2048]{3,2,1,0:T(8,128)} custom-call(f32[4,512,2048]{2,1,0:T(8,128)} %get-tuple-element.123.ho_ref, f32[4,512,2048]{2,1,0:T(8,128)} %get-tuple-element.124.hs_ref, f32[4,8,2048]{2,1,0:T(8,128)} %stack.84.cf_ref, f32[4,4,512,1]{3,2,1,0:T(8,128)} %reshape.1274.w_ref), custom_call_target="tpu_custom_call" | custom-call | flops 15728640 | bytes 2621440 | tf_op jit(solution)/shard_map/pallas_call | solution.py:529
  443.1 14.0 %all-gather.4.cloned.1.call-done = bf16[10240,2048]{1,0:T(8,128)(2,1)} async-done(((bf16[320,2048]{1,0:T(8,128)(2,1)}), bf16[10240,2048]{1,0:T(8,128)(2,1)}) %all-gather.4.cloned.1.call-update) | async-done | bytes 41943056 | tf_op jit(solution)/shard_map/all_gather | solution.py:1128
  463.6 6.0 fusion.119
  470.4 6.0 fusion.118
  509.7 6.0 fusion.116
  523.9 6.1 fusion.27
  577.5 9.3 %collective-permute-done.53 = f32[4,3,2048]{2,0,1:T(4,128)S(1)} collective-permute-done((f32[4,3,2048]{2,0,1:T(4,128)S(1)}, f32[4,3,2048]{2,0,1:T(4,128)S(1)}, u32[]{:S(2)}, u32[]{:S(2)}) %collective-permute-start.53) | collective-permute-done | bytes 98336 | tf_op jit(solution)/shard_map/ppermute | solution.py:850
  588.3 13.2 %collective-permute-done.54 = f32[4,3,2048]{2,0,1:T(4,128)S(1)} collective-permute-done((f32[4,3,2048]{2,0,1:T(4,128)S(1)}, f32[4,3,2048]{2,0,1:T(4,128)S(1)}, u32[]{:S(2)}, u32[]{:S(2)}) %collective-permute-start.54) | collective-permute-done | bytes 98336 | tf_op jit(solution)/shard_map/ppermute | solution.py:850
  602.9 53.2 %shard_map.143 = (f32[4,512,512]{2,1,0:T(8,128)}, f32[4,8,512]{2,1,0:T(8,128)}, bf16[8,1536,256]{2,1,0:T(8,128)(2,1)}) custom-call(f32[4,512,2048]{2,1,0:T(8,128)} %get-tuple-element.123.ho_ref, f32[4,512,2048]{2,1,0:T(8,128)} %get-tuple-element.124.hs_ref, f32[4,32,2048]{2,1,0:T(8,128)} %copy-done.6, f32[4,8,2048]{2,1,0:T(8,128)} %copy.242.cf_ref, ...), custom_call_target="tpu_custom_call" | custom-call | flops 2147483648 | bytes 5242880 | tf_op jit(solution)/shard_map/pallas_call | solution.py:620
  679.5 59.8 %shard_map.144 = (bf16[4,4,512,512]{3,2,1,0:T(8,128)(2,1)}, f32[4,2,256,512]{3,2,1,0:T(8,128)}, f32[4,8,512]{2,1,0:T(8,128)}, bf16[8,1152,256]{2,1,0:T(8,128)(2,1)}) custom-call(f32[4,512,512]{2,1,0:T(8,128)} %get-tuple-element.118.hm_ref, f32[4,512,512]{2,1,0:T(8,128)} %get-tuple-element.134.d_ref, f32[4,8,512]{2,1,0:T(8,128)} %stack.86.cm_ref, ...), custom_call_target="tpu_custom_call" | custom-call | flops 2415919104 | bytes 7864320 | tf_op jit(solution)/shard_map/pallas_call | solution.py:739
  771.7 30.1 %shard_map.145 = bf16[8,256,256]{2,1,0:T(8,128)(2,1)} custom-call(f32[4,4,512,512]{3,2,1,0:T(8,128)} %get-tuple-element.104.h_ref, bf16[4,4,512,512]{3,2,1,0:T(8,128)(2,1)} %get-tuple-element.138.din_ref, f32[4,2,256,512]{3,2,1,0:T(8,128)} %get-tuple-element.139.dh_ref, f32[4,8,512]{2,1,0:T(8,128)} %stack.89.cf_ref, f32[4,4,512,1]{3,2,1,0:T(8,128)} %reshape.1274.w_ref, ...), custom_call_target="tpu_custom_call" | custom-call | flops 1342177280 | bytes 6553600 | tf_op jit(solution)/shard_map/pallas_call | solution.py:823
  811.3 15.4 %collective-permute-done.72 = bf16[1152,256]{1,0:T(8,128)(2,1)S(1)} collective-permute-done((bf16[1152,256]{1,0:T(8,128)(2,1)S(1)}, bf16[1152,256]{1,0:T(8,128)(2,1)S(1)}, u32[]{:S(2)}, u32[]{:S(2)}) %collective-permute-start.72) | collective-permute-done | bytes 589856 | tf_op jit(solution)/shard_map/ppermute | solution.py:916
  841.9 6.2 collective-permute-done.78
  857.8 12.6 %collective-permute-done.75 = bf16[1152,256]{1,0:T(8,128)(2,1)S(1)} collective-permute-done((bf16[1152,256]{1,0:T(8,128)(2,1)S(1)}, bf16[1152,256]{1,0:T(8,128)(2,1)S(1)}, u32[]{:S(2)}, u32[]{:S(2)}) %collective-permute-start.75) | collective-permute-done | bytes 589856 | tf_op jit(solution)/shard_map/ppermute | solution.py:916
  887.1 9.6 %all-to-all-done.1 = bf16[8,320,256]{2,1,0:T(8,128)(2,1)S(1)} async-done(((bf16[8,320,256]{2,1,0:T(8,128)(2,1)}), bf16[8,320,256]{2,1,0:T(8,128)(2,1)S(1)}, u32[]{:S(2)}, u32[]{:S(2)}) %all-to-all-start.1) | async-done | bytes 1310752 | tf_op jit(solution)/shard_map/all_to_all | solution.py:1239
  899.8 8.3 collective-permute-done.76
  908.3 8.7 shard_map.146
  (689 shorter events, 372.0 us)
Async XLA Ops:
  7.2 201.7 %all-gather.6.cloned.1.call-start = ((), (), s32[]{:S(2)}) async-start(), calls=%async_computation.9 | async-start | bytes 12435456 | tf_op jit(solution)/shard_map/all_gather | solution.py:1104
  46.1 23.8 %collective-permute-start.3 = (bf16[736,256]{1,0:T(8,128)(2,1)S(1)}, bf16[736,256]{1,0:T(8,128)(2,1)S(1)}, u32[]{:S(2)}, u32[]{:S(2)}) collective-permute-start(bf16[736,256]{1,0:T(8,128)(2,1)S(1)} %get-tuple-element.215), channel_id=1, source_target_pairs={{0,16},{1,17},{2,18},{3,19},{4,20},{5,21},{6,22},{7,23}} | collective-permute-start | bytes 1130504 | tf_op jit(solution)/shard_map/ppermute | solution.py:930
  50.6 19.3 %collective-permute-start.4 = (bf16[736,256]{1,0:T(8,128)(2,1)S(1)}, bf16[736,256]{1,0:T(8,128)(2,1)S(1)}, u32[]{:S(2)}, u32[]{:S(2)}) collective-permute-start(bf16[736,256]{1,0:T(8,128)(2,1)S(1)} %get-tuple-element.214), channel_id=1, source_target_pairs={{0,8},{1,9},{2,10},{3,11},{4,12},{5,13},{6,14},{7,15}} | collective-permute-start | bytes 1130504 | tf_op jit(solution)/shard_map/ppermute | solution.py:930
  51.9 18.0 %collective-permute-start.2 = (bf16[384,256]{1,0:T(8,128)(2,1)S(1)}, bf16[384,256]{1,0:T(8,128)(2,1)S(1)}, u32[]{:S(2)}, u32[]{:S(2)}) collective-permute-start(bf16[384,256]{1,0:T(8,128)(2,1)S(1)} %slice.412), channel_id=1, source_target_pairs={{8,24},{9,25},{10,26},{11,27},{12,28},{13,29},{14,30},{15,31}} | collective-permute-start | bytes 589832 | tf_op jit(solution)/shard_map/ppermute | solution.py:930
  52.6 17.3 %collective-permute-start.1 = (bf16[352,256]{1,0:T(8,128)(2,1)S(1)}, bf16[352,256]{1,0:T(8,128)(2,1)}, u32[]{:S(2)}, u32[]{:S(2)}) collective-permute-start(bf16[352,256]{1,0:T(8,128)(2,1)S(1)} %slice.411), channel_id=1, source_target_pairs={{0,24},{1,25},{2,26},{3,27},{4,28},{5,29},{6,30},{7,31}} | collective-permute-start | bytes 540680 | tf_op jit(solution)/shard_map/ppermute | solution.py:930
  71.8 385.3 %all-gather.4.cloned.1.call-start = ((), (), s32[]{:S(2)}) async-start(), calls=%async_computation.5 | async-start | bytes 43253760 | tf_op jit(solution)/shard_map/all_gather | solution.py:1128
  110.7 90.0 %collective-permute-start.16 = (bf16[4,32,16,1024]{3,2,1,0:T(8,128)(2,1)}, bf16[4,32,16,1024]{3,2,1,0:T(8,128)(2,1)}, u32[]{:S(2)}, u32[]{:S(2)}) collective-permute-start(bf16[4,32,16,1024]{3,2,1,0:T(8,128)(2,1)} %slice_bitcast_fusion), channel_id=1, source_target_pairs={{0,1},{1,2},{2,3},{4,5},{5,6},{6,7},{8,9},{9,10},{10,11},{12,13},{... | collective-permute-start | bytes 12582920 | tf_op jit(solution)/shard_map/ppermute | solution.py:1112
  147.0 12.8 %collective-permute-start.11 = (f32[4,2,640]{2,0,1:T(4,128)S(1)}, f32[4,2,640]{2,0,1:T(4,128)S(1)}, u32[]{:S(2)}, u32[]{:S(2)}) collective-permute-start(f32[4,2,640]{2,0,1:T(4,128)S(1)} %pad_maximum_fusion.7), channel_id=1, source_target_pairs={{0,1},{1,0},{2,3},{3,2},{4,5},{5,4},{6,7},{7,6},{8,9},{9,8},{10,11... | collective-permute-start | bytes 61448 | tf_op jit(solution)/shard_map/ppermute | solution.py:850
  152.6 39.0 %collective-permute-start.18 = (f32[4,32]{1,0:T(4,128)S(1)}, f32[4,32]{1,0:T(4,128)S(1)}, u32[]{:S(2)}, u32[]{:S(2)}) collective-permute-start(f32[4,32]{1,0:T(4,128)S(1)} %get-tuple-element.111), channel_id=1, source_target_pairs={{0,1},{1,0},{2,3},{3,2},{4,5},{5,4},{6,7},{7,6},{8,9},{9,8},{10,11... | collective-permute-start | bytes 1544 | tf_op jit(solution)/shard_map/ppermute | solution.py:850
  167.5 28.3 %collective-permute-start.14 = (f32[4,2,640]{2,0,1:T(4,128)S(1)}, f32[4,2,640]{2,0,1:T(4,128)S(1)}, u32[]{:S(2)}, u32[]{:S(2)}) collective-permute-start(f32[4,2,640]{2,0,1:T(4,128)S(1)} %add.787), channel_id=1, source_target_pairs={{0,8},{8,0},{16,24},{24,16},{1,9},{9,1},{17,25},{25,17},{2,10},{10... | collective-permute-start | bytes 61448 | tf_op jit(solution)/shard_map/ppermute | solution.py:850
  168.1 27.8 %collective-permute-start.25 = (f32[1,2,2,4,8,2]{4,3,5,2,1,0:T(4,128)S(1)}, f32[1,2,2,4,8,2]{4,3,5,2,1,0:T(4,128)S(1)}, u32[]{:S(2)}, u32[]{:S(2)}) collective-permute-start(f32[1,2,2,4,8,2]{4,3,5,2,1,0:T(4,128)S(1)} %maximum_select_fusion.10), channel_id=1, source_target_pairs={{0,1},{1,0},{2,3},{3,2},{4,5},{5,4},{6,7},{7,6},{8,9},{9,8},{10,11... | collective-permute-start | bytes 3080 | tf_op jit(solution)/shard_map/ppermute | solution.py:850
  208.9 451.1 %reduce-scatter.4.cloned.1.call-start = ((), (), s32[]{:S(2)}) async-start(), calls=%async_computation.6 | async-start | bytes 6553600 | tf_op jit(solution)/shard_map/reduce_scatter | solution.py:1191
  331.2 11.9 %collective-permute-start.35 = (f32[4,2,2048]{2,0,1:T(4,128)S(1)}, f32[4,2,2048]{2,0,1:T(4,128)S(1)}, u32[]{:S(2)}, u32[]{:S(2)}) collective-permute-start(f32[4,2,2048]{2,0,1:T(4,128)S(1)} %add.811), channel_id=1, source_target_pairs={{0,16},{8,24},{16,0},{24,8},{1,17},{9,25},{17,1},{25,9},{2,18},{10... | collective-permute-start | bytes 196616 | tf_op jit(solution)/shard_map/ppermute | solution.py:850
  366.2 23.1 %collective-permute-start.36 = (f32[4,16,2048]{2,1,0:T(8,128)S(1)}, f32[4,16,2048]{2,1,0:T(8,128)S(1)}, u32[]{:S(2)}, u32[]{:S(2)}) collective-permute-start(f32[4,16,2048]{2,1,0:T(8,128)S(1)} %constant_dynamic-slice_fusion.7), channel_id=1, source_target_pairs={{0,2},{2,0},{1,3},{3,1},{4,6},{6,4},{5,7},{7,5},{8,10},{10,8},{9,1... | collective-permute-start | bytes 1572872 | tf_op jit(solution)/shard_map/ppermute | solution.py:850
  392.2 11.9 %collective-permute-start.39 = (bf16[1,8,2048]{2,1,0:T(8,128)(2,1)S(1)}, bf16[1,8,2048]{2,1,0:T(8,128)(2,1)S(1)}, u32[]{:S(2)}, u32[]{:S(2)}) collective-permute-start(bf16[1,8,2048]{2,1,0:T(8,128)(2,1)S(1)} %get-tuple-element.241), channel_id=1, source_target_pairs={{0,16},{8,24},{16,0},{24,8},{1,17},{9,25},{17,1},{25,9},{2,18},{10... | collective-permute-start | bytes 98312 | tf_op jit(solution)/shard_map/ppermute | solution.py:875
  416.4 26.6 %collective-permute-start.43 = (bf16[1,2,2,4,8,2048]{5,4,0,1,2,3:T(8,128)(2,1)S(1)}, bf16[1,2,2,4,8,2048]{5,4,0,1,2,3:T(8,128)(2,1)S(1)}, u32[]{:S(2)}, u32[]{:S(2)}) collective-permute-start(bf16[1,2,2,4,8,2048]{5,4,0,1,2,3:T(8,128)(2,1)S(1)} %maximum_select_fusion.4), channel_id=1, source_target_pairs={{0,1},{1,0},{2,3},{3,2},{4,5},{5,4},{6,7},{7,6},{8,9},{9,8},{10,11... | collective-permute-start | bytes 1572872 | tf_op jit(solution)/shard_map/ppermute | solution.py:850
  496.1 58.6 %collective-permute-start.44 = (f32[1,106,128]{2,1,0:T(8,128)}, f32[1,106,128]{2,1,0:T(8,128)}, u32[]{:S(2)}, u32[]{:S(2)}) collective-permute-start(f32[1,106,128]{2,1,0:T(8,128)} %add_bitcast_fusion), channel_id=1, source_target_pairs={{0,8},{8,16},{16,24},{24,0},{1,9},{9,17},{17,25},{25,1},{2,10},{10... | collective-permute-start | bytes 162824 | tf_op jit(solution)/shard_map/ppermute | solution.py:875
  496.1 62.3 %collective-permute-start.45 = (f32[1,106,128]{2,1,0:T(8,128)}, f32[1,106,128]{2,1,0:T(8,128)}, u32[]{:S(2)}, u32[]{:S(2)}) collective-permute-start(f32[1,106,128]{2,1,0:T(8,128)} %add_bitcast_fusion), channel_id=1, source_target_pairs={{0,16},{8,24},{16,0},{24,8},{1,17},{9,25},{17,1},{25,9},{2,18},{10... | collective-permute-start | bytes 162824 | tf_op jit(solution)/shard_map/ppermute | solution.py:875
  498.2 61.1 %collective-permute-start.46 = (f32[1,106,128]{2,1,0:T(8,128)}, f32[1,106,128]{2,1,0:T(8,128)}, u32[]{:S(2)}, u32[]{:S(2)}) collective-permute-start(f32[1,106,128]{2,1,0:T(8,128)} %add_bitcast_fusion), channel_id=1, source_target_pairs={{0,24},{8,0},{16,8},{24,16},{1,25},{9,1},{17,9},{25,17},{2,26},{10... | collective-permute-start | bytes 162824 | tf_op jit(solution)/shard_map/ppermute | solution.py:875
  531.8 28.4 %collective-permute-start.47 = (bf16[1,32,2048]{2,1,0:T(8,128)(2,1)}, bf16[1,32,2048]{2,1,0:T(8,128)(2,1)}, u32[]{:S(2)}, u32[]{:S(2)}) collective-permute-start(bf16[1,32,2048]{2,1,0:T(8,128)(2,1)} %get-tuple-element.218), channel_id=1, source_target_pairs={{0,8},{8,16},{16,24},{24,0},{1,9},{9,17},{17,25},{25,1},{2,10},{10... | collective-permute-start | bytes 393224 | tf_op jit(solution)/shard_map/ppermute | solution.py:875
  532.2 28.9 %collective-permute-start.48 = (bf16[1,32,2048]{2,1,0:T(8,128)(2,1)}, bf16[1,32,2048]{2,1,0:T(8,128)(2,1)}, u32[]{:S(2)}, u32[]{:S(2)}) collective-permute-start(bf16[1,32,2048]{2,1,0:T(8,128)(2,1)} %get-tuple-element.217), channel_id=1, source_target_pairs={{0,16},{8,24},{16,0},{24,8},{1,17},{9,25},{17,1},{25,9},{2,18},{10... | collective-permute-start | bytes 393224 | tf_op jit(solution)/shard_map/ppermute | solution.py:875
  562.9 176.4 %reduce-scatter.6.cloned.1.call-start = ((), (), s32[]{:S(2)}) async-start(), calls=%async_computation.7 | async-start | bytes 7077888 | tf_op jit(solution)/shard_map/reduce_scatter | solution.py:1204
  586.9 14.6 %collective-permute-start.54 = (f32[4,3,2048]{2,0,1:T(4,128)S(1)}, f32[4,3,2048]{2,0,1:T(4,128)S(1)}, u32[]{:S(2)}, u32[]{:S(2)}) collective-permute-start(f32[4,3,2048]{2,0,1:T(4,128)S(1)} %add.881), channel_id=1, source_target_pairs={{0,16},{8,24},{16,0},{24,8},{1,17},{9,25},{17,1},{25,9},{2,18},{10... | collective-permute-start | bytes 294920 | tf_op jit(solution)/shard_map/ppermute | solution.py:850
  660.1 171.9 %reduce-scatter.8.cloned.1.call-start = ((), (), s32[]{:S(2)}) async-start(), calls=%async_computation.8 | async-start | bytes 5308416 | tf_op jit(solution)/shard_map/reduce_scatter | solution.py:1213
  757.9 13.0 %collective-permute-start.65 = (bf16[1152,256]{1,0:T(8,128)(2,1)S(1)}, bf16[1152,256]{1,0:T(8,128)(2,1)S(1)}, u32[]{:S(2)}, u32[]{:S(2)}) collective-permute-start(bf16[1152,256]{1,0:T(8,128)(2,1)S(1)} %slice.394), channel_id=1, source_target_pairs={{8,0},{24,16},{9,1},{25,17},{10,2},{26,18},{11,3},{27,19},{12,4},{... | collective-permute-start | bytes 1769480 | tf_op jit(solution)/shard_map/ppermute | solution.py:916
  805.9 20.8 %collective-permute-start.72 = (bf16[1152,256]{1,0:T(8,128)(2,1)S(1)}, bf16[1152,256]{1,0:T(8,128)(2,1)S(1)}, u32[]{:S(2)}, u32[]{:S(2)}) collective-permute-start(bf16[1152,256]{1,0:T(8,128)(2,1)S(1)} %slice_add_fusion.6), channel_id=1, source_target_pairs={{16,0},{17,1},{18,2},{19,3},{20,4},{21,5},{22,6},{23,7}} | collective-permute-start | bytes 1769480 | tf_op jit(solution)/shard_map/ppermute | solution.py:916
  808.4 18.5 %collective-permute-start.68 = (bf16[2,128,256]{2,1,0:T(8,128)(2,1)S(1)}, bf16[2,128,256]{2,1,0:T(8,128)(2,1)S(1)}, u32[]{:S(2)}, u32[]{:S(2)}) collective-permute-start(bf16[2,128,256]{2,1,0:T(8,128)(2,1)S(1)} %dynamic-slice_bitcast_fusion.2), channel_id=1, source_target_pairs={{0,2},{2,0},{1,3},{3,1},{4,6},{6,4},{5,7},{7,5},{8,10},{10,8},{9,1... | collective-permute-start | bytes 393224 | tf_op jit(solution)/shard_map/ppermute | solution.py:850
  810.6 16.9 %collective-permute-start.70 = (bf16[2,128,256]{2,1,0:T(8,128)(2,1)S(1)}, bf16[2,128,256]{2,1,0:T(8,128)(2,1)S(1)}, u32[]{:S(2)}, u32[]{:S(2)}) collective-permute-start(bf16[2,128,256]{2,1,0:T(8,128)(2,1)S(1)} %dynamic-slice_bitcast_fusion.1), channel_id=1, source_target_pairs={{0,4},{4,0},{1,5},{5,1},{2,6},{6,2},{3,7},{7,3},{8,12},{12,8},{9,1... | collective-permute-start | bytes 393224 | tf_op jit(solution)/shard_map/ppermute | solution.py:850
  833.5 20.5 %collective-permute-start.74 = (bf16[1152,256]{1,0:T(8,128)(2,1)}, bf16[1152,256]{1,0:T(8,128)(2,1)S(1)}, u32[]{:S(2)}, u32[]{:S(2)}) collective-permute-start(bf16[1152,256]{1,0:T(8,128)(2,1)} %bitcast.340), channel_id=1, source_target_pairs={{8,0},{24,16},{9,1},{25,17},{10,2},{26,18},{11,3},{27,19},{12,4},{... | collective-permute-start | bytes 1769480 | tf_op jit(solution)/shard_map/ppermute | solution.py:916
  854.1 16.3 %collective-permute-start.75 = (bf16[1152,256]{1,0:T(8,128)(2,1)S(1)}, bf16[1152,256]{1,0:T(8,128)(2,1)S(1)}, u32[]{:S(2)}, u32[]{:S(2)}) collective-permute-start(bf16[1152,256]{1,0:T(8,128)(2,1)S(1)} %add.908), channel_id=1, source_target_pairs={{16,0},{17,1},{18,2},{19,3},{20,4},{21,5},{22,6},{23,7}} | collective-permute-start | bytes 1769480 | tf_op jit(solution)/shard_map/ppermute | solution.py:916
  856.4 23.6 %collective-permute-start.80 = (bf16[1,2,256,256]{3,2,1,0:T(8,128)(2,1)S(1)}, bf16[1,2,256,256]{3,2,1,0:T(8,128)(2,1)S(1)}, u32[]{:S(2)}, u32[]{:S(2)}) collective-permute-start(bf16[1,2,256,256]{3,2,1,0:T(8,128)(2,1)S(1)} %maximum_select_fusion.8), channel_id=1, source_target_pairs={{0,2},{2,0},{1,3},{3,1},{4,6},{6,4},{5,7},{7,5},{8,10},{10,8},{9,1... | collective-permute-start | bytes 786440 | tf_op jit(solution)/shard_map/ppermute | solution.py:850
  875.5 21.2 %all-to-all-start.1 = ((bf16[8,320,256]{2,1,0:T(8,128)(2,1)}), bf16[8,320,256]{2,1,0:T(8,128)(2,1)S(1)}, u32[]{:S(2)}, u32[]{:S(2)}) async-start(bf16[8,320,256]{2,1,0:T(8,128)(2,1)} %bitcast.79), calls=%async_computation.4 | async-start | bytes 2621440 | tf_op jit(solution)/shard_map/all_to_all | solution.py:1239
  (184 other events, 2153.1 us)
Sparse Core Ops, SparseCore 0:
  71.9 98.2 all-gather.5
  209.0 248.0 all-gather.3
  563.0 96.9 reduce-scatter.3
  663.3 62.0 reduce-scatter.5
  739.6 54.6 reduce-scatter.7
